TPU v7x, 32 devices: a whole 2x2x4 slice. The times are simulated.
32 devices in a mesh: groups: 2 (over x), ep: 4 (over y, core), sub: 4 (over z).
Axes of the slice: x: 2, y: 2, z: 4, core: 2. Of those that a mesh axis runs over, the one named last changes fastest.
Arguments:
- tokens: bfloat16 [256, 7168], P(('groups', 'ep', 'sub')), parts along dimension 0, may hold values from -6 to 6
- routes: int32 [256, 2], P(('groups', 'ep', 'sub')), parts along dimension 0, may hold values from 0 to 3, as said below
- gates: bfloat16 [256, 2], P(('groups', 'ep', 'sub')), parts along dimension 0, may hold values from 0.099609375 to 1
- expert_up: bfloat16 [4, 7168, 2, 1024], P('ep', None, None, 'sub'), may hold values from -0.0625 to 0.0625
- expert_down: bfloat16 [4, 1024, 7168], P('ep', 'sub'), may hold values from -0.1875 to 0.1875
- shared_up: bfloat16 [7168, 2, 2048], P(None, None, 'ep'), may hold values from -0.0625 to 0.0625
- shared_down: bfloat16 [2048, 7168], P('ep'), may hold values from -0.125 to 0.125
Outputs:
- mixed: bfloat16 [256, 7168], P(('groups', 'ep', 'sub')), parts along dimension 0
There are 2 independent parts, one for each index of `groups`. A program takes and returns all parts, laid end to end along the dimension named above; an argument that names none is the same for every part. Nothing has to cross between parts.
Inputs may be any that keep to these rules, and one draw needn't show every extreme that they name: `routes`: each row names 2 different experts. The rows of one device name one expert at most 6 times; one expert is named exactly 6 times by the rows of every device, and the other experts share the remaining 2 * 8 - 6 names of a device as evenly as possible.
All inputs are finite; a program needn't handle non-finite values.
Results may differ from a plain program's by a relative error of at most 0.015.
Values may be sent and summed in bfloat16 or wider, within the bound.
No kernel may reach another device: no remote copies, remote signals or barrier semaphores. Data moves between devices by JAX's collectives and lax.ppermute only.
A program may use at most 128 MiB of HBM per device.

v0:
```python
import jax
import jax.numpy as jnp
from jax import lax
from jax.sharding import PartitionSpec as P

QBLOCK = 128
CAP = 6


def hidden_rows(token_rows, weights):
    projected = jnp.dot(token_rows, weights, preferred_element_type=jnp.float32)
    half_width = weights.shape[1] // 2
    return (jax.nn.silu(projected[:, :half_width]) * projected[:, half_width:]).astype(jnp.bfloat16)


def rounded_term(left, right):
    partial_value = jnp.dot(left, right, preferred_element_type=jnp.float32).astype(jnp.bfloat16)
    return lax.optimization_barrier(partial_value).astype(jnp.float32)


def block_scaled(rows):
    count, width = rows.shape
    blocks = rows.astype(jnp.float32).reshape(count, width // QBLOCK, QBLOCK)
    largest = jnp.max(jnp.abs(blocks), axis=2)
    scale = ((largest + 1e-06) / 448.0).astype(jnp.bfloat16)
    scaled = (blocks / scale.astype(jnp.float32)[:, :, None]).astype(jnp.bfloat16)
    return (scaled.reshape(count, width), scale)


def block_restored(scaled, scale):
    count, width = scaled.shape
    blocks = scaled.astype(jnp.float32).reshape(count, width // QBLOCK, QBLOCK)
    values = blocks * scale.astype(jnp.float32)[:, :, None]
    return values.astype(jnp.bfloat16).reshape(count, width)


def per_device(tokens, routes, gates, expert_up, expert_down, shared_up, shared_down):
    count_tok, model_width = tokens.shape
    experts = lax.axis_size("ep")
    sub_count = lax.axis_size("sub")
    block_count = model_width // QBLOCK
    shared_weights = shared_up.reshape(model_width, -1)
    shared_hidden = hidden_rows(lax.all_gather(tokens, "ep", axis=0, tiled=True), shared_weights)
    hidden_part = shared_hidden
    shared_out = lax.psum_scatter(
        rounded_term(hidden_part, shared_down).astype(jnp.bfloat16),
        "ep",
        scatter_dimension=0,
        tiled=True,
    ).astype(jnp.float32)
    scaled, scale = block_scaled(tokens)
    expert_ids = jnp.arange(experts, dtype=jnp.int32)
    chosen = routes[:, :, None] == expert_ids
    named_any = jnp.any(chosen, axis=1).astype(jnp.int32)
    earlier = jnp.cumsum(named_any, axis=0) - named_any
    slot_ids = jnp.arange(CAP, dtype=jnp.int32)
    placement = (named_any[:, :, None] == 1) & (earlier[:, :, None] == slot_ids)
    place_mat = placement.reshape(count_tok, experts * CAP).astype(jnp.bfloat16)
    place_float = placement.astype(jnp.float32)
    weight = jnp.sum(jnp.where(chosen, gates[:, :, None].astype(jnp.float32), 0.0), axis=1)
    send_rows = jnp.dot(place_mat.T, scaled, preferred_element_type=jnp.float32)
    send_rows = send_rows.astype(jnp.bfloat16).reshape(experts, CAP, model_width)
    send_scales = jnp.einsum(
        "tec,tb->ecb", place_float, scale.astype(jnp.float32), precision=lax.Precision.HIGHEST
    ).astype(jnp.bfloat16)
    send_gates = jnp.einsum(
        "tec,te->ec", place_float, weight, precision=lax.Precision.HIGHEST
    ).astype(jnp.bfloat16)
    expert_weights = expert_up.reshape(model_width, -1)
    wide_rows = jnp.broadcast_to(send_rows[:, None], (experts, sub_count, CAP, model_width))
    wide_rows = wide_rows.reshape(experts * sub_count, CAP, model_width)
    wide_scales = jnp.broadcast_to(send_scales[:, None], (experts, sub_count, CAP, block_count))
    wide_scales = wide_scales.reshape(experts * sub_count, CAP, block_count)
    wide_gates = jnp.broadcast_to(send_gates[:, None], (experts, sub_count, CAP))
    wide_gates = wide_gates.reshape(experts * sub_count, CAP)
    got_rows, got_scales, got_gates = (
        lax.all_to_all(wide_rows, ("ep", "sub"), split_axis=0, concat_axis=0, tiled=True),
        lax.all_to_all(wide_scales, ("ep", "sub"), split_axis=0, concat_axis=0, tiled=True),
        lax.all_to_all(wide_gates, ("ep", "sub"), split_axis=0, concat_axis=0, tiled=True),
    )
    restored = block_restored(
        got_rows.reshape(-1, model_width), got_scales.reshape(-1, block_count)
    )
    hidden = hidden_rows(restored, expert_weights)
    hidden = hidden.reshape(experts, sub_count, CAP, -1).transpose(1, 0, 2, 3)
    hidden = hidden.reshape(sub_count * experts * CAP, -1)
    own_gates = lax.dynamic_index_in_dim(
        got_gates.reshape(experts, sub_count, CAP), lax.axis_index("sub"), 1, keepdims=False
    )
    down_weights = expert_down.reshape(-1, model_width)
    hidden_part = hidden
    summed = lax.psum_scatter(
        rounded_term(hidden_part, down_weights).astype(jnp.bfloat16),
        "sub",
        scatter_dimension=0,
        tiled=True,
    ).astype(jnp.float32)
    weighted = (own_gates.astype(jnp.float32).reshape(-1, 1) * summed).astype(jnp.bfloat16)
    weighted = weighted.reshape(experts, CAP, model_width)
    returned_rows = lax.all_to_all(weighted, "ep", split_axis=0, concat_axis=0, tiled=True)
    routed = jnp.dot(
        place_mat,
        returned_rows.reshape(experts * CAP, model_width),
        preferred_element_type=jnp.float32,
    )
    return (shared_out + routed).astype(jnp.bfloat16)


def solution(mesh):
    return jax.shard_map(
        per_device,
        mesh=mesh,
        in_specs=(
            P(("groups", "ep", "sub"), None),
            P(("groups", "ep", "sub"), None),
            P(("groups", "ep", "sub"), None),
            P("ep", None, None, "sub"),
            P("ep", "sub", None),
            P(None, None, "ep"),
            P("ep", None),
        ),
        out_specs=P(("groups", "ep", "sub"), None),
        check_vma=False,
    )
```

profile of v0, /device:TPU:0, one launch (start us, length us, event | category | flops | bytes accessed | tf_op | source)
XLA Modules:
  0.0 148.5 jit_solution(5762976507262740331)
XLA Ops:
  7.6 1.0 fusion.7
  9.0 0.7 reshape.130
  9.7 7.4 %all-to-all-start.2 = ((bf16[16,2,168]{2,1,0:T(2,128)(2,1)}), bf16[16,2,168]{2,1,0:T(2,128)(2,1)S(1)}, u32[]{:S(2)}, u32[]{:S(2)}) async-start(bf16[16,2,168]{2,1,0:T(2,128)(2,1)} %reshape.130), calls=%async_computation.3 | async-start | bytes 32768 | tf_op jit(solution)/shard_map/all_to_all | solution.py:78
  17.6 1.2 convolution_convert_fusion.2
  19.0 4.6 %all-to-all-done.2 = bf16[16,2,168]{2,1,0:T(2,128)(2,1)S(1)} async-done(((bf16[16,2,168]{2,1,0:T(2,128)(2,1)}), bf16[16,2,168]{2,1,0:T(2,128)(2,1)S(1)}, u32[]{:S(2)}, u32[]{:S(2)}) %all-to-all-start.2) | async-done | bytes 10784 | tf_op jit(solution)/shard_map/all_to_all | solution.py:78
  23.5 1.4 broadcast_in_dim.24
  25.0 4.4 %all-to-all-start.1 = ((bf16[16,6,7168]{2,1,0:T(8,128)(2,1)}), bf16[16,6,7168]{2,1,0:T(8,128)(2,1)}, u32[]{:S(2)}, u32[]{:S(2)}) async-start(bf16[16,6,7168]{2,1,0:T(8,128)(2,1)} %bitcast.7), calls=%async_computation.2 | async-start | bytes 3670016 | tf_op jit(solution)/shard_map/all_to_all | solution.py:77
  29.5 7.3 %copy.52 = bf16[896,8,2,256]{3,1,2,0:T(8,128)(2,1)} copy(bf16[896,8,2,256]{3,2,1,0:T(2,128)(2,1)} %bitcast.51) | data formatting | bytes 14680064
  36.9 36.3 %all-to-all-done.1 = bf16[16,6,7168]{2,1,0:T(8,128)(2,1)} async-done(((bf16[16,6,7168]{2,1,0:T(8,128)(2,1)}), bf16[16,6,7168]{2,1,0:T(8,128)(2,1)}, u32[]{:S(2)}, u32[]{:S(2)}) %all-to-all-start.1) | async-done | bytes 1376288 | tf_op jit(solution)/shard_map/all_to_all | solution.py:77
  73.2 3.2 %reshape.117 = f32[96,56,128]{2,1,0:T(8,128)S(1)} reshape(bf16[16,6,7168]{2,1,0:T(8,128)(2,1)} %all-to-all-done.1) | data formatting | bytes 4128768 | tf_op jit(solution)/shard_map/convert_element_type | solution.py:32
  76.5 0.9 multiply_convert_fusion
  77.4 4.4 %fusion.3 = f32[96,512]{1,0:T(8,128)S(1)} fusion(bf16[7168,512]{1,0:T(8,128)(2,1)} %bitcast.46, bf16[12,8,56,128]{3,2,1,0:T(8,128)(2,1)S(1)} %bitcast.50), kind=kOutput, calls=%fused_computation.8 | convolution fusion | flops 704643072 | bytes 8912896 | tf_op jit(solution)/shard_map/dot_general | solution.py:11
  81.9 3.8 %convolution_convert_fusion = bf16[96,7168]{1,0:T(8,128)(2,1)} fusion(bf16[96,256]{1,0:T(8,128)(2,1)S(1)} %reshape.113, bf16[1,256,7168]{2,1,0:T(8,128)(2,1)} %param.11), kind=kOutput, calls=%fused_computation | convolution fusion | flops 353009664 | bytes 5095424 | tf_op jit(solution)/shard_map/dot_general | solution.py:17
  86.6 3.6 %all-to-all-start = ((bf16[16,1,6]{2,1,0:T(2,128)(2,1)}), bf16[16,1,6]{2,1,0:T(2,128)(2,1)S(1)}, u32[]{:S(2)}, u32[]{:S(2)}) async-start(bf16[16,1,6]{2,1,0:T(2,128)(2,1)} %copy.41), calls=%async_computation.1 | async-start | bytes 16384 | tf_op jit(solution)/shard_map/all_to_all | solution.py:79
  90.3 10.4 %copy.50 = bf16[896,8,2,512]{3,1,2,0:T(8,128)(2,1)S(1)} copy(bf16[896,8,2,512]{3,2,1,0:T(2,128)(2,1)} %bitcast.49) | data formatting | bytes 29360128
  100.7 7.2 %all_gather.3 = bf16[32,7168]{1,0:T(8,128)(2,1)S(1)} all-gather(bf16[8,7168]{1,0:T(8,128)(2,1)S(1)} %copy-done), channel_id=1, replica_groups=mesh['groups'=2,'ep'=4,'sub'=4] {'ep'}, dimensions={0}, use_global_device_ids=true | all-gather | bytes 573440 | tf_op jit(solution)/shard_map/all_gather | solution.py:43
  107.8 2.6 %fusion.30 = f32[32,1024]{1,0:T(8,128)S(1)} fusion(bf16[32,7168]{1,0:T(8,128)(2,1)S(1)} %all_gather.3, bf16[7168,1024]{1,0:T(8,128)(2,1)S(1)} %bitcast.45), kind=kOutput, calls=%fused_computation.46 | convolution fusion | flops 469762048 | bytes 15269888 | tf_op jit(solution)/shard_map/dot_general | solution.py:11
  110.5 2.1 %convolution_convert_fusion.1 = bf16[32,7168]{1,0:T(8,128)(2,1)} fusion(bf16[512,7168]{1,0:T(8,128)(2,1)S(1)} %bitcast.48, f32[32,1024]{1,0:T(8,128)S(1)} %fusion.30), kind=kOutput, calls=%fused_computation.1 | convolution fusion | flops 235208704 | bytes 7929856 | tf_op jit(solution)/shard_map/dot_general | solution.py:17
  112.8 4.1 %reduce-scatter.5.cloned.1.call-done = bf16[24,7168]{1,0:T(8,128)(2,1)} async-done(((bf16[96,7168]{1,0:T(8,128)(2,1)}), bf16[24,7168]{1,0:T(8,128)(2,1)}) %reduce-scatter.5.cloned.1.call-update) | async-done | bytes 344080 | tf_op jit(solution)/shard_map/reduce_scatter | solution.py:92
  116.9 1.1 multiply_convert_fusion.1
  118.0 0.9 reshape.115
  118.9 3.5 %all-to-all-start.3 = ((bf16[4,6,7168]{2,1,0:T(8,128)(2,1)}), bf16[4,6,7168]{2,1,0:T(8,128)(2,1)S(1)}, u32[]{:S(2)}, u32[]{:S(2)}) async-start(bf16[4,6,7168]{2,1,0:T(8,128)(2,1)} %reshape.115), calls=%async_computation.5 | async-start | bytes 917504 | tf_op jit(solution)/shard_map/all_to_all | solution.py:100
  122.4 17.3 %reduce-scatter.3.cloned.1.call-done = bf16[8,7168]{1,0:T(8,128)(2,1)} async-done(((bf16[32,7168]{1,0:T(8,128)(2,1)}), bf16[8,7168]{1,0:T(8,128)(2,1)}) %reduce-scatter.3.cloned.1.call-update) | async-done | bytes 114704 | tf_op jit(solution)/shard_map/reduce_scatter | solution.py:45
  139.6 2.0 %fusion.1 = bf16[8,7168]{1,0:T(8,128)(2,1)} fusion(bf16[4,6,7168]{2,1,0:T(8,128)(2,1)S(1)} %all-to-all-done.3, bf16[8,7168]{1,0:T(8,128)(2,1)} %reduce-scatter.3.cloned.1.call-done, pred[8,4,6]{2,1,0:T(4,128)(4,1)S(1)} %fusion.15), kind=kOutput, calls=%fused_computation.5 | convolution fusion | flops 2924544 | bytes 573632 | tf_op jit(solution)/shard_map/dot_general | solution.py:101
  (51 shorter events, 3.3 us)
Async XLA Ops:
  9.7 13.8 %all-to-all-start.2 = ((bf16[16,2,168]{2,1,0:T(2,128)(2,1)}), bf16[16,2,168]{2,1,0:T(2,128)(2,1)S(1)}, u32[]{:S(2)}, u32[]{:S(2)}) async-start(bf16[16,2,168]{2,1,0:T(2,128)(2,1)} %reshape.130), calls=%async_computation.3 | async-start | bytes 32768 | tf_op jit(solution)/shard_map/all_to_all | solution.py:78
  25.0 48.3 %all-to-all-start.1 = ((bf16[16,6,7168]{2,1,0:T(8,128)(2,1)}), bf16[16,6,7168]{2,1,0:T(8,128)(2,1)}, u32[]{:S(2)}, u32[]{:S(2)}) async-start(bf16[16,6,7168]{2,1,0:T(8,128)(2,1)} %bitcast.7), calls=%async_computation.2 | async-start | bytes 3670016 | tf_op jit(solution)/shard_map/all_to_all | solution.py:77
  29.4 87.5 %reduce-scatter.5.cloned.1.call-start = ((), (), s32[]{:S(2)}) async-start(), calls=%async_computation.7 | async-start | bytes 1720320 | tf_op jit(solution)/shard_map/reduce_scatter | solution.py:92
  81.7 4.0 %copy-start.2 = (bf16[8,2]{0,1:T(2,128)(2,1)S(1)}, bf16[8,2]{0,1:T(2,128)(2,1)}, u32[]{:S(2)}) copy-start(bf16[8,2]{0,1:T(2,128)(2,1)} %param.9) | copy-start | bytes 100
  81.8 4.0 %copy-start.1 = (s32[8,2]{0,1:T(2,128)S(1)}, s32[8,2]{0,1:T(2,128)}, u32[]{:S(2)}) copy-start(s32[8,2]{0,1:T(2,128)} %param.8) | copy-start | bytes 196
  85.7 24.7 %slice-start = ((s8[7340032]{0:T(1024)(128)(4,1)}), s8[3145728]{0:T(1024)(128)(4,1)S(1)}, s32[]{:S(2)}) async-start(s8[7340032]{0:T(1024)(128)(4,1)} %bitcast.47), calls=%async_computation.8 | async-start | bytes 6291456
  86.6 26.1 %all-to-all-start = ((bf16[16,1,6]{2,1,0:T(2,128)(2,1)}), bf16[16,1,6]{2,1,0:T(2,128)(2,1)S(1)}, u32[]{:S(2)}, u32[]{:S(2)}) async-start(bf16[16,1,6]{2,1,0:T(2,128)(2,1)} %copy.41), calls=%async_computation.1 | async-start | bytes 16384 | tf_op jit(solution)/shard_map/all_to_all | solution.py:79
  90.2 49.5 %reduce-scatter.3.cloned.1.call-start = ((), (), s32[]{:S(2)}) async-start(), calls=%async_computation.6 | async-start | bytes 573440 | tf_op jit(solution)/shard_map/reduce_scatter | solution.py:45
  90.2 10.4 %copy-start = (bf16[8,7168]{1,0:T(8,128)(2,1)S(1)}, bf16[8,7168]{1,0:T(8,128)(2,1)}, u32[]{:S(2)}) copy-start(bf16[8,7168]{1,0:T(8,128)(2,1)} %param.7) | copy-start | bytes 344068
  90.2 20.2 %slice-start.1 = ((s8[7340032]{0:T(1024)(128)(4,1)}), s8[4194304]{0:T(1024)(128)(4,1)S(1)}, s32[]{:S(2)}) async-start(s8[7340032]{0:T(1024)(128)(4,1)} %bitcast.47), calls=%async_computation.9 | async-start | bytes 8388608
  118.9 20.8 %all-to-all-start.3 = ((bf16[4,6,7168]{2,1,0:T(8,128)(2,1)}), bf16[4,6,7168]{2,1,0:T(8,128)(2,1)S(1)}, u32[]{:S(2)}, u32[]{:S(2)}) async-start(bf16[4,6,7168]{2,1,0:T(8,128)(2,1)} %reshape.115), calls=%async_computation.5 | async-start | bytes 917504 | tf_op jit(solution)/shard_map/all_to_all | solution.py:100
Sparse Core Ops, SparseCore 0:
  85.9 30.9 reduce-scatter.4
  119.6 20.0 reduce-scatter.2
where the time goes:
time: 149 us; the launch traced here: 148 us
  waiting for transfers between devices  62.3 us (42%)
  local copies, waits for them, and re-layouts  25.8 us (17%)
  starting transfers between devices  19 us (13%)
  matrix products  16.5 us (11%)
  between operations  13.7 us (9%)
  blocking collectives  7.17 us (5%)
  other arithmetic  4.09 us (3%)
    all_to_all x1, waiting for transfers between devices, per_device(): lax.all_to_all(wide_rows, ('ep', 'sub'), split_axis=0, concat_axis=0, til...  36.3 us
    unnamed x15, local copies, waits for them, and re-layouts  18.6 us
    reduce_scatter x1, waiting for transfers between devices, per_device(): lax.psum_scatter(rounded_term(hidden_part, shared_down).astype(jnp.bfloat...  17.3 us
    all_to_all x1, starting transfers between devices, per_device(): lax.all_to_all(wide_scales, ('ep', 'sub'), split_axis=0, concat_axis=0, t...  7.39 us
    all_gather x1, blocking collectives, per_device(): lax.all_gather(tokens, 'ep', axis=0, tiled=True)  7.17 us
    dot_general x2, matrix products, hidden_rows(): projected = jnp.dot(token_rows, weights, preferred_element_type=jnp.float32)  6.98 us
    dot_general x2, matrix products, rounded_term(): jnp.dot(left, right, preferred_element_type=jnp.float32)  6 us
    all_to_all x1, waiting for transfers between devices, per_device(): lax.all_to_all(wide_scales, ('ep', 'sub'), split_axis=0, concat_axis=0, t...  4.56 us
  transfers between devices with their start and end apart: 6, of which 4 were waited for; matrix products, arithmetic and copies ran while one was open for 18% of the time, Pallas kernels for 0%

commit v1 on v0

v1 whole, which is shorter than its diff:
```python
import jax
import jax.numpy as jnp
from jax import lax
from jax.sharding import PartitionSpec as P

QBLOCK = 128
LANES = 128
CORES = 2


def silu_product(projected):
    half_width = projected.shape[1] // 2
    return (jax.nn.silu(projected[:, :half_width]) * projected[:, half_width:]).astype(jnp.bfloat16)


def block_restored(rows):
    count, width = rows.shape
    blocks = rows.astype(jnp.float32).reshape(count, width // QBLOCK, QBLOCK)
    largest = jnp.max(jnp.abs(blocks), axis=2)
    scale = ((largest + 1e-06) / 448.0).astype(jnp.bfloat16).astype(jnp.float32)[:, :, None]
    scaled = (blocks / scale).astype(jnp.bfloat16).astype(jnp.float32)
    return (scaled * scale).astype(jnp.bfloat16).reshape(count, width)


def exchange(rows, axis, flip):
    size = lax.axis_size(axis)
    return lax.ppermute(rows, axis, [(i, i ^ flip) for i in range(size)])


def gathered_ep(rows, experts):
    parts = [rows] + [exchange(rows, "ep", chip) for chip in range(CORES, experts, CORES)]
    half = jnp.concatenate(parts, axis=0)
    return jnp.concatenate([half, exchange(half, "ep", 1)], axis=0)


def summed_ep(partial, experts):
    half = partial.shape[0] // CORES
    other = exchange(partial[half:], "ep", 1)
    pair = (partial[:half].astype(jnp.float32) + other.astype(jnp.float32)).astype(jnp.bfloat16)
    count = half * CORES // experts
    total = pair[:count].astype(jnp.float32)
    for chip in range(CORES, experts, CORES):
        at = chip // CORES * count
        total = total + exchange(pair[at:at + count], "ep", chip).astype(jnp.float32)
    return total


def per_device(tokens, routes, gates, expert_up, expert_down, shared_up, shared_down):
    count, width = tokens.shape
    experts = lax.axis_size("ep")
    subs = lax.axis_size("sub")
    me = lax.axis_index("ep")
    bf = jnp.bfloat16

    lanes = -(-experts // LANES) * LANES
    chosen = routes[:, :, None] == jnp.arange(lanes, dtype=jnp.int32)
    weight = jnp.sum(jnp.where(chosen, gates[:, :, None], jnp.zeros((), bf)), axis=1)
    routed_rows = jnp.concatenate([block_restored(tokens), weight.astype(bf)], axis=1)
    own = jnp.concatenate([tokens, routed_rows], axis=1)

    far = [exchange(routed_rows, "sub", k) for k in range(subs - 1, 0, -1)]
    own_all = gathered_ep(own, experts)
    far_all = gathered_ep(jnp.concatenate(far, axis=0), experts)

    shared_weights = shared_up.reshape(width, -1)
    expert_weights = expert_up.reshape(width, -1)
    down_weights = expert_down.reshape(-1, width)

    def routed(rows):
        hidden = silu_product(jnp.dot(rows[:, :width], expert_weights, preferred_element_type=jnp.float32))
        out = jnp.dot(hidden, down_weights, preferred_element_type=jnp.float32)
        named = jnp.arange(lanes, dtype=jnp.int32) == me
        gate = jnp.sum(jnp.where(named, rows[:, width:].astype(jnp.float32), 0.0), axis=1)
        return gate[:, None] * out

    shared_hidden = silu_product(jnp.dot(own_all[:, :width], shared_weights, preferred_element_type=jnp.float32))
    own_part = jnp.dot(shared_hidden, shared_down, preferred_element_type=jnp.float32)
    own_part = (own_part + routed(own_all[:, width:])).astype(bf)
    far_part = routed(far_all).astype(bf)

    total = summed_ep(own_part, experts)
    far_sum = summed_ep(far_part, experts).astype(bf)
    for at, k in enumerate(range(subs - 1, 0, -1)):
        total = total + exchange(far_sum[at * count:(at + 1) * count], "sub", k).astype(jnp.float32)
    return total.astype(bf)


def solution(mesh):
    return jax.shard_map(
        per_device,
        mesh=mesh,
        in_specs=(
            P(("groups", "ep", "sub"), None),
            P(("groups", "ep", "sub"), None),
            P(("groups", "ep", "sub"), None),
            P("ep", None, None, "sub"),
            P("ep", "sub", None),
            P(None, None, "ep"),
            P("ep", None),
        ),
        out_specs=P(("groups", "ep", "sub"), None),
        check_vma=False,
    )
```

time: 149 us -> 70.2 us (0.47)
  waiting for transfers between devices: 62.3 us -> 25.6 us
  between operations: 13.7 us -> 0.28 us
  local copies, waits for them, and re-layouts: 25.8 us -> 16.1 us
  matrix products: 16.5 us -> 8.13 us
  blocking collectives: 7.17 us -> 0 us
  starting transfers between devices: 19 us -> 14.5 us
    all_to_all x4 -> x0, waiting for transfers between devices: 40.9 us -> none  [the longest x1 36.3 us: per_device(): lax.all_to_all(wide_rows, ('ep', 'sub'), split_axis=0, concat_axis=0, til...]
    ppermute x0 -> x14, waiting for transfers between devices: none -> 25.6 us  [exchange(): return lax.ppermute(rows, axis, [(i, i ^ flip) for i in range(size)])]
    reduce_scatter x2 -> x0, waiting for transfers between devices: 21.4 us -> none  [the longest x1 17.3 us: per_device(): lax.psum_scatter(rounded_term(hidden_part, shared_down).astype(jnp.bfloat...]
    all_to_all x4 -> x0, starting transfers between devices: 18.9 us -> none  [the longest x1 7.39 us: per_device(): lax.all_to_all(wide_scales, ('ep', 'sub'), split_axis=0, concat_axis=0, t...]
    ppermute x0 -> x14, starting transfers between devices: none -> 14.5 us  [exchange(): return lax.ppermute(rows, axis, [(i, i ^ flip) for i in range(size)])]
    dot_general x8 -> x6, matrix products: 16.5 us -> 8.13 us  [the longest x1 2.67 us: per_device(): jnp.dot(own_all[:, :width], shared_weights, preferred_element_type=jnp.fl...]
    all_gather x1 -> x0, blocking collectives: 7.17 us -> none  [per_device(): lax.all_gather(tokens, 'ep', axis=0, tiled=True)]
    convert_element_type x4 -> x1, local copies, waits for them, and re-layouts: 3.43 us -> 0.09 us  [block_restored(): ((largest + 1e-06) / 448.0).astype(jnp.bfloat16).astype(jnp.float32)]
  transfers between devices with their start and end apart: 6 -> 14, of which waited for: 4 -> 6; matrix products, arithmetic and copies ran while one was open for 18% -> 32% of each run, Pallas kernels for 0% -> 0%
where the time goes in v1:
time: 70.2 us; the launch traced here: 69.8 us
  waiting for transfers between devices  25.6 us (36%)
  local copies, waits for them, and re-layouts  16.1 us (23%)
  starting transfers between devices  14.5 us (21%)
  matrix products  8.13 us (12%)
  other arithmetic  5.2 us (7%)
    ppermute x14, waiting for transfers between devices, exchange(): return lax.ppermute(rows, axis, [(i, i ^ flip) for i in range(size)])  25.6 us
    unnamed x14, local copies, waits for them, and re-layouts  15.7 us
    ppermute x14, starting transfers between devices, exchange(): return lax.ppermute(rows, axis, [(i, i ^ flip) for i in range(size)])  14.5 us
    dot_general x1, matrix products, per_device(): jnp.dot(own_all[:, :width], shared_weights, preferred_element_type=jnp.fl...  2.67 us
    dot_general x2, matrix products, routed(): jnp.dot(rows[:, :width], expert_weights, preferred_element_type=jnp.float32)  2.63 us
    dot_general x2, matrix products, routed(): out = jnp.dot(hidden, down_weights, preferred_element_type=jnp.float32)  1.47 us
  transfers between devices with their start and end apart: 14, of which 6 were waited for; matrix products, arithmetic and copies ran while one was open for 32% of the time, Pallas kernels for 0%

profile of v1, /device:TPU:0, one launch (start us, length us, event | category | flops | bytes accessed | tf_op | source)
XLA Modules:
  0.0 69.8 jit_solution(11723480951900242546)
XLA Ops:
  0.0 1.0 %fusion.20 = f32[8,56]{0,1:T(8,128)S(1)} fusion(bf16[8,7168]{1,0:T(8,128)(2,1)} %param.7), kind=kLoop, calls=%fused_computation.33 | loop fusion | flops 171584 | bytes 116480 | tf_op jit(solution)/shard_map/reduce_max | solution.py:19
  1.2 1.0 %fusion.22 = bf16[8,7168]{1,0:T(8,128)(2,1)S(1)} fusion(bf16[8,7168]{1,0:T(8,128)(2,1)} %param.7, f32[8,56]{0,1:T(8,128)S(1)} %copy.12), kind=kLoop, calls=%fused_computation.35 | loop fusion | flops 344064 | bytes 231168 | tf_op jit(solution)/shard_map/convert_element_type | solution.py:22
  2.2 0.8 %fusion.34 = bf16[8,128]{1,0:T(8,128)(2,1)S(1)} fusion(s32[8,2]{0,1:T(2,128)} %param.8, bf16[8,2]{0,1:T(2,128)(2,1)} %param.9), kind=kLoop, calls=%fused_computation.57 | loop fusion | flops 5120 | bytes 2144 | tf_op jit(solution)/shard_map/reduce_sum | solution.py:57
  3.0 3.1 %collective-permute-start.6 = (bf16[8,7296]{1,0:T(8,128)(2,1)S(1)}, bf16[8,7296]{1,0:T(8,128)(2,1)S(1)}, u32[]{:S(2)}, u32[]{:S(2)}) collective-permute-start(bf16[8,7296]{1,0:T(8,128)(2,1)S(1)} %pad_maximum_fusion.5), channel_id=1, source_target_pairs={{0,1},{1,0},{2,3},{3,2},{4,5},{5,4},{6,7},{7,6},{8,9},{9,8},{10,11... | collective-permute-start | bytes 350216 | tf_op jit(solution)/shard_map/ppermute | solution.py:27
  6.1 2.6 %collective-permute-start.5 = (bf16[8,7296]{1,0:T(8,128)(2,1)S(1)}, bf16[8,7296]{1,0:T(8,128)(2,1)S(1)}, u32[]{:S(2)}, u32[]{:S(2)}) collective-permute-start(bf16[8,7296]{1,0:T(8,128)(2,1)S(1)} %pad_maximum_fusion.5), channel_id=1, source_target_pairs={{0,2},{1,3},{2,0},{3,1},{4,6},{5,7},{6,4},{7,5},{8,10},{9,11},{10,... | collective-permute-start | bytes 350216 | tf_op jit(solution)/shard_map/ppermute | solution.py:27
  8.7 0.9 %pad_maximum_fusion.4 = bf16[8,14464]{1,0:T(8,128)(2,1)S(1)} fusion(bf16[8,128]{1,0:T(8,128)(2,1)S(1)} %fusion.34, bf16[8,7168]{1,0:T(8,128)(2,1)S(1)} %fusion.22, bf16[8,7168]{1,0:T(8,128)(2,1)} %param.7), kind=kLoop, calls=%fused_computation.31 | loop fusion | flops 694272 | bytes 462848 | tf_op jit(solution)/shard_map/concatenate | solution.py:59
  9.6 1.8 %collective-permute-start = (bf16[8,14464]{1,0:T(8,128)(2,1)S(1)}, bf16[8,14464]{1,0:T(8,128)(2,1)S(1)}, u32[]{:S(2)}, u32[]{:S(2)}) collective-permute-start(bf16[8,14464]{1,0:T(8,128)(2,1)S(1)} %pad_maximum_fusion.4), channel_id=1, source_target_pairs={{0,8},{4,12},{8,0},{12,4},{1,9},{5,13},{9,1},{13,5},{2,10},{6,14},... | collective-permute-start | bytes 694280 | tf_op jit(solution)/shard_map/ppermute | solution.py:27
  11.4 4.4 %copy.14 = bf16[896,8,2,256]{3,1,2,0:T(8,128)(2,1)S(1)} copy(bf16[896,8,2,256]{3,2,1,0:T(2,128)(2,1)} %bitcast.33) | data formatting | bytes 14680064
  15.8 10.2 %copy.13 = bf16[896,8,2,512]{3,1,2,0:T(8,128)(2,1)S(1)} copy(bf16[896,8,2,512]{3,2,1,0:T(2,128)(2,1)} %bitcast.32) | data formatting | bytes 29360128
  26.6 8.4 %collective-permute-done.7 = bf16[24,7296]{1,0:T(8,128)(2,1)S(1)} collective-permute-done((bf16[24,7296]{1,0:T(8,128)(2,1)S(1)}, bf16[24,7296]{1,0:T(8,128)(2,1)S(1)}, u32[]{:S(2)}, u32[]{:S(2)}) %collective-permute-start.7) | collective-permute-done | bytes 350240 | tf_op jit(solution)/shard_map/ppermute | solution.py:27
  35.3 2.7 %fusion.17 = f32[32,1024]{1,0:T(8,128)S(1)} fusion(bf16[7168,1024]{1,0:T(8,128)(2,1)S(1)} %bitcast.29, bf16[32,14464]{1,0:T(8,128)(2,1)S(1)} %pad_maximum_fusion), kind=kOutput, calls=%fused_computation.24 | convolution fusion | flops 469762048 | bytes 15269888 | tf_op jit(solution)/shard_map/dot_general | solution.py:76
  38.4 1.4 %fusion.27 = f32[32,7168]{1,0:T(8,128)S(1)} fusion(bf16[512,7168]{1,0:T(8,128)(2,1)S(1)} %bitcast.31, f32[32,1024]{1,0:T(8,128)S(1)} %fusion.17), kind=kOutput, calls=%fused_computation.44 | convolution fusion | flops 234979328 | bytes 8388608 | tf_op jit(solution)/shard_map/dot_general | solution.py:77
  40.0 1.3 %fusion.5 = f32[96,512]{1,0:T(8,128)S(1)} fusion(bf16[7168,512]{1,0:T(8,128)(2,1)S(1)} %bitcast.27, bf16[96,7296]{1,0:T(8,128)(2,1)S(1)} %constant_dynamic-update-slice_fusion), kind=kOutput, calls=%fused_computation.7 | convolution fusion | flops 704643072 | bytes 8912896 | tf_op jit(solution)/shard_map/dot_general | solution.py:70
  41.3 0.7 %copy-done = bf16[1,256,7168]{2,1,0:T(8,128)(2,1)S(1)} copy-done((bf16[1,256,7168]{2,1,0:T(8,128)(2,1)S(1)}, bf16[1,256,7168]{2,1,0:T(8,128)(2,1)}, u32[]{:S(2)}) %copy-start) | copy-done | bytes 3670040
  43.3 1.3 %fusion.7 = f32[32,512]{1,0:T(8,128)S(1)} fusion(bf16[7168,512]{1,0:T(8,128)(2,1)S(1)} %bitcast.28, bf16[16,14464]{1,0:T(8,128)(2,1)S(1)} %collective-permute-done.1, bf16[8,14464]{1,0:T(8,128)(2,1)S(1)} %collective-permute-done, bf16[8,128]{1,0:T(8,128)(2,1)S(1)} %fusion.34, bf16[8,7168]{1,0:T(8,128)(2,1)S(1)} %fusion.22, bf16[8,7168]{1,0:T(8,128)(2,1)S(1)} %copy-done.1), kind=kOutput, calls=%fused_computation.14 | convolution fusion | flops 237174784 | bytes 8331264 | tf_op jit(solution)/shard_map/dot_general | solution.py:70
  44.7 0.8 %fusion.2 = bf16[32,7168]{1,0:T(8,128)(2,1)S(1)} fusion(f32[32,7168]{1,0:T(8,128)S(1)} %fusion.27, bf16[1,256,7168]{2,1,0:T(8,128)(2,1)S(1)} %copy-done, f32[32]{0:T(128)S(1)} %select_reduce_fusion.1, f32[32,512]{1,0:T(8,128)S(1)} %fusion.7), kind=kOutput, calls=%fused_computation.4 | convolution fusion | flops 118177792 | bytes 5111936 | tf_op jit(solution)/shard_map/dot_general | solution.py:71
  47.1 0.9 %collective-permute-start.3 = (bf16[8,7168]{1,0:T(8,128)(2,1)S(1)}, bf16[8,7168]{1,0:T(8,128)(2,1)S(1)}, u32[]{:S(2)}, u32[]{:S(2)}) collective-permute-start(bf16[8,7168]{1,0:T(8,128)(2,1)S(1)} %slice.99), channel_id=1, source_target_pairs={{0,8},{4,12},{8,0},{12,4},{1,9},{5,13},{9,1},{13,5},{2,10},{6,14},... | collective-permute-start | bytes 344072 | tf_op jit(solution)/shard_map/ppermute | solution.py:27
  48.0 8.7 %collective-permute-done.10 = bf16[24,7168]{1,0:T(8,128)(2,1)S(1)} collective-permute-done((bf16[24,7168]{1,0:T(8,128)(2,1)S(1)}, bf16[24,7168]{1,0:T(8,128)(2,1)S(1)}, u32[]{:S(2)}, u32[]{:S(2)}) %collective-permute-start.10) | collective-permute-done | bytes 344096 | tf_op jit(solution)/shard_map/ppermute | solution.py:27
  56.8 3.6 %collective-permute-start.11 = (bf16[8,7168]{1,0:T(8,128)(2,1)S(1)}, bf16[8,7168]{1,0:T(8,128)(2,1)S(1)}, u32[]{:S(2)}, u32[]{:S(2)}) collective-permute-start(bf16[8,7168]{1,0:T(8,128)(2,1)S(1)} %get-tuple-element.5), channel_id=1, source_target_pairs={{0,3},{1,2},{2,1},{3,0},{4,7},{5,6},{6,5},{7,4},{8,11},{9,10},{10,... | collective-permute-start | bytes 344072 | tf_op jit(solution)/shard_map/ppermute | solution.py:27
  60.4 0.8 %collective-permute-start.12 = (bf16[8,7168]{1,0:T(8,128)(2,1)S(1)}, bf16[8,7168]{1,0:T(8,128)(2,1)S(1)}, u32[]{:S(2)}, u32[]{:S(2)}) collective-permute-start(bf16[8,7168]{1,0:T(8,128)(2,1)S(1)} %get-tuple-element.7), channel_id=1, source_target_pairs={{0,2},{1,3},{2,0},{3,1},{4,6},{5,7},{6,4},{7,5},{8,10},{9,11},{10,... | collective-permute-start | bytes 344072 | tf_op jit(solution)/shard_map/ppermute | solution.py:27
  61.3 3.2 %collective-permute-done.11 = bf16[8,7168]{1,0:T(8,128)(2,1)S(1)} collective-permute-done((bf16[8,7168]{1,0:T(8,128)(2,1)S(1)}, bf16[8,7168]{1,0:T(8,128)(2,1)S(1)}, u32[]{:S(2)}, u32[]{:S(2)}) %collective-permute-start.11) | collective-permute-done | bytes 114720 | tf_op jit(solution)/shard_map/ppermute | solution.py:27
  64.4 2.6 %collective-permute-done.13 = bf16[8,7168]{1,0:T(8,128)(2,1)S(1)} collective-permute-done((bf16[8,7168]{1,0:T(8,128)(2,1)S(1)}, bf16[8,7168]{1,0:T(8,128)(2,1)S(1)}, u32[]{:S(2)}, u32[]{:S(2)}) %collective-permute-start.13) | collective-permute-done | bytes 114720 | tf_op jit(solution)/shard_map/ppermute | solution.py:27
  67.1 2.0 %collective-permute-done.12 = bf16[8,7168]{1,0:T(8,128)(2,1)S(1)} collective-permute-done((bf16[8,7168]{1,0:T(8,128)(2,1)S(1)}, bf16[8,7168]{1,0:T(8,128)(2,1)S(1)}, u32[]{:S(2)}, u32[]{:S(2)}) %collective-permute-start.12) | collective-permute-done | bytes 114720 | tf_op jit(solution)/shard_map/ppermute | solution.py:27
  69.1 0.7 %add_convert_fusion.3 = bf16[8,7168]{1,0:T(8,128)(2,1)} fusion(bf16[8,7168]{1,0:T(8,128)(2,1)S(1)} %collective-permute-done.13, bf16[8,7168]{1,0:T(8,128)(2,1)S(1)} %collective-permute-done.12, bf16[8,7168]{1,0:T(8,128)(2,1)S(1)} %collective-permute-done.11, bf16[8,7168]{1,0:T(8,128)(2,1)S(1)} %collective-permute-done.3, ...), kind=kLoop, calls=%fused_computation.36 | loop fusion | flops 573440 | bytes 688128 | tf_op jit(solution)/shard_map/convert_element_type | solution.py:85
  (50 shorter events, 4.6 us)
Async XLA Ops:
  3.0 23.0 %collective-permute-start.6 = (bf16[8,7296]{1,0:T(8,128)(2,1)S(1)}, bf16[8,7296]{1,0:T(8,128)(2,1)S(1)}, u32[]{:S(2)}, u32[]{:S(2)}) collective-permute-start(bf16[8,7296]{1,0:T(8,128)(2,1)S(1)} %pad_maximum_fusion.5), channel_id=1, source_target_pairs={{0,1},{1,0},{2,3},{3,2},{4,5},{5,4},{6,7},{7,6},{8,9},{9,8},{10,11... | collective-permute-start | bytes 350216 | tf_op jit(solution)/shard_map/ppermute | solution.py:27
  6.1 19.9 %collective-permute-start.5 = (bf16[8,7296]{1,0:T(8,128)(2,1)S(1)}, bf16[8,7296]{1,0:T(8,128)(2,1)S(1)}, u32[]{:S(2)}, u32[]{:S(2)}) collective-permute-start(bf16[8,7296]{1,0:T(8,128)(2,1)S(1)} %pad_maximum_fusion.5), channel_id=1, source_target_pairs={{0,2},{1,3},{2,0},{3,1},{4,6},{5,7},{6,4},{7,5},{8,10},{9,11},{10,... | collective-permute-start | bytes 350216 | tf_op jit(solution)/shard_map/ppermute | solution.py:27
  8.7 17.4 %collective-permute-start.4 = (bf16[8,7296]{1,0:T(8,128)(2,1)S(1)}, bf16[8,7296]{1,0:T(8,128)(2,1)S(1)}, u32[]{:S(2)}, u32[]{:S(2)}) collective-permute-start(bf16[8,7296]{1,0:T(8,128)(2,1)S(1)} %pad_maximum_fusion.5), channel_id=1, source_target_pairs={{0,3},{1,2},{2,1},{3,0},{4,7},{5,6},{6,5},{7,4},{8,11},{9,10},{10,... | collective-permute-start | bytes 350216 | tf_op jit(solution)/shard_map/ppermute | solution.py:27
  9.6 16.9 %collective-permute-start = (bf16[8,14464]{1,0:T(8,128)(2,1)S(1)}, bf16[8,14464]{1,0:T(8,128)(2,1)S(1)}, u32[]{:S(2)}, u32[]{:S(2)}) collective-permute-start(bf16[8,14464]{1,0:T(8,128)(2,1)S(1)} %pad_maximum_fusion.4), channel_id=1, source_target_pairs={{0,8},{4,12},{8,0},{12,4},{1,9},{5,13},{9,1},{13,5},{2,10},{6,14},... | collective-permute-start | bytes 694280 | tf_op jit(solution)/shard_map/ppermute | solution.py:27
  15.8 10.7 %copy-start.1 = (bf16[8,7168]{1,0:T(8,128)(2,1)S(1)}, bf16[8,7168]{1,0:T(8,128)(2,1)}, u32[]{:S(2)}) copy-start(bf16[8,7168]{1,0:T(8,128)(2,1)} %param.7) | copy-start | bytes 344068
  26.1 8.9 %collective-permute-start.7 = (bf16[24,7296]{1,0:T(8,128)(2,1)S(1)}, bf16[24,7296]{1,0:T(8,128)(2,1)S(1)}, u32[]{:S(2)}, u32[]{:S(2)}) collective-permute-start(bf16[24,7296]{1,0:T(8,128)(2,1)S(1)} %pad_maximum_fusion.3), channel_id=1, source_target_pairs={{0,8},{4,12},{8,0},{12,4},{1,9},{5,13},{9,1},{13,5},{2,10},{6,14},... | collective-permute-start | bytes 1050632 | tf_op jit(solution)/shard_map/ppermute | solution.py:27
  26.6 8.6 %collective-permute-start.1 = (bf16[16,14464]{1,0:T(8,128)(2,1)S(1)}, bf16[16,14464]{1,0:T(8,128)(2,1)S(1)}, u32[]{:S(2)}, u32[]{:S(2)}) collective-permute-start(bf16[16,14464]{1,0:T(8,128)(2,1)S(1)} %pad_maximum_fusion.2), channel_id=1, source_target_pairs={{0,4},{4,0},{8,12},{12,8},{1,5},{5,1},{9,13},{13,9},{2,6},{6,2},{1... | collective-permute-start | bytes 1388552 | tf_op jit(solution)/shard_map/ppermute | solution.py:27
  35.1 4.7 %collective-permute-start.8 = (bf16[48,7296]{1,0:T(8,128)(2,1)S(1)}, bf16[48,7296]{1,0:T(8,128)(2,1)S(1)}, u32[]{:S(2)}, u32[]{:S(2)}) collective-permute-start(bf16[48,7296]{1,0:T(8,128)(2,1)S(1)} %pad_maximum_fusion.1), channel_id=1, source_target_pairs={{0,4},{4,0},{8,12},{12,8},{1,5},{5,1},{9,13},{13,9},{2,6},{6,2},{1... | collective-permute-start | bytes 2101256 | tf_op jit(solution)/shard_map/ppermute | solution.py:27
  35.2 2.9 %slice-start = ((s8[7340032]{0:T(1024)(128)(4,1)}), s8[4194304]{0:T(1024)(128)(4,1)S(1)}, s32[]{:S(2)}) async-start(s8[7340032]{0:T(1024)(128)(4,1)} %bitcast.30), calls=%async_computation | async-start | bytes 8388608
  35.3 3.1 %slice-start.1 = ((s8[7340032]{0:T(1024)(128)(4,1)}), s8[3145728]{0:T(1024)(128)(4,1)S(1)}, s32[]{:S(2)}) async-start(s8[7340032]{0:T(1024)(128)(4,1)} %bitcast.30), calls=%async_computation.1 | async-start | bytes 6291456
  40.0 2.0 %copy-start = (bf16[1,256,7168]{2,1,0:T(8,128)(2,1)S(1)}, bf16[1,256,7168]{2,1,0:T(8,128)(2,1)}, u32[]{:S(2)}) copy-start(bf16[1,256,7168]{2,1,0:T(8,128)(2,1)} %param.11) | copy-start | bytes 11010052
  42.8 2.8 %collective-permute-start.9 = (bf16[48,7168]{1,0:T(8,128)(2,1)S(1)}, bf16[48,7168]{1,0:T(8,128)(2,1)S(1)}, u32[]{:S(2)}, u32[]{:S(2)}) collective-permute-start(bf16[48,7168]{1,0:T(8,128)(2,1)S(1)} %slice.105), channel_id=1, source_target_pairs={{0,4},{4,0},{8,12},{12,8},{1,5},{5,1},{9,13},{13,9},{2,6},{6,2},{1... | collective-permute-start | bytes 2064392 | tf_op jit(solution)/shard_map/ppermute | solution.py:27
  45.5 1.6 %collective-permute-start.2 = (bf16[16,7168]{1,0:T(8,128)(2,1)S(1)}, bf16[16,7168]{1,0:T(8,128)(2,1)S(1)}, u32[]{:S(2)}, u32[]{:S(2)}) collective-permute-start(bf16[16,7168]{1,0:T(8,128)(2,1)S(1)} %slice.97), channel_id=1, source_target_pairs={{0,4},{4,0},{8,12},{12,8},{1,5},{5,1},{9,13},{13,9},{2,6},{6,2},{1... | collective-permute-start | bytes 688136 | tf_op jit(solution)/shard_map/ppermute | solution.py:27
  45.8 10.9 %collective-permute-start.10 = (bf16[24,7168]{1,0:T(8,128)(2,1)S(1)}, bf16[24,7168]{1,0:T(8,128)(2,1)S(1)}, u32[]{:S(2)}, u32[]{:S(2)}) collective-permute-start(bf16[24,7168]{1,0:T(8,128)(2,1)S(1)} %slice.107), channel_id=1, source_target_pairs={{0,8},{4,12},{8,0},{12,4},{1,9},{5,13},{9,1},{13,5},{2,10},{6,14},... | collective-permute-start | bytes 1032200 | tf_op jit(solution)/shard_map/ppermute | solution.py:27
  47.1 14.2 %collective-permute-start.3 = (bf16[8,7168]{1,0:T(8,128)(2,1)S(1)}, bf16[8,7168]{1,0:T(8,128)(2,1)S(1)}, u32[]{:S(2)}, u32[]{:S(2)}) collective-permute-start(bf16[8,7168]{1,0:T(8,128)(2,1)S(1)} %slice.99), channel_id=1, source_target_pairs={{0,8},{4,12},{8,0},{12,4},{1,9},{5,13},{9,1},{13,5},{2,10},{6,14},... | collective-permute-start | bytes 344072 | tf_op jit(solution)/shard_map/ppermute | solution.py:27
  56.8 7.6 %collective-permute-start.11 = (bf16[8,7168]{1,0:T(8,128)(2,1)S(1)}, bf16[8,7168]{1,0:T(8,128)(2,1)S(1)}, u32[]{:S(2)}, u32[]{:S(2)}) collective-permute-start(bf16[8,7168]{1,0:T(8,128)(2,1)S(1)} %get-tuple-element.5), channel_id=1, source_target_pairs={{0,3},{1,2},{2,1},{3,0},{4,7},{5,6},{6,5},{7,4},{8,11},{9,10},{10,... | collective-permute-start | bytes 344072 | tf_op jit(solution)/shard_map/ppermute | solution.py:27
  60.4 6.7 %collective-permute-start.13 = (bf16[8,7168]{1,0:T(8,128)(2,1)S(1)}, bf16[8,7168]{1,0:T(8,128)(2,1)S(1)}, u32[]{:S(2)}, u32[]{:S(2)}) collective-permute-start(bf16[8,7168]{1,0:T(8,128)(2,1)S(1)} %get-tuple-element.6), channel_id=1, source_target_pairs={{0,1},{1,0},{2,3},{3,2},{4,5},{5,4},{6,7},{7,6},{8,9},{9,8},{10,11... | collective-permute-start | bytes 344072 | tf_op jit(solution)/shard_map/ppermute | solution.py:27
  60.4 8.7 %collective-permute-start.12 = (bf16[8,7168]{1,0:T(8,128)(2,1)S(1)}, bf16[8,7168]{1,0:T(8,128)(2,1)S(1)}, u32[]{:S(2)}, u32[]{:S(2)}) collective-permute-start(bf16[8,7168]{1,0:T(8,128)(2,1)S(1)} %get-tuple-element.7), channel_id=1, source_target_pairs={{0,2},{1,3},{2,0},{3,1},{4,6},{5,7},{6,4},{7,5},{8,10},{9,11},{10,... | collective-permute-start | bytes 344072 | tf_op jit(solution)/shard_map/ppermute | solution.py:27

commit v2 on v1

v2 whole, which is shorter than its diff:
```python
import jax
import jax.numpy as jnp
from jax import lax
from jax.experimental import pallas as pl
from jax.experimental.pallas import tpu as pltpu
from jax.sharding import PartitionSpec as P

QBLOCK = 128
LANES = 128
CORES = 2


def silu_product(projected):
    half_width = projected.shape[1] // 2
    return (jax.nn.silu(projected[:, :half_width]) * projected[:, half_width:]).astype(jnp.bfloat16)


def owner_kernel(tokens_ref, routes_ref, gates_ref, ready_ref, routed_ref, tokens, routes, gates, sems):
    del ready_ref
    copies = [
        pltpu.make_async_copy(source, target, sems.at[i])
        for i, (source, target) in enumerate(
            ((tokens_ref, tokens), (routes_ref, routes), (gates_ref, gates))
        )
    ]
    for copy in copies:
        copy.start()
    for copy in copies:
        copy.wait()
    count, width = tokens.shape
    for at in range(0, width, QBLOCK):
        block = tokens[:, at:at + QBLOCK].astype(jnp.float32)
        largest = jnp.max(jnp.abs(block), axis=1, keepdims=True)
        scale = ((largest + 1e-06) / 448.0).astype(jnp.bfloat16).astype(jnp.float32)
        scaled = (block / scale).astype(jnp.bfloat16).astype(jnp.float32)
        routed_ref[:, at:at + QBLOCK] = (scaled * scale).astype(jnp.bfloat16)
    lanes = routed_ref.shape[1] - width
    expert = lax.broadcasted_iota(jnp.int32, (count, lanes), 1)
    diagonal = (
        lax.broadcasted_iota(jnp.int32, (count, count), 0)
        == lax.broadcasted_iota(jnp.int32, (count, count), 1)
    )

    def column(row):
        return jnp.sum(jnp.where(diagonal, row, 0), axis=1, keepdims=True)

    weight = jnp.zeros((count, lanes), jnp.float32)
    for k in range(routes.shape[0]):
        gate = column(gates[k:k + 1, :].astype(jnp.float32))
        named = column(routes[k:k + 1, :])
        weight = weight + jnp.where(named == expert, gate, 0.0)
    routed_ref[:, width:] = weight.astype(jnp.bfloat16)


def owner_rows(tokens, routes, gates, ready, lanes):
    count, width = tokens.shape
    operands = (tokens, routes.T, gates.T)
    return pl.pallas_call(
        owner_kernel,
        in_specs=[pl.BlockSpec(memory_space=pltpu.HBM)] * 3 + [pl.BlockSpec(memory_space=pl.ANY)],
        out_specs=pl.BlockSpec(memory_space=pltpu.VMEM),
        out_shape=jax.ShapeDtypeStruct((count, width + lanes), tokens.dtype),
        scratch_shapes=[pltpu.VMEM(x.shape, x.dtype) for x in operands]
        + [pltpu.SemaphoreType.DMA((len(operands),))],
        compiler_params=pltpu.CompilerParams(vmem_limit_bytes=4 << 20),
    )(*(pltpu.with_memory_space_constraint(x, pltpu.HBM) for x in operands), ready)


def split_kernel(pair_ref, ready_ref, flat_ref, raw, sems):
    del ready_ref
    step, steps = pl.program_id(0), pl.num_programs(0)
    block, hidden = flat_ref.shape[0], pair_ref.shape[2]

    def fetch(i):
        rows = pl.ds(i * block, block)
        return pltpu.make_async_copy(pair_ref.at[rows], raw.at[rows], sems.at[i])

    @pl.when(step == 0)
    def _():
        for i in range(sems.shape[0]):
            fetch(i).start()

    fetch(step).wait()
    both = jnp.swapaxes(raw[pl.ds(step * block, block)], 0, 1)
    flat_ref[:, :hidden] = both[0]
    flat_ref[:, hidden:] = both[1]


def flat_pairs(pairs, ready, steps):
    depth, _, hidden = pairs.shape
    block = depth // steps
    return pl.pallas_call(
        split_kernel,
        grid=(steps,),
        in_specs=[pl.BlockSpec(memory_space=pltpu.HBM), pl.BlockSpec(memory_space=pl.ANY)],
        out_specs=pl.BlockSpec((block, 2 * hidden), lambda i: (i, 0)),
        out_shape=jax.ShapeDtypeStruct((depth, 2 * hidden), pairs.dtype),
        scratch_shapes=[pltpu.VMEM(pairs.shape, pairs.dtype), pltpu.SemaphoreType.DMA((steps,))],
        compiler_params=pltpu.CompilerParams(vmem_limit_bytes=16 << 20),
        cost_estimate=pl.CostEstimate(
            flops=0, bytes_accessed=8 * depth * hidden, transcendentals=0
        ),
    )(pltpu.with_memory_space_constraint(pairs, pltpu.HBM), ready)


def shared_up_kernel(rows_ref, up_ref, ready_ref, middle_ref, up, sums, sems):
    del ready_ref
    steps = sems.shape[0]
    block = up.shape[0] // steps

    def fetch(i):
        at = pl.ds(i * block, block)
        return pltpu.make_async_copy(up_ref.at[at], up.at[at], sems.at[i])

    for i in range(steps):
        fetch(i).start()
    for i in range(steps):
        fetch(i).wait()
        both = jnp.swapaxes(up[i * block:(i + 1) * block], 0, 1)
        left = rows_ref[:, i * block:(i + 1) * block]
        for half in range(2):
            term = jnp.dot(left, both[half], preferred_element_type=jnp.float32)
            sums[half] = term if i == 0 else sums[half] + term
    gate, lift = sums[0], sums[1]
    middle_ref[...] = (gate / (1.0 + jnp.exp(-gate)) * lift).astype(jnp.bfloat16)


def shared_middle(rows, up, ready):
    count, (width, _, hidden) = rows.shape[0], up.shape
    steps = 7
    return pl.pallas_call(
        shared_up_kernel,
        in_specs=[
            pl.BlockSpec(memory_space=pltpu.VMEM),
            pl.BlockSpec(memory_space=pltpu.HBM),
            pl.BlockSpec(memory_space=pl.ANY),
        ],
        out_specs=pl.BlockSpec(memory_space=pltpu.VMEM),
        out_shape=jax.ShapeDtypeStruct((count, hidden), jnp.bfloat16),
        scratch_shapes=[
            pltpu.VMEM(up.shape, up.dtype),
            pltpu.VMEM((2, count, hidden), jnp.float32),
            pltpu.SemaphoreType.DMA((steps,)),
        ],
        compiler_params=pltpu.CompilerParams(vmem_limit_bytes=20 << 20),
        cost_estimate=pl.CostEstimate(
            flops=4 * count * hidden * width,
            bytes_accessed=4 * hidden * width,
            transcendentals=0,
        ),
    )(rows, pltpu.with_memory_space_constraint(up, pltpu.HBM), ready)


def after(value, ready):
    return lax.optimization_barrier((value, ready))[0]


def exchange(rows, axis, flip):
    size = lax.axis_size(axis)
    return lax.ppermute(rows, axis, [(i, i ^ flip) for i in range(size)])


def half_ep(rows, experts):
    parts = [exchange(rows, "ep", chip) for chip in range(CORES, experts, CORES)]
    return jnp.concatenate([rows] + parts, axis=0)


def summed_ep(partial, experts):
    half = partial.shape[0] // CORES
    other = exchange(partial[half:], "ep", 1)
    pair = (partial[:half].astype(jnp.float32) + other.astype(jnp.float32)).astype(jnp.bfloat16)
    count = half * CORES // experts
    total = pair[:count].astype(jnp.float32)
    for chip in range(CORES, experts, CORES):
        at = chip // CORES * count
        total = total + exchange(pair[at:at + count], "ep", chip).astype(jnp.float32)
    return total


def per_device(tokens, routes, gates, expert_up, expert_down, shared_up, shared_down):
    count, width = tokens.shape
    experts = lax.axis_size("ep")
    subs = lax.axis_size("sub")
    me = lax.axis_index("ep")
    bf = jnp.bfloat16

    lanes = -(-experts // LANES) * LANES
    named = (jnp.arange(lanes, dtype=jnp.int32) == me).astype(jnp.float32)
    token_half = half_ep(tokens, experts)
    routed_rows = owner_rows(tokens, routes, gates, named, lanes)

    groups = [[subs // 2], [k for k in range(subs - 1, 0, -1) if k != subs // 2]]
    order = [k for group in groups for k in group]
    far = jnp.concatenate([exchange(routed_rows, "sub", k) for k in order], axis=0)
    own_half = half_ep(routed_rows, experts)
    token_all = jnp.concatenate([token_half, exchange(token_half, "ep", 1)], axis=0)
    expert_weights = flat_pairs(expert_up[0], routed_rows, 4)
    far, expert_weights = lax.optimization_barrier((far, expert_weights))
    middle = shared_middle(token_all, shared_up, far)

    far_half = half_ep(far, experts)
    half = after(jnp.concatenate([own_half, far_half], axis=0), middle)
    other = exchange(half, "ep", 1)
    rows = jnp.concatenate([half, other], axis=0)
    hidden = silu_product(jnp.dot(rows[:, :width], expert_weights, preferred_element_type=jnp.float32))
    gate = jnp.sum(named * rows[:, width:].astype(jnp.float32), axis=1)
    down_weights = expert_down.reshape(-1, width)

    hidden = hidden.reshape(CORES, half.shape[0], -1)
    gate = gate.reshape(CORES, half.shape[0])

    def routed(first, last):
        out = jnp.dot(hidden[:, first:last].reshape(CORES * (last - first), -1), down_weights, preferred_element_type=jnp.float32)
        return gate[:, first:last].reshape(-1, 1) * out

    split = own_half.shape[0]
    far_part = routed(split, half.shape[0]).astype(bf).reshape(experts, len(order), count, width)
    sums, at = [], 0
    for group in groups:
        part = far_part[:, at:at + len(group)].reshape(-1, width)
        sums.append(summed_ep(part, experts).astype(bf))
        at += len(group)

    middle = after(middle, far_part)
    own_part = jnp.dot(middle, shared_down, preferred_element_type=jnp.float32)
    own_part = (own_part + routed(0, split)).astype(bf)
    total = summed_ep(own_part, experts)
    for rows, group in zip(sums, groups):
        for at, k in enumerate(group):
            total = total + exchange(rows[at * count:(at + 1) * count], "sub", k).astype(jnp.float32)
    return total.astype(bf)


def solution(mesh):
    return jax.shard_map(
        per_device,
        mesh=mesh,
        in_specs=(
            P(("groups", "ep", "sub"), None),
            P(("groups", "ep", "sub"), None),
            P(("groups", "ep", "sub"), None),
            P("ep", None, None, "sub"),
            P("ep", "sub", None),
            P(None, None, "ep"),
            P("ep", None),
        ),
        out_specs=P(("groups", "ep", "sub"), None),
        check_vma=False,
    )
```

time: 70.2 us -> 64.2 us (0.915)
  local copies, waits for them, and re-layouts: 16.1 us -> 0.66 us
  Pallas kernels: 0 us -> 13.2 us
  other arithmetic: 5.2 us -> 1.37 us
  waiting for transfers between devices: 25.6 us -> 23.3 us
  starting transfers between devices: 14.5 us -> 16 us
  matrix products: 8.13 us -> 9.28 us
    unnamed x14 -> x5, local copies, waits for them, and re-layouts: 15.7 us -> 0.07 us
    pallas_call x0 -> x3, Pallas kernels: none -> 13.2 us  [the longest x1 6.6 us: shared_middle(): pl.pallas_call(shared_up_kernel, in_specs=[pl.BlockSpec(memory_space=pltp...]
    ppermute x14 -> x17, waiting for transfers between devices: 25.6 us -> 23.3 us  [exchange(): return lax.ppermute(rows, axis, [(i, i ^ flip) for i in range(size)])]
    ppermute x14 -> x17, starting transfers between devices: 14.5 us -> 16 us  [exchange(): return lax.ppermute(rows, axis, [(i, i ^ flip) for i in range(size)])]
    dot_general x6 -> x4, matrix products: 8.13 us -> 9.28 us  [the longest x1 4.63 us: per_device(): own_part = jnp.dot(middle, shared_down, preferred_element_type=jnp.float32)]
    reduce_max x1 -> x0, other arithmetic: 1.03 us -> none  [block_restored(): largest = jnp.max(jnp.abs(blocks), axis=2)]
    convert_element_type x3 -> x4, other arithmetic: 1.13 us -> 0.14 us  [the longest x2 0.09 us: per_device(): sums.append(summed_ep(part, experts).astype(bf))]
    concatenate x6 -> x4, other arithmetic: 1.11 us -> 0.14 us  [the longest x1 0.07 us: per_device(): half = after(jnp.concatenate([own_half, far_half], axis=0), middle)]
  transfers between devices with their start and end apart: 14 -> 17, of which waited for: 6 -> 8; matrix products, arithmetic and copies ran while one was open for 32% -> 9% of each run, Pallas kernels for 0% -> 21%
where the time goes in v2:
time: 64.2 us; the launch traced here: 64 us
  waiting for transfers between devices  23.3 us (36%)
  starting transfers between devices  16 us (25%)
  Pallas kernels  13.2 us (21%)
  matrix products  9.28 us (14%)
  other arithmetic  1.37 us (2%)
  local copies, waits for them, and re-layouts  0.66 us (1%)
    ppermute x17, waiting for transfers between devices, exchange(): return lax.ppermute(rows, axis, [(i, i ^ flip) for i in range(size)])  23.3 us
    ppermute x17, starting transfers between devices, exchange(): return lax.ppermute(rows, axis, [(i, i ^ flip) for i in range(size)])  16 us
    pallas_call x1, Pallas kernels, shared_middle(): pl.pallas_call(shared_up_kernel, in_specs=[pl.BlockSpec(memory_space=pltp...  6.6 us
    pallas_call x1, Pallas kernels, flat_pairs(): pl.pallas_call(split_kernel, grid=(steps,), in_specs=[pl.BlockSpec(memory...  5.45 us
    dot_general x1, matrix products, per_device(): own_part = jnp.dot(middle, shared_down, preferred_element_type=jnp.float32)  4.63 us
    dot_general x2, matrix products, routed(): jnp.dot(hidden[:, first:last].reshape(CORES * (last - first), -1), down_w...  3.51 us
  transfers between devices with their start and end apart: 17, of which 8 were waited for; matrix products, arithmetic and copies ran while one was open for 9% of the time, Pallas kernels for 21%

profile of v2, /device:TPU:0, one launch (start us, length us, event | category | flops | bytes accessed | tf_op | source)
XLA Modules:
  0.0 64.0 jit_solution(7928864155934158843)
XLA Ops:
  0.0 3.0 %collective-permute-start = (bf16[8,7168]{1,0:T(8,128)(2,1)}, bf16[8,7168]{1,0:T(8,128)(2,1)S(1)}, u32[]{:S(2)}, u32[]{:S(2)}) collective-permute-start(bf16[8,7168]{1,0:T(8,128)(2,1)} %tokens_ref.1), channel_id=1, source_target_pairs={{0,8},{4,12},{8,0},{12,4},{1,9},{5,13},{9,1},{13,5},{2,10},{6,14},... | collective-permute-start | bytes 344072 | tf_op jit(solution)/shard_map/ppermute | solution.py:160
  3.0 1.1 %shard_map.73.ready_ref = bf16[8,7296]{1,0:T(8,128)(2,1)S(1)} custom-call(bf16[8,7168]{1,0:T(8,128)(2,1)} %tokens_ref.1, s32[2,8]{1,0:T(2,128)} %bitcast.38, bf16[2,8]{1,0:T(2,128)(2,1)} %bitcast.40, f32[128]{0:T(128)S(1)} %compare_convert_fusion.ready_ref), custom_call_target="tpu_custom_call" | custom-call | tf_op jit(solution)/shard_map/pallas_call | solution.py:58
  4.2 2.1 %collective-permute-start.4 = (bf16[8,7296]{1,0:T(8,128)(2,1)S(1)}, bf16[8,7296]{1,0:T(8,128)(2,1)S(1)}, u32[]{:S(2)}, u32[]{:S(2)}) collective-permute-start(bf16[8,7296]{1,0:T(8,128)(2,1)S(1)} %shard_map.73.ready_ref), channel_id=1, source_target_pairs={{0,1},{1,0},{2,3},{3,2},{4,5},{5,4},{6,7},{7,6},{8,9},{9,8},{10,11... | collective-permute-start | bytes 350216 | tf_op jit(solution)/shard_map/ppermute | solution.py:160
  6.2 2.5 %collective-permute-start.3 = (bf16[8,7296]{1,0:T(8,128)(2,1)S(1)}, bf16[8,7296]{1,0:T(8,128)(2,1)S(1)}, u32[]{:S(2)}, u32[]{:S(2)}) collective-permute-start(bf16[8,7296]{1,0:T(8,128)(2,1)S(1)} %shard_map.73.ready_ref), channel_id=1, source_target_pairs={{0,3},{1,2},{2,1},{3,0},{4,7},{5,6},{6,5},{7,4},{8,11},{9,10},{10,... | collective-permute-start | bytes 350216 | tf_op jit(solution)/shard_map/ppermute | solution.py:160
  8.8 5.5 %shard_map.74 = bf16[7168,512]{1,0:T(8,128)(2,1)S(1)} custom-call(bf16[7168,2,256]{2,1,0:T(2,128)(2,1)} %bitcast.29, bf16[8,7296]{1,0:T(8,128)(2,1)S(1)} %shard_map.73.ready_ref), custom_call_target="tpu_custom_call" | custom-call | bytes 14680064 | tf_op jit(solution)/shard_map/pallas_call | solution.py:92
  14.4 0.4 collective-permute-done.3
  14.8 3.9 %collective-permute-done.2 = bf16[8,7296]{1,0:T(8,128)(2,1)S(1)} collective-permute-done((bf16[8,7296]{1,0:T(8,128)(2,1)S(1)}, bf16[8,7296]{1,0:T(8,128)(2,1)S(1)}, u32[]{:S(2)}, u32[]{:S(2)}) %collective-permute-start.2) | collective-permute-done | bytes 116768 | tf_op jit(solution)/shard_map/ppermute | solution.py:160
  18.7 1.6 %collective-permute-start.6 = (bf16[24,7296]{1,0:T(8,128)(2,1)S(1)}, bf16[24,7296]{1,0:T(8,128)(2,1)S(1)}, u32[]{:S(2)}, u32[]{:S(2)}) collective-permute-start(bf16[24,7296]{1,0:T(8,128)(2,1)S(1)} %pad_maximum_fusion.2.ready_ref), channel_id=1, source_target_pairs={{0,8},{4,12},{8,0},{12,4},{1,9},{5,13},{9,1},{13,5},{2,10},{6,14},... | collective-permute-start | bytes 1050632 | tf_op jit(solution)/shard_map/ppermute | solution.py:160
  20.3 6.6 %shard_map.75 = bf16[32,512]{1,0:T(8,128)(2,1)S(1)} custom-call(bf16[32,7168]{1,0:T(8,128)(2,1)S(1)} %pad_maximum_fusion.1.rows_ref, bf16[7168,2,512]{2,1,0:T(2,128)(2,1)} %up_ref.1, bf16[24,7296]{1,0:T(8,128)(2,1)S(1)} %pad_maximum_fusion.2.ready_ref), custom_call_target="tpu_custom_call" | custom-call | flops 469762048 | bytes 14680064 | tf_op jit(solution)/shard_map/pallas_call | solution.py:131
  27.0 1.0 %collective-permute-done.6 = bf16[24,7296]{1,0:T(8,128)(2,1)S(1)} collective-permute-done((bf16[24,7296]{1,0:T(8,128)(2,1)S(1)}, bf16[24,7296]{1,0:T(8,128)(2,1)S(1)}, u32[]{:S(2)}, u32[]{:S(2)}) %collective-permute-start.6) | collective-permute-done | bytes 350240 | tf_op jit(solution)/shard_map/ppermute | solution.py:160
  28.2 2.4 %collective-permute-done.7 = bf16[64,7296]{1,0:T(8,128)(2,1)S(1)} collective-permute-done((bf16[64,7296]{1,0:T(8,128)(2,1)S(1)}, bf16[64,7296]{1,0:T(8,128)(2,1)S(1)}, u32[]{:S(2)}, u32[]{:S(2)}) %collective-permute-start.7) | collective-permute-done | bytes 933920 | tf_op jit(solution)/shard_map/ppermute | solution.py:160
  30.8 1.1 %fusion.5 = f32[128,512]{1,0:T(8,128)S(1)} fusion(bf16[7168,512]{1,0:T(8,128)(2,1)S(1)} %shard_map.74, bf16[128,7296]{1,0:T(8,128)(2,1)S(1)} %constant_dynamic-update-slice_fusion), kind=kOutput, calls=%fused_computation.7 | convolution fusion | flops 939524096 | bytes 9437184 | tf_op jit(solution)/shard_map/dot_general | solution.py:205
  32.2 2.8 %fusion = bf16[96,7168]{1,0:T(8,128)(2,1)S(1)} fusion(bf16[96,256]{1,0:T(8,128)(2,1)S(1)} %bitcast.36, bf16[1,256,7168]{2,1,0:T(8,128)(2,1)} %param.11, f32[96]{0:T(128)S(1)} %mul.37), kind=kOutput, calls=%fused_computation.1 | convolution fusion | flops 353697792 | bytes 5095808 | tf_op jit(solution)/shard_map/dot_general | solution.py:213
  35.7 4.6 %fusion.12 = f32[32,7168]{1,0:T(8,128)S(1)} fusion(bf16[32,512]{1,0:T(8,128)(2,1)S(1)} %shard_map.75, bf16[512,7168]{1,0:T(8,128)(2,1)} %param.13), kind=kOutput, calls=%fused_computation.31 | convolution fusion | flops 234881024 | bytes 8290304 | tf_op jit(solution)/shard_map/dot_general | solution.py:225
  40.3 0.8 %fusion.2 = bf16[32,7168]{1,0:T(8,128)(2,1)S(1)} fusion(f32[32,7168]{1,0:T(8,128)S(1)} %fusion.12, bf16[32,256]{1,0:T(8,128)(2,1)S(1)} %bitcast.37, bf16[1,256,7168]{2,1,0:T(8,128)(2,1)S(1)} %copy-done, f32[32]{0:T(128)S(1)} %mul.42), kind=kOutput, calls=%fused_computation.4 | convolution fusion | flops 118128640 | bytes 5062784 | tf_op jit(solution)/shard_map/dot_general | solution.py:213
  41.3 1.6 %collective-permute-start.11 = (bf16[8,7168]{1,0:T(8,128)(2,1)S(1)}, bf16[8,7168]{1,0:T(8,128)(2,1)S(1)}, u32[]{:S(2)}, u32[]{:S(2)}) collective-permute-start(bf16[8,7168]{1,0:T(8,128)(2,1)S(1)} %slice.117), channel_id=1, source_target_pairs={{0,8},{4,12},{8,0},{12,4},{1,9},{5,13},{9,1},{13,5},{2,10},{6,14},... | collective-permute-start | bytes 344072 | tf_op jit(solution)/shard_map/ppermute | solution.py:160
  43.0 1.3 %collective-permute-start.9 = (bf16[8,7168]{1,0:T(8,128)(2,1)S(1)}, bf16[8,7168]{1,0:T(8,128)(2,1)S(1)}, u32[]{:S(2)}, u32[]{:S(2)}) collective-permute-start(bf16[8,7168]{1,0:T(8,128)(2,1)S(1)} %slice.113), channel_id=1, source_target_pairs={{0,8},{4,12},{8,0},{12,4},{1,9},{5,13},{9,1},{13,5},{2,10},{6,14},... | collective-permute-start | bytes 344072 | tf_op jit(solution)/shard_map/ppermute | solution.py:160
  44.5 0.9 %collective-permute-start.14 = (bf16[16,7168]{1,0:T(8,128)(2,1)S(1)}, bf16[16,7168]{1,0:T(8,128)(2,1)S(1)}, u32[]{:S(2)}, u32[]{:S(2)}) collective-permute-start(bf16[16,7168]{1,0:T(8,128)(2,1)S(1)} %slice.121), channel_id=1, source_target_pairs={{0,8},{4,12},{8,0},{12,4},{1,9},{5,13},{9,1},{13,5},{2,10},{6,14},... | collective-permute-start | bytes 688136 | tf_op jit(solution)/shard_map/ppermute | solution.py:160
  45.3 2.0 %collective-permute-done.11 = bf16[8,7168]{1,0:T(8,128)(2,1)S(1)} collective-permute-done((bf16[8,7168]{1,0:T(8,128)(2,1)S(1)}, bf16[8,7168]{1,0:T(8,128)(2,1)S(1)}, u32[]{:S(2)}, u32[]{:S(2)}) %collective-permute-start.11) | collective-permute-done | bytes 114720 | tf_op jit(solution)/shard_map/ppermute | solution.py:160
  47.5 6.8 %collective-permute-done.14 = bf16[16,7168]{1,0:T(8,128)(2,1)S(1)} collective-permute-done((bf16[16,7168]{1,0:T(8,128)(2,1)S(1)}, bf16[16,7168]{1,0:T(8,128)(2,1)S(1)}, u32[]{:S(2)}, u32[]{:S(2)}) %collective-permute-start.14) | collective-permute-done | bytes 229408 | tf_op jit(solution)/shard_map/ppermute | solution.py:160
  54.4 2.1 %collective-permute-start.15 = (bf16[8,7168]{1,0:T(8,128)(2,1)S(1)}, bf16[8,7168]{1,0:T(8,128)(2,1)S(1)}, u32[]{:S(2)}, u32[]{:S(2)}) collective-permute-start(bf16[8,7168]{1,0:T(8,128)(2,1)S(1)} %get-tuple-element.15), channel_id=1, source_target_pairs={{0,3},{1,2},{2,1},{3,0},{4,7},{5,6},{6,5},{7,4},{8,11},{9,10},{10,... | collective-permute-start | bytes 344072 | tf_op jit(solution)/shard_map/ppermute | solution.py:160
  56.4 5.7 %collective-permute-done.15 = bf16[8,7168]{1,0:T(8,128)(2,1)S(1)} collective-permute-done((bf16[8,7168]{1,0:T(8,128)(2,1)S(1)}, bf16[8,7168]{1,0:T(8,128)(2,1)S(1)}, u32[]{:S(2)}, u32[]{:S(2)}) %collective-permute-start.15) | collective-permute-done | bytes 114720 | tf_op jit(solution)/shard_map/ppermute | solution.py:160
  62.2 1.1 %collective-permute-done.16 = bf16[8,7168]{1,0:T(8,128)(2,1)S(1)} collective-permute-done((bf16[8,7168]{1,0:T(8,128)(2,1)S(1)}, bf16[8,7168]{1,0:T(8,128)(2,1)S(1)}, u32[]{:S(2)}, u32[]{:S(2)}) %collective-permute-start.16) | collective-permute-done | bytes 114720 | tf_op jit(solution)/shard_map/ppermute | solution.py:160
  63.3 0.7 %add_convert_fusion.2 = bf16[8,7168]{1,0:T(8,128)(2,1)} fusion(bf16[8,7168]{1,0:T(8,128)(2,1)S(1)} %collective-permute-done.16, bf16[8,7168]{1,0:T(8,128)(2,1)S(1)} %collective-permute-done.15, bf16[8,7168]{1,0:T(8,128)(2,1)S(1)} %collective-permute-done.12, bf16[8,7168]{1,0:T(8,128)(2,1)S(1)} %collective-permute-done.9, ...), kind=kLoop, calls=%fused_computation.21 | loop fusion | flops 573440 | bytes 688128 | tf_op jit(solution)/shard_map/convert_element_type | solution.py:231
  (49 shorter events, 2.4 us)
Async XLA Ops:
  0.0 14.3 %collective-permute-start = (bf16[8,7168]{1,0:T(8,128)(2,1)}, bf16[8,7168]{1,0:T(8,128)(2,1)S(1)}, u32[]{:S(2)}, u32[]{:S(2)}) collective-permute-start(bf16[8,7168]{1,0:T(8,128)(2,1)} %tokens_ref.1), channel_id=1, source_target_pairs={{0,8},{4,12},{8,0},{12,4},{1,9},{5,13},{9,1},{13,5},{2,10},{6,14},... | collective-permute-start | bytes 344072 | tf_op jit(solution)/shard_map/ppermute | solution.py:160
  4.1 22.9 %collective-permute-start.5 = (bf16[8,7296]{1,0:T(8,128)(2,1)S(1)}, bf16[8,7296]{1,0:T(8,128)(2,1)S(1)}, u32[]{:S(2)}, u32[]{:S(2)}) collective-permute-start(bf16[8,7296]{1,0:T(8,128)(2,1)S(1)} %shard_map.73.ready_ref), channel_id=1, source_target_pairs={{0,8},{4,12},{8,0},{12,4},{1,9},{5,13},{9,1},{13,5},{2,10},{6,14},... | collective-permute-start | bytes 350216 | tf_op jit(solution)/shard_map/ppermute | solution.py:160
  4.2 10.3 %collective-permute-start.4 = (bf16[8,7296]{1,0:T(8,128)(2,1)S(1)}, bf16[8,7296]{1,0:T(8,128)(2,1)S(1)}, u32[]{:S(2)}, u32[]{:S(2)}) collective-permute-start(bf16[8,7296]{1,0:T(8,128)(2,1)S(1)} %shard_map.73.ready_ref), channel_id=1, source_target_pairs={{0,1},{1,0},{2,3},{3,2},{4,5},{5,4},{6,7},{7,6},{8,9},{9,8},{10,11... | collective-permute-start | bytes 350216 | tf_op jit(solution)/shard_map/ppermute | solution.py:160
  6.2 8.6 %collective-permute-start.3 = (bf16[8,7296]{1,0:T(8,128)(2,1)S(1)}, bf16[8,7296]{1,0:T(8,128)(2,1)S(1)}, u32[]{:S(2)}, u32[]{:S(2)}) collective-permute-start(bf16[8,7296]{1,0:T(8,128)(2,1)S(1)} %shard_map.73.ready_ref), channel_id=1, source_target_pairs={{0,3},{1,2},{2,1},{3,0},{4,7},{5,6},{6,5},{7,4},{8,11},{9,10},{10,... | collective-permute-start | bytes 350216 | tf_op jit(solution)/shard_map/ppermute | solution.py:160
  8.7 10.0 %collective-permute-start.2 = (bf16[8,7296]{1,0:T(8,128)(2,1)S(1)}, bf16[8,7296]{1,0:T(8,128)(2,1)S(1)}, u32[]{:S(2)}, u32[]{:S(2)}) collective-permute-start(bf16[8,7296]{1,0:T(8,128)(2,1)S(1)} %shard_map.73.ready_ref), channel_id=1, source_target_pairs={{0,2},{1,3},{2,0},{3,1},{4,6},{5,7},{6,4},{7,5},{8,10},{9,11},{10,... | collective-permute-start | bytes 350216 | tf_op jit(solution)/shard_map/ppermute | solution.py:160
  8.8 5.5 %copy-start.1 = (bf16[8,7168]{1,0:T(8,128)(2,1)S(1)}, bf16[8,7168]{1,0:T(8,128)(2,1)}, u32[]{:S(2)}) copy-start(bf16[8,7168]{1,0:T(8,128)(2,1)} %tokens_ref.1) | copy-start | bytes 344068
  14.3 6.0 %collective-permute-start.1 = (bf16[16,7168]{1,0:T(8,128)(2,1)S(1)}, bf16[16,7168]{1,0:T(8,128)(2,1)S(1)}, u32[]{:S(2)}, u32[]{:S(2)}) collective-permute-start(bf16[16,7168]{1,0:T(8,128)(2,1)S(1)} %pad_maximum_fusion.3), channel_id=1, source_target_pairs={{0,4},{4,0},{8,12},{12,8},{1,5},{5,1},{9,13},{13,9},{2,6},{6,2},{1... | collective-permute-start | bytes 688136 | tf_op jit(solution)/shard_map/ppermute | solution.py:160
  18.7 9.2 %collective-permute-start.6 = (bf16[24,7296]{1,0:T(8,128)(2,1)S(1)}, bf16[24,7296]{1,0:T(8,128)(2,1)S(1)}, u32[]{:S(2)}, u32[]{:S(2)}) collective-permute-start(bf16[24,7296]{1,0:T(8,128)(2,1)S(1)} %pad_maximum_fusion.2.ready_ref), channel_id=1, source_target_pairs={{0,8},{4,12},{8,0},{12,4},{1,9},{5,13},{9,1},{13,5},{2,10},{6,14},... | collective-permute-start | bytes 1050632 | tf_op jit(solution)/shard_map/ppermute | solution.py:160
  28.0 2.6 %collective-permute-start.7 = (bf16[64,7296]{1,0:T(8,128)(2,1)S(1)}, bf16[64,7296]{1,0:T(8,128)(2,1)S(1)}, u32[]{:S(2)}, u32[]{:S(2)}) collective-permute-start(bf16[64,7296]{1,0:T(8,128)(2,1)S(1)} %pad_maximum_fusion), channel_id=1, source_target_pairs={{0,4},{4,0},{8,12},{12,8},{1,5},{5,1},{9,13},{13,9},{2,6},{6,2},{1... | collective-permute-start | bytes 2801672 | tf_op jit(solution)/shard_map/ppermute | solution.py:160
  35.2 6.1 %collective-permute-start.10 = (bf16[16,7168]{1,0:T(8,128)(2,1)S(1)}, bf16[16,7168]{1,0:T(8,128)(2,1)S(1)}, u32[]{:S(2)}, u32[]{:S(2)}) collective-permute-start(bf16[16,7168]{1,0:T(8,128)(2,1)S(1)} %slice_bitcast_fusion), channel_id=1, source_target_pairs={{0,4},{4,0},{8,12},{12,8},{1,5},{5,1},{9,13},{13,9},{2,6},{6,2},{1... | collective-permute-start | bytes 688136 | tf_op jit(solution)/shard_map/ppermute | solution.py:160
  35.3 5.0 %copy-start = (bf16[1,256,7168]{2,1,0:T(8,128)(2,1)S(1)}, bf16[1,256,7168]{2,1,0:T(8,128)(2,1)}, u32[]{:S(2)}) copy-start(bf16[1,256,7168]{2,1,0:T(8,128)(2,1)} %param.11) | copy-start | bytes 11010052
  35.3 9.0 %collective-permute-start.13 = (bf16[32,7168]{1,0:T(8,128)(2,1)S(1)}, bf16[32,7168]{1,0:T(8,128)(2,1)S(1)}, u32[]{:S(2)}, u32[]{:S(2)}) collective-permute-start(bf16[32,7168]{1,0:T(8,128)(2,1)S(1)} %bitcast.33), channel_id=1, source_target_pairs={{0,4},{4,0},{8,12},{12,8},{1,5},{5,1},{9,13},{13,9},{2,6},{6,2},{1... | collective-permute-start | bytes 1376264 | tf_op jit(solution)/shard_map/ppermute | solution.py:160
  41.1 1.8 %collective-permute-start.8 = (bf16[16,7168]{1,0:T(8,128)(2,1)S(1)}, bf16[16,7168]{1,0:T(8,128)(2,1)S(1)}, u32[]{:S(2)}, u32[]{:S(2)}) collective-permute-start(bf16[16,7168]{1,0:T(8,128)(2,1)S(1)} %slice.111), channel_id=1, source_target_pairs={{0,4},{4,0},{8,12},{12,8},{1,5},{5,1},{9,13},{13,9},{2,6},{6,2},{1... | collective-permute-start | bytes 688136 | tf_op jit(solution)/shard_map/ppermute | solution.py:160
  41.3 6.0 %collective-permute-start.11 = (bf16[8,7168]{1,0:T(8,128)(2,1)S(1)}, bf16[8,7168]{1,0:T(8,128)(2,1)S(1)}, u32[]{:S(2)}, u32[]{:S(2)}) collective-permute-start(bf16[8,7168]{1,0:T(8,128)(2,1)S(1)} %slice.117), channel_id=1, source_target_pairs={{0,8},{4,12},{8,0},{12,4},{1,9},{5,13},{9,1},{13,5},{2,10},{6,14},... | collective-permute-start | bytes 344072 | tf_op jit(solution)/shard_map/ppermute | solution.py:160
  43.0 13.4 %collective-permute-start.9 = (bf16[8,7168]{1,0:T(8,128)(2,1)S(1)}, bf16[8,7168]{1,0:T(8,128)(2,1)S(1)}, u32[]{:S(2)}, u32[]{:S(2)}) collective-permute-start(bf16[8,7168]{1,0:T(8,128)(2,1)S(1)} %slice.113), channel_id=1, source_target_pairs={{0,8},{4,12},{8,0},{12,4},{1,9},{5,13},{9,1},{13,5},{2,10},{6,14},... | collective-permute-start | bytes 344072 | tf_op jit(solution)/shard_map/ppermute | solution.py:160
  44.5 9.8 %collective-permute-start.14 = (bf16[16,7168]{1,0:T(8,128)(2,1)S(1)}, bf16[16,7168]{1,0:T(8,128)(2,1)S(1)}, u32[]{:S(2)}, u32[]{:S(2)}) collective-permute-start(bf16[16,7168]{1,0:T(8,128)(2,1)S(1)} %slice.121), channel_id=1, source_target_pairs={{0,8},{4,12},{8,0},{12,4},{1,9},{5,13},{9,1},{13,5},{2,10},{6,14},... | collective-permute-start | bytes 688136 | tf_op jit(solution)/shard_map/ppermute | solution.py:160
  47.4 9.0 %collective-permute-start.12 = (bf16[8,7168]{1,0:T(8,128)(2,1)S(1)}, bf16[8,7168]{1,0:T(8,128)(2,1)S(1)}, u32[]{:S(2)}, u32[]{:S(2)}) collective-permute-start(bf16[8,7168]{1,0:T(8,128)(2,1)S(1)} %add_convert_fusion.3), channel_id=1, source_target_pairs={{0,2},{1,3},{2,0},{3,1},{4,6},{5,7},{6,4},{7,5},{8,10},{9,11},{10,... | collective-permute-start | bytes 344072 | tf_op jit(solution)/shard_map/ppermute | solution.py:160
  54.4 7.8 %collective-permute-start.15 = (bf16[8,7168]{1,0:T(8,128)(2,1)S(1)}, bf16[8,7168]{1,0:T(8,128)(2,1)S(1)}, u32[]{:S(2)}, u32[]{:S(2)}) collective-permute-start(bf16[8,7168]{1,0:T(8,128)(2,1)S(1)} %get-tuple-element.15), channel_id=1, source_target_pairs={{0,3},{1,2},{2,1},{3,0},{4,7},{5,6},{6,5},{7,4},{8,11},{9,10},{10,... | collective-permute-start | bytes 344072 | tf_op jit(solution)/shard_map/ppermute | solution.py:160
  56.4 6.9 %collective-permute-start.16 = (bf16[8,7168]{1,0:T(8,128)(2,1)S(1)}, bf16[8,7168]{1,0:T(8,128)(2,1)S(1)}, u32[]{:S(2)}, u32[]{:S(2)}) collective-permute-start(bf16[8,7168]{1,0:T(8,128)(2,1)S(1)} %get-tuple-element.16), channel_id=1, source_target_pairs={{0,1},{1,0},{2,3},{3,2},{4,5},{5,4},{6,7},{7,6},{8,9},{9,8},{10,11... | collective-permute-start | bytes 344072 | tf_op jit(solution)/shard_map/ppermute | solution.py:160

commit v3 on v2

--- a/solution.py
+++ b/solution.py
@@ -1,3 +1,5 @@
+import functools
+
 import jax
 import jax.numpy as jnp
 from jax import lax
@@ -8,11 +10,7 @@
 QBLOCK = 128
 LANES = 128
 CORES = 2
-
-
-def silu_product(projected):
-    half_width = projected.shape[1] // 2
-    return (jax.nn.silu(projected[:, :half_width]) * projected[:, half_width:]).astype(jnp.bfloat16)
+VMEM_LIMIT = 30 << 20
 
 
 def owner_kernel(tokens_ref, routes_ref, gates_ref, ready_ref, routed_ref, tokens, routes, gates, sems):
@@ -66,41 +64,52 @@
     )(*(pltpu.with_memory_space_constraint(x, pltpu.HBM) for x in operands), ready)
 
 
-def split_kernel(pair_ref, ready_ref, flat_ref, raw, sems):
+def weights_kernel(pair_ref, down_ref, shared_ref, ready_ref, flat_ref, down_out, shared_out, raw, sems):
     del ready_ref
-    step, steps = pl.program_id(0), pl.num_programs(0)
-    block, hidden = flat_ref.shape[0], pair_ref.shape[2]
+    steps = sems.shape[0] - 2
+    block, hidden = raw.shape[0] // steps, pair_ref.shape[2]
 
     def fetch(i):
         rows = pl.ds(i * block, block)
         return pltpu.make_async_copy(pair_ref.at[rows], raw.at[rows], sems.at[i])
 
-    @pl.when(step == 0)
-    def _():
-        for i in range(sems.shape[0]):
-            fetch(i).start()
-
-    fetch(step).wait()
-    both = jnp.swapaxes(raw[pl.ds(step * block, block)], 0, 1)
-    flat_ref[:, :hidden] = both[0]
-    flat_ref[:, hidden:] = both[1]
-
-
-def flat_pairs(pairs, ready, steps):
+    downs = [
+        pltpu.make_async_copy(down_ref, down_out, sems.at[steps]),
+        pltpu.make_async_copy(shared_ref, shared_out, sems.at[steps + 1]),
+    ]
+    for i in range(steps):
+        fetch(i).start()
+    for copy in downs:
+        copy.start()
+    for i in range(steps):
+        fetch(i).wait()
+        at = slice(i * block, (i + 1) * block)
+        both = jnp.swapaxes(raw[at], 0, 1)
+        flat_ref[at, :hidden] = both[0]
+        flat_ref[at, hidden:] = both[1]
+    for copy in downs:
+        copy.wait()
+
+
+def held_weights(pairs, down, shared, ready):
     depth, _, hidden = pairs.shape
-    block = depth // steps
-    return pl.pallas_call(
-        split_kernel,
-        grid=(steps,),
-        in_specs=[pl.BlockSpec(memory_space=pltpu.HBM), pl.BlockSpec(memory_space=pl.ANY)],
-        out_specs=pl.BlockSpec((block, 2 * hidden), lambda i: (i, 0)),
-        out_shape=jax.ShapeDtypeStruct((depth, 2 * hidden), pairs.dtype),
-        scratch_shapes=[pltpu.VMEM(pairs.shape, pairs.dtype), pltpu.SemaphoreType.DMA((steps,))],
-        compiler_params=pltpu.CompilerParams(vmem_limit_bytes=16 << 20),
+    steps = 4
+    operands = [pltpu.with_memory_space_constraint(x, pltpu.HBM) for x in (pairs, down, shared)]
+    return pl.pallas_call(
+        weights_kernel,
+        in_specs=[pl.BlockSpec(memory_space=pltpu.HBM)] * 3 + [pl.BlockSpec(memory_space=pl.ANY)],
+        out_specs=[pl.BlockSpec(memory_space=pltpu.VMEM)] * 3,
+        out_shape=(
+            jax.ShapeDtypeStruct((depth, 2 * hidden), pairs.dtype),
+            jax.ShapeDtypeStruct(down.shape, down.dtype),
+            jax.ShapeDtypeStruct(shared.shape, shared.dtype),
+        ),
+        scratch_shapes=[pltpu.VMEM(pairs.shape, pairs.dtype), pltpu.SemaphoreType.DMA((steps + 2,))],
+        compiler_params=pltpu.CompilerParams(vmem_limit_bytes=VMEM_LIMIT),
         cost_estimate=pl.CostEstimate(
             flops=0, bytes_accessed=8 * depth * hidden, transcendentals=0
         ),
-    )(pltpu.with_memory_space_constraint(pairs, pltpu.HBM), ready)
+    )(*operands, ready)
 
 
 def shared_up_kernel(rows_ref, up_ref, ready_ref, middle_ref, up, sums, sems):
@@ -151,6 +160,44 @@
     )(rows, pltpu.with_memory_space_constraint(up, pltpu.HBM), ready)
 
 
+def routed_up_kernel(layout, half_ref, other_ref, flat_ref, named_ref, *rest):
+    outs, sums = rest[:-1], rest[-1]
+    depth, hidden = flat_ref.shape[0], flat_ref.shape[1] // 2
+    steps = 7
+    block = depth // steps
+    for i in range(steps):
+        at = slice(i * block, (i + 1) * block)
+        left = jnp.concatenate([half_ref[:, at], other_ref[:, at]], axis=0)
+        term = jnp.dot(left, flat_ref[at, :], preferred_element_type=jnp.float32)
+        sums[...] = term if i == 0 else sums[...] + term
+    weight = jnp.concatenate([half_ref[:, depth:], other_ref[:, depth:]], axis=0)
+    named = weight.astype(jnp.float32) * named_ref[...]
+    weight = jnp.sum(named, axis=1, keepdims=True)
+    gate, lift = sums[:, :hidden], sums[:, hidden:]
+    sums[:, :hidden] = gate / (1.0 + jnp.exp(-gate)) * lift * weight
+    for out, pieces in zip(outs, layout):
+        rows = [sums[first:first + count, :hidden] for first, count in pieces]
+        out[...] = jnp.concatenate(rows, axis=0).astype(jnp.bfloat16)
+
+
+def routed_hidden(half, other, flat, named, layout):
+    count, hidden = 2 * half.shape[0], flat.shape[1] // 2
+    return pl.pallas_call(
+        functools.partial(routed_up_kernel, layout),
+        in_specs=[pl.BlockSpec(memory_space=pltpu.VMEM)] * 4,
+        out_specs=[pl.BlockSpec(memory_space=pltpu.VMEM)] * len(layout),
+        out_shape=[
+            jax.ShapeDtypeStruct((sum(rows for _, rows in pieces), hidden), jnp.bfloat16)
+            for pieces in layout
+        ],
+        scratch_shapes=[pltpu.VMEM((count, 2 * hidden), jnp.float32)],
+        compiler_params=pltpu.CompilerParams(vmem_limit_bytes=VMEM_LIMIT),
+        cost_estimate=pl.CostEstimate(
+            flops=2 * count * flat.size, bytes_accessed=2 * flat.size, transcendentals=0
+        ),
+    )(half, other, flat, named)
+
+
 def after(value, ready):
     return lax.optimization_barrier((value, ready))[0]
 
@@ -165,11 +212,14 @@
     return jnp.concatenate([rows] + parts, axis=0)
 
 
-def summed_ep(partial, experts):
+def pair_sum(partial):
     half = partial.shape[0] // CORES
     other = exchange(partial[half:], "ep", 1)
-    pair = (partial[:half].astype(jnp.float32) + other.astype(jnp.float32)).astype(jnp.bfloat16)
-    count = half * CORES // experts
+    return (partial[:half].astype(jnp.float32) + other.astype(jnp.float32)).astype(jnp.bfloat16)
+
+
+def chip_sum(pair, experts):
+    count = pair.shape[0] * CORES // experts
     total = pair[:count].astype(jnp.float32)
     for chip in range(CORES, experts, CORES):
         at = chip // CORES * count
@@ -185,46 +235,45 @@
     bf = jnp.bfloat16
 
     lanes = -(-experts // LANES) * LANES
-    named = (jnp.arange(lanes, dtype=jnp.int32) == me).astype(jnp.float32)
-    token_half = half_ep(tokens, experts)
+    named = (lax.broadcasted_iota(jnp.int32, (1, lanes), 1) == me).astype(jnp.float32)
     routed_rows = owner_rows(tokens, routes, gates, named, lanes)
+    token_half = half_ep(after(tokens, routed_rows), experts)
 
     groups = [[subs // 2], [k for k in range(subs - 1, 0, -1) if k != subs // 2]]
     order = [k for group in groups for k in group]
     far = jnp.concatenate([exchange(routed_rows, "sub", k) for k in order], axis=0)
     own_half = half_ep(routed_rows, experts)
     token_all = jnp.concatenate([token_half, exchange(token_half, "ep", 1)], axis=0)
-    expert_weights = flat_pairs(expert_up[0], routed_rows, 4)
+    expert_weights, down_weights, shared_weights = held_weights(
+        expert_up[0], expert_down[0], shared_down, routed_rows
+    )
     far, expert_weights = lax.optimization_barrier((far, expert_weights))
     middle = shared_middle(token_all, shared_up, far)
 
     far_half = half_ep(far, experts)
     half = after(jnp.concatenate([own_half, far_half], axis=0), middle)
     other = exchange(half, "ep", 1)
-    rows = jnp.concatenate([half, other], axis=0)
-    hidden = silu_product(jnp.dot(rows[:, :width], expert_weights, preferred_element_type=jnp.float32))
-    gate = jnp.sum(named * rows[:, width:].astype(jnp.float32), axis=1)
-    down_weights = expert_down.reshape(-1, width)
-
-    hidden = hidden.reshape(CORES, half.shape[0], -1)
-    gate = gate.reshape(CORES, half.shape[0])
-
-    def routed(first, last):
-        out = jnp.dot(hidden[:, first:last].reshape(CORES * (last - first), -1), down_weights, preferred_element_type=jnp.float32)
-        return gate[:, first:last].reshape(-1, 1) * out
-
-    split = own_half.shape[0]
-    far_part = routed(split, half.shape[0]).astype(bf).reshape(experts, len(order), count, width)
-    sums, at = [], 0
+
+    chips, split = experts // CORES, own_half.shape[0]
+    layout = [[(core * half.shape[0], split) for core in range(CORES)]]
+    at = 0
     for group in groups:
-        part = far_part[:, at:at + len(group)].reshape(-1, width)
-        sums.append(summed_ep(part, experts).astype(bf))
-        at += len(group)
-
-    middle = after(middle, far_part)
-    own_part = jnp.dot(middle, shared_down, preferred_element_type=jnp.float32)
-    own_part = (own_part + routed(0, split)).astype(bf)
-    total = summed_ep(own_part, experts)
+        size = len(group) * count
+        layout.append([
+            (core * half.shape[0] + split + chip * len(order) * count + at, size)
+            for core in range(CORES) for chip in range(chips)
+        ])
+        at += size
+    own_hidden, *far_hidden = routed_hidden(half, other, expert_weights, named, layout)
+
+    def down(hidden, weights):
+        return jnp.dot(hidden, weights, preferred_element_type=jnp.float32)
+
+    pairs = [pair_sum(down(hidden, down_weights).astype(bf)) for hidden in far_hidden]
+    middle, own_hidden = after((middle, own_hidden), pairs[-1])
+    own_part = (down(middle, shared_weights) + down(own_hidden, down_weights)).astype(bf)
+    sums = [chip_sum(pair, experts).astype(bf) for pair in pairs]
+    total = chip_sum(pair_sum(own_part), experts)
     for rows, group in zip(sums, groups):
         for at, k in enumerate(group):
             total = total + exchange(rows[at * count:(at + 1) * count], "sub", k).astype(jnp.float32)

time: 64.2 us -> 55.6 us (0.87)
  waiting for transfers between devices: 23.3 us -> 16.8 us
  matrix products: 9.28 us -> 3.62 us
  starting transfers between devices: 16 us -> 18.3 us
  Pallas kernels: 13.2 us -> 15.2 us
    ppermute x17, waiting for transfers between devices: 23.3 us -> 16.8 us  [exchange(): return lax.ppermute(rows, axis, [(i, i ^ flip) for i in range(size)])]
    dot_general x4, matrix products: 9.28 us -> 3.62 us  [down(): return jnp.dot(hidden, weights, preferred_element_type=jnp.float32)]
    ppermute x17, starting transfers between devices: 16 us -> 18.3 us  [exchange(): return lax.ppermute(rows, axis, [(i, i ^ flip) for i in range(size)])]
    pallas_call x1 -> x2, Pallas kernels: 5.45 us -> 7.52 us  [the longest x1 6.38 us: held_weights(): pl.pallas_call(weights_kernel, in_specs=[pl.BlockSpec(memory_space=pltpu....]
  transfers between devices with their start and end apart: 17 -> 17, of which waited for: 8 -> 9; matrix products, arithmetic and copies ran while one was open for 9% -> 6% of each run, Pallas kernels for 21% -> 23%
where the time goes in v3:
time: 55.6 us; the launch traced here: 55.5 us
  starting transfers between devices  18.3 us (33%)
  waiting for transfers between devices  16.8 us (30%)
  Pallas kernels  15.2 us (27%)
  matrix products  3.62 us (7%)
  other arithmetic  1.22 us (2%)
    ppermute x17, starting transfers between devices, exchange(): return lax.ppermute(rows, axis, [(i, i ^ flip) for i in range(size)])  18.3 us
    ppermute x17, waiting for transfers between devices, exchange(): return lax.ppermute(rows, axis, [(i, i ^ flip) for i in range(size)])  16.8 us
    pallas_call x1, Pallas kernels, shared_middle(): pl.pallas_call(shared_up_kernel, in_specs=[pl.BlockSpec(memory_space=pltp...  6.62 us
    pallas_call x1, Pallas kernels, held_weights(): pl.pallas_call(weights_kernel, in_specs=[pl.BlockSpec(memory_space=pltpu....  6.38 us
    dot_general x4, matrix products, down(): return jnp.dot(hidden, weights, preferred_element_type=jnp.float32)  3.62 us
    pallas_call x1, Pallas kernels, routed_hidden(): pl.pallas_call(functools.partial(routed_up_kernel, layout), in_specs=[pl....  1.14 us
  transfers between devices with their start and end apart: 17, of which 9 were waited for; matrix products, arithmetic and copies ran while one was open for 6% of the time, Pallas kernels for 23%

profile of v3, /device:TPU:0, one launch (start us, length us, event | category | flops | bytes accessed | tf_op | source)
XLA Modules:
  0.0 55.5 jit_solution(4363912098442313099)
XLA Ops:
  0.0 1.1 %shard_map.73.ready_ref = bf16[8,7296]{1,0:T(8,128)(2,1)S(1)} custom-call(bf16[8,7168]{1,0:T(8,128)(2,1)} %tokens_ref.1, s32[2,8]{1,0:T(2,128)} %bitcast.14, bf16[2,8]{1,0:T(2,128)(2,1)} %bitcast.15, f32[1,128]{1,0:T(1,128)S(1)} %compare_convert_fusion.ready_ref.named_ref), custom_call_target="tpu_custom_call" | custom-call | tf_op jit(solution)/shard_map/pallas_call | solution.py:56
  1.1 3.0 %collective-permute-start = (bf16[8,7168]{1,0:T(8,128)(2,1)}, bf16[8,7168]{1,0:T(8,128)(2,1)S(1)}, u32[]{:S(2)}, u32[]{:S(2)}) collective-permute-start(bf16[8,7168]{1,0:T(8,128)(2,1)} %tokens_ref.1), channel_id=1, source_target_pairs={{0,8},{4,12},{8,0},{12,4},{1,9},{5,13},{9,1},{13,5},{2,10},{6,14},... | collective-permute-start | bytes 344072 | tf_op jit(solution)/shard_map/ppermute | solution.py:207
  4.2 2.0 %collective-permute-start.4 = (bf16[8,7296]{1,0:T(8,128)(2,1)S(1)}, bf16[8,7296]{1,0:T(8,128)(2,1)S(1)}, u32[]{:S(2)}, u32[]{:S(2)}) collective-permute-start(bf16[8,7296]{1,0:T(8,128)(2,1)S(1)} %shard_map.73.ready_ref), channel_id=1, source_target_pairs={{0,1},{1,0},{2,3},{3,2},{4,5},{5,4},{6,7},{7,6},{8,9},{9,8},{10,11... | collective-permute-start | bytes 350216 | tf_op jit(solution)/shard_map/ppermute | solution.py:207
  6.2 2.5 %collective-permute-start.3 = (bf16[8,7296]{1,0:T(8,128)(2,1)S(1)}, bf16[8,7296]{1,0:T(8,128)(2,1)S(1)}, u32[]{:S(2)}, u32[]{:S(2)}) collective-permute-start(bf16[8,7296]{1,0:T(8,128)(2,1)S(1)} %shard_map.73.ready_ref), channel_id=1, source_target_pairs={{0,3},{1,2},{2,1},{3,0},{4,7},{5,6},{6,5},{7,4},{8,11},{9,10},{10,... | collective-permute-start | bytes 350216 | tf_op jit(solution)/shard_map/ppermute | solution.py:207
  8.8 6.4 %shard_map.74 = (bf16[7168,512]{1,0:T(8,128)(2,1)S(1)}, bf16[256,7168]{1,0:T(8,128)(2,1)S(1)}, bf16[512,7168]{1,0:T(8,128)(2,1)S(1)}) custom-call(bf16[7168,2,256]{2,1,0:T(2,128)(2,1)} %bitcast.12, bf16[256,7168]{1,0:T(8,128)(2,1)} %bitcast.13, bf16[512,7168]{1,0:T(8,128)(2,1)} %shared_ref.1, bf16[8,7296]{1,0:T(8,128)(2,1)S(1)} %shard_map.73.ready_ref), custom_call_target="tpu_custom_call" | custom-call | bytes 14680064 | tf_op jit(solution)/shard_map/pallas_call | solution.py:98
  15.4 3.3 %collective-permute-done.2 = bf16[8,7296]{1,0:T(8,128)(2,1)S(1)} collective-permute-done((bf16[8,7296]{1,0:T(8,128)(2,1)S(1)}, bf16[8,7296]{1,0:T(8,128)(2,1)S(1)}, u32[]{:S(2)}, u32[]{:S(2)}) %collective-permute-start.2) | collective-permute-done | bytes 116768 | tf_op jit(solution)/shard_map/ppermute | solution.py:207
  18.7 1.6 %collective-permute-start.6 = (bf16[24,7296]{1,0:T(8,128)(2,1)S(1)}, bf16[24,7296]{1,0:T(8,128)(2,1)S(1)}, u32[]{:S(2)}, u32[]{:S(2)}) collective-permute-start(bf16[24,7296]{1,0:T(8,128)(2,1)S(1)} %pad_maximum_fusion.2.ready_ref), channel_id=1, source_target_pairs={{0,8},{4,12},{8,0},{12,4},{1,9},{5,13},{9,1},{13,5},{2,10},{6,14},... | collective-permute-start | bytes 1050632 | tf_op jit(solution)/shard_map/ppermute | solution.py:207
  20.3 6.6 %shard_map.75 = bf16[32,512]{1,0:T(8,128)(2,1)S(1)} custom-call(bf16[32,7168]{1,0:T(8,128)(2,1)S(1)} %pad_maximum_fusion.1.rows_ref, bf16[7168,2,512]{2,1,0:T(2,128)(2,1)} %up_ref.1, bf16[24,7296]{1,0:T(8,128)(2,1)S(1)} %pad_maximum_fusion.2.ready_ref), custom_call_target="tpu_custom_call" | custom-call | flops 469762048 | bytes 14680064 | tf_op jit(solution)/shard_map/pallas_call | solution.py:140
  27.0 0.9 %collective-permute-done.6 = bf16[24,7296]{1,0:T(8,128)(2,1)S(1)} collective-permute-done((bf16[24,7296]{1,0:T(8,128)(2,1)S(1)}, bf16[24,7296]{1,0:T(8,128)(2,1)S(1)}, u32[]{:S(2)}, u32[]{:S(2)}) %collective-permute-start.6) | collective-permute-done | bytes 350240 | tf_op jit(solution)/shard_map/ppermute | solution.py:207
  28.1 2.5 %collective-permute-done.7.other_ref = bf16[64,7296]{1,0:T(8,128)(2,1)S(1)} collective-permute-done((bf16[64,7296]{1,0:T(8,128)(2,1)S(1)}, bf16[64,7296]{1,0:T(8,128)(2,1)S(1)}, u32[]{:S(2)}, u32[]{:S(2)}) %collective-permute-start.7) | collective-permute-done | bytes 933920 | tf_op jit(solution)/shard_map/ppermute | solution.py:207
  30.5 1.1 %shard_map.76 = (bf16[32,256]{1,0:T(8,128)(2,1)S(1)}, bf16[32,256]{1,0:T(8,128)(2,1)S(1)}, bf16[64,256]{1,0:T(8,128)(2,1)S(1)}) custom-call(bf16[64,7296]{1,0:T(8,128)(2,1)S(1)} %pad_maximum_fusion.half_ref, bf16[64,7296]{1,0:T(8,128)(2,1)S(1)} %collective-permute-done.7.other_ref, bf16[7168,512]{1,0:T(8,128)(2,1)S(1)} %get-tuple-element.21.flat_ref, ...), custom_call_target="tpu_custom_call" | custom-call | flops 939524096 | bytes 7340032 | tf_op jit(solution)/shard_map/pallas_call | solution.py:185
  32.7 1.4 %collective-permute-done.11 = bf16[16,7168]{1,0:T(8,128)(2,1)S(1)} collective-permute-done((bf16[16,7168]{1,0:T(8,128)(2,1)S(1)}, bf16[16,7168]{1,0:T(8,128)(2,1)S(1)}, u32[]{:S(2)}, u32[]{:S(2)}) %collective-permute-start.11) | collective-permute-done | bytes 229408 | tf_op jit(solution)/shard_map/ppermute | solution.py:207
  34.1 1.6 %collective-permute-start.12 = (bf16[8,7168]{1,0:T(8,128)(2,1)S(1)}, bf16[8,7168]{1,0:T(8,128)(2,1)S(1)}, u32[]{:S(2)}, u32[]{:S(2)}) collective-permute-start(bf16[8,7168]{1,0:T(8,128)(2,1)S(1)} %slice.65), channel_id=1, source_target_pairs={{0,8},{4,12},{8,0},{12,4},{1,9},{5,13},{9,1},{13,5},{2,10},{6,14},... | collective-permute-start | bytes 344072 | tf_op jit(solution)/shard_map/ppermute | solution.py:207
  35.7 0.8 %convolution_convert_fusion = bf16[64,7168]{1,0:T(8,128)(2,1)S(1)} fusion(bf16[64,256]{1,0:T(8,128)(2,1)S(1)} %get-tuple-element.23, bf16[256,7168]{1,0:T(8,128)(2,1)S(1)} %get-tuple-element.24), kind=kOutput, calls=%fused_computation | convolution fusion | flops 235339776 | bytes 4620288 | tf_op jit(solution)/shard_map/dot_general | solution.py:270
  36.7 2.6 %collective-permute-done.12 = bf16[8,7168]{1,0:T(8,128)(2,1)S(1)} collective-permute-done((bf16[8,7168]{1,0:T(8,128)(2,1)S(1)}, bf16[8,7168]{1,0:T(8,128)(2,1)S(1)}, u32[]{:S(2)}, u32[]{:S(2)}) %collective-permute-start.12) | collective-permute-done | bytes 114720 | tf_op jit(solution)/shard_map/ppermute | solution.py:207
  39.4 1.0 %collective-permute-start.13 = (bf16[8,7168]{1,0:T(8,128)(2,1)S(1)}, bf16[8,7168]{1,0:T(8,128)(2,1)S(1)}, u32[]{:S(2)}, u32[]{:S(2)}) collective-permute-start(bf16[8,7168]{1,0:T(8,128)(2,1)S(1)} %add_convert_fusion.5), channel_id=1, source_target_pairs={{0,2},{1,3},{2,0},{3,1},{4,6},{5,7},{6,4},{7,5},{8,10},{9,11},{10,... | collective-permute-start | bytes 344072 | tf_op jit(solution)/shard_map/ppermute | solution.py:207
  40.5 1.6 %collective-permute-start.14 = (bf16[16,7168]{1,0:T(8,128)(2,1)S(1)}, bf16[16,7168]{1,0:T(8,128)(2,1)S(1)}, u32[]{:S(2)}, u32[]{:S(2)}) collective-permute-start(bf16[16,7168]{1,0:T(8,128)(2,1)S(1)} %slice.67), channel_id=1, source_target_pairs={{0,8},{4,12},{8,0},{12,4},{1,9},{5,13},{9,1},{13,5},{2,10},{6,14},... | collective-permute-start | bytes 688136 | tf_op jit(solution)/shard_map/ppermute | solution.py:207
  42.1 1.4 %fusion.2 = f32[32,7168]{1,0:T(8,128)S(1)} fusion(bf16[32,512]{1,0:T(8,128)(2,1)S(1)} %shard_map.75, bf16[512,7168]{1,0:T(8,128)(2,1)S(1)} %get-tuple-element.26), kind=kOutput, calls=%fused_computation.16 | convolution fusion | flops 234881024 | bytes 8290304 | tf_op jit(solution)/shard_map/dot_general | solution.py:270
  43.5 0.8 %fusion = bf16[32,7168]{1,0:T(8,128)(2,1)S(1)} fusion(f32[32,7168]{1,0:T(8,128)S(1)} %fusion.2, bf16[32,256]{1,0:T(8,128)(2,1)S(1)} %get-tuple-element.27, bf16[256,7168]{1,0:T(8,128)(2,1)S(1)} %get-tuple-element.24), kind=kOutput, calls=%fused_computation.2 | convolution fusion | flops 117899264 | bytes 5062656 | tf_op jit(solution)/shard_map/dot_general | solution.py:270
  44.4 2.8 %collective-permute-done.14 = bf16[16,7168]{1,0:T(8,128)(2,1)S(1)} collective-permute-done((bf16[16,7168]{1,0:T(8,128)(2,1)S(1)}, bf16[16,7168]{1,0:T(8,128)(2,1)S(1)}, u32[]{:S(2)}, u32[]{:S(2)}) %collective-permute-start.14) | collective-permute-done | bytes 229408 | tf_op jit(solution)/shard_map/ppermute | solution.py:207
  47.2 1.4 %collective-permute-start.15 = (bf16[8,7168]{1,0:T(8,128)(2,1)S(1)}, bf16[8,7168]{1,0:T(8,128)(2,1)S(1)}, u32[]{:S(2)}, u32[]{:S(2)}) collective-permute-start(bf16[8,7168]{1,0:T(8,128)(2,1)S(1)} %get-tuple-element.29), channel_id=1, source_target_pairs={{0,3},{1,2},{2,1},{3,0},{4,7},{5,6},{6,5},{7,4},{8,11},{9,10},{10,... | collective-permute-start | bytes 344072 | tf_op jit(solution)/shard_map/ppermute | solution.py:207
  48.7 1.2 %collective-permute-start.16 = (bf16[8,7168]{1,0:T(8,128)(2,1)S(1)}, bf16[8,7168]{1,0:T(8,128)(2,1)S(1)}, u32[]{:S(2)}, u32[]{:S(2)}) collective-permute-start(bf16[8,7168]{1,0:T(8,128)(2,1)S(1)} %get-tuple-element.30), channel_id=1, source_target_pairs={{0,1},{1,0},{2,3},{3,2},{4,5},{5,4},{6,7},{7,6},{8,9},{9,8},{10,11... | collective-permute-start | bytes 344072 | tf_op jit(solution)/shard_map/ppermute | solution.py:207
  49.9 1.6 %collective-permute-start.10 = (bf16[8,7168]{1,0:T(8,128)(2,1)S(1)}, bf16[8,7168]{1,0:T(8,128)(2,1)S(1)}, u32[]{:S(2)}, u32[]{:S(2)}) collective-permute-start(bf16[8,7168]{1,0:T(8,128)(2,1)S(1)} %slice.61), channel_id=1, source_target_pairs={{0,8},{4,12},{8,0},{12,4},{1,9},{5,13},{9,1},{13,5},{2,10},{6,14},... | collective-permute-start | bytes 344072 | tf_op jit(solution)/shard_map/ppermute | solution.py:207
  51.5 2.5 %collective-permute-done.15 = bf16[8,7168]{1,0:T(8,128)(2,1)S(1)} collective-permute-done((bf16[8,7168]{1,0:T(8,128)(2,1)S(1)}, bf16[8,7168]{1,0:T(8,128)(2,1)S(1)}, u32[]{:S(2)}, u32[]{:S(2)}) %collective-permute-start.15) | collective-permute-done | bytes 114720 | tf_op jit(solution)/shard_map/ppermute | solution.py:207
  (38 shorter events, 3.7 us)
Async XLA Ops:
  1.1 14.1 %collective-permute-start = (bf16[8,7168]{1,0:T(8,128)(2,1)}, bf16[8,7168]{1,0:T(8,128)(2,1)S(1)}, u32[]{:S(2)}, u32[]{:S(2)}) collective-permute-start(bf16[8,7168]{1,0:T(8,128)(2,1)} %tokens_ref.1), channel_id=1, source_target_pairs={{0,8},{4,12},{8,0},{12,4},{1,9},{5,13},{9,1},{13,5},{2,10},{6,14},... | collective-permute-start | bytes 344072 | tf_op jit(solution)/shard_map/ppermute | solution.py:207
  4.1 22.8 %collective-permute-start.5 = (bf16[8,7296]{1,0:T(8,128)(2,1)S(1)}, bf16[8,7296]{1,0:T(8,128)(2,1)S(1)}, u32[]{:S(2)}, u32[]{:S(2)}) collective-permute-start(bf16[8,7296]{1,0:T(8,128)(2,1)S(1)} %shard_map.73.ready_ref), channel_id=1, source_target_pairs={{0,8},{4,12},{8,0},{12,4},{1,9},{5,13},{9,1},{13,5},{2,10},{6,14},... | collective-permute-start | bytes 350216 | tf_op jit(solution)/shard_map/ppermute | solution.py:207
  4.2 11.1 %collective-permute-start.4 = (bf16[8,7296]{1,0:T(8,128)(2,1)S(1)}, bf16[8,7296]{1,0:T(8,128)(2,1)S(1)}, u32[]{:S(2)}, u32[]{:S(2)}) collective-permute-start(bf16[8,7296]{1,0:T(8,128)(2,1)S(1)} %shard_map.73.ready_ref), channel_id=1, source_target_pairs={{0,1},{1,0},{2,3},{3,2},{4,5},{5,4},{6,7},{7,6},{8,9},{9,8},{10,11... | collective-permute-start | bytes 350216 | tf_op jit(solution)/shard_map/ppermute | solution.py:207
  6.2 9.1 %collective-permute-start.3 = (bf16[8,7296]{1,0:T(8,128)(2,1)S(1)}, bf16[8,7296]{1,0:T(8,128)(2,1)S(1)}, u32[]{:S(2)}, u32[]{:S(2)}) collective-permute-start(bf16[8,7296]{1,0:T(8,128)(2,1)S(1)} %shard_map.73.ready_ref), channel_id=1, source_target_pairs={{0,3},{1,2},{2,1},{3,0},{4,7},{5,6},{6,5},{7,4},{8,11},{9,10},{10,... | collective-permute-start | bytes 350216 | tf_op jit(solution)/shard_map/ppermute | solution.py:207
  8.7 10.0 %collective-permute-start.2 = (bf16[8,7296]{1,0:T(8,128)(2,1)S(1)}, bf16[8,7296]{1,0:T(8,128)(2,1)S(1)}, u32[]{:S(2)}, u32[]{:S(2)}) collective-permute-start(bf16[8,7296]{1,0:T(8,128)(2,1)S(1)} %shard_map.73.ready_ref), channel_id=1, source_target_pairs={{0,2},{1,3},{2,0},{3,1},{4,6},{5,7},{6,4},{7,5},{8,10},{9,11},{10,... | collective-permute-start | bytes 350216 | tf_op jit(solution)/shard_map/ppermute | solution.py:207
  8.8 6.4 %copy-start = (bf16[8,7168]{1,0:T(8,128)(2,1)S(1)}, bf16[8,7168]{1,0:T(8,128)(2,1)}, u32[]{:S(2)}) copy-start(bf16[8,7168]{1,0:T(8,128)(2,1)} %tokens_ref.1) | copy-start | bytes 344068
  15.3 5.0 %collective-permute-start.1 = (bf16[16,7168]{1,0:T(8,128)(2,1)S(1)}, bf16[16,7168]{1,0:T(8,128)(2,1)S(1)}, u32[]{:S(2)}, u32[]{:S(2)}) collective-permute-start(bf16[16,7168]{1,0:T(8,128)(2,1)S(1)} %pad_maximum_fusion.3), channel_id=1, source_target_pairs={{0,4},{4,0},{8,12},{12,8},{1,5},{5,1},{9,13},{13,9},{2,6},{6,2},{1... | collective-permute-start | bytes 688136 | tf_op jit(solution)/shard_map/ppermute | solution.py:207
  18.7 9.2 %collective-permute-start.6 = (bf16[24,7296]{1,0:T(8,128)(2,1)S(1)}, bf16[24,7296]{1,0:T(8,128)(2,1)S(1)}, u32[]{:S(2)}, u32[]{:S(2)}) collective-permute-start(bf16[24,7296]{1,0:T(8,128)(2,1)S(1)} %pad_maximum_fusion.2.ready_ref), channel_id=1, source_target_pairs={{0,8},{4,12},{8,0},{12,4},{1,9},{5,13},{9,1},{13,5},{2,10},{6,14},... | collective-permute-start | bytes 1050632 | tf_op jit(solution)/shard_map/ppermute | solution.py:207
  28.0 2.6 %collective-permute-start.7 = (bf16[64,7296]{1,0:T(8,128)(2,1)S(1)}, bf16[64,7296]{1,0:T(8,128)(2,1)S(1)}, u32[]{:S(2)}, u32[]{:S(2)}) collective-permute-start(bf16[64,7296]{1,0:T(8,128)(2,1)S(1)} %pad_maximum_fusion.half_ref), channel_id=1, source_target_pairs={{0,4},{4,0},{8,12},{12,8},{1,5},{5,1},{9,13},{13,9},{2,6},{6,2},{1... | collective-permute-start | bytes 2801672 | tf_op jit(solution)/shard_map/ppermute | solution.py:207
  32.5 1.6 %collective-permute-start.11 = (bf16[16,7168]{1,0:T(8,128)(2,1)S(1)}, bf16[16,7168]{1,0:T(8,128)(2,1)S(1)}, u32[]{:S(2)}, u32[]{:S(2)}) collective-permute-start(bf16[16,7168]{1,0:T(8,128)(2,1)S(1)} %slice.63), channel_id=1, source_target_pairs={{0,4},{4,0},{8,12},{12,8},{1,5},{5,1},{9,13},{13,9},{2,6},{6,2},{1... | collective-permute-start | bytes 688136 | tf_op jit(solution)/shard_map/ppermute | solution.py:207
  34.1 5.3 %collective-permute-start.12 = (bf16[8,7168]{1,0:T(8,128)(2,1)S(1)}, bf16[8,7168]{1,0:T(8,128)(2,1)S(1)}, u32[]{:S(2)}, u32[]{:S(2)}) collective-permute-start(bf16[8,7168]{1,0:T(8,128)(2,1)S(1)} %slice.65), channel_id=1, source_target_pairs={{0,8},{4,12},{8,0},{12,4},{1,9},{5,13},{9,1},{13,5},{2,10},{6,14},... | collective-permute-start | bytes 344072 | tf_op jit(solution)/shard_map/ppermute | solution.py:207
  36.5 3.9 %collective-permute-start.8 = (bf16[32,7168]{1,0:T(8,128)(2,1)S(1)}, bf16[32,7168]{1,0:T(8,128)(2,1)S(1)}, u32[]{:S(2)}, u32[]{:S(2)}) collective-permute-start(bf16[32,7168]{1,0:T(8,128)(2,1)S(1)} %slice.57), channel_id=1, source_target_pairs={{0,4},{4,0},{8,12},{12,8},{1,5},{5,1},{9,13},{13,9},{2,6},{6,2},{1... | collective-permute-start | bytes 1376264 | tf_op jit(solution)/shard_map/ppermute | solution.py:207
  39.4 12.1 %collective-permute-start.13 = (bf16[8,7168]{1,0:T(8,128)(2,1)S(1)}, bf16[8,7168]{1,0:T(8,128)(2,1)S(1)}, u32[]{:S(2)}, u32[]{:S(2)}) collective-permute-start(bf16[8,7168]{1,0:T(8,128)(2,1)S(1)} %add_convert_fusion.5), channel_id=1, source_target_pairs={{0,2},{1,3},{2,0},{3,1},{4,6},{5,7},{6,4},{7,5},{8,10},{9,11},{10,... | collective-permute-start | bytes 344072 | tf_op jit(solution)/shard_map/ppermute | solution.py:207
  40.5 6.6 %collective-permute-start.14 = (bf16[16,7168]{1,0:T(8,128)(2,1)S(1)}, bf16[16,7168]{1,0:T(8,128)(2,1)S(1)}, u32[]{:S(2)}, u32[]{:S(2)}) collective-permute-start(bf16[16,7168]{1,0:T(8,128)(2,1)S(1)} %slice.67), channel_id=1, source_target_pairs={{0,8},{4,12},{8,0},{12,4},{1,9},{5,13},{9,1},{13,5},{2,10},{6,14},... | collective-permute-start | bytes 688136 | tf_op jit(solution)/shard_map/ppermute | solution.py:207
  44.3 5.6 %collective-permute-start.9 = (bf16[16,7168]{1,0:T(8,128)(2,1)S(1)}, bf16[16,7168]{1,0:T(8,128)(2,1)S(1)}, u32[]{:S(2)}, u32[]{:S(2)}) collective-permute-start(bf16[16,7168]{1,0:T(8,128)(2,1)S(1)} %slice.59), channel_id=1, source_target_pairs={{0,4},{4,0},{8,12},{12,8},{1,5},{5,1},{9,13},{13,9},{2,6},{6,2},{1... | collective-permute-start | bytes 688136 | tf_op jit(solution)/shard_map/ppermute | solution.py:207
  47.2 6.8 %collective-permute-start.15 = (bf16[8,7168]{1,0:T(8,128)(2,1)S(1)}, bf16[8,7168]{1,0:T(8,128)(2,1)S(1)}, u32[]{:S(2)}, u32[]{:S(2)}) collective-permute-start(bf16[8,7168]{1,0:T(8,128)(2,1)S(1)} %get-tuple-element.29), channel_id=1, source_target_pairs={{0,3},{1,2},{2,1},{3,0},{4,7},{5,6},{6,5},{7,4},{8,11},{9,10},{10,... | collective-permute-start | bytes 344072 | tf_op jit(solution)/shard_map/ppermute | solution.py:207
  48.7 6.0 %collective-permute-start.16 = (bf16[8,7168]{1,0:T(8,128)(2,1)S(1)}, bf16[8,7168]{1,0:T(8,128)(2,1)S(1)}, u32[]{:S(2)}, u32[]{:S(2)}) collective-permute-start(bf16[8,7168]{1,0:T(8,128)(2,1)S(1)} %get-tuple-element.30), channel_id=1, source_target_pairs={{0,1},{1,0},{2,3},{3,2},{4,5},{5,4},{6,7},{7,6},{8,9},{9,8},{10,11... | collective-permute-start | bytes 344072 | tf_op jit(solution)/shard_map/ppermute | solution.py:207
  49.9 4.9 %collective-permute-start.10 = (bf16[8,7168]{1,0:T(8,128)(2,1)S(1)}, bf16[8,7168]{1,0:T(8,128)(2,1)S(1)}, u32[]{:S(2)}, u32[]{:S(2)}) collective-permute-start(bf16[8,7168]{1,0:T(8,128)(2,1)S(1)} %slice.61), channel_id=1, source_target_pairs={{0,8},{4,12},{8,0},{12,4},{1,9},{5,13},{9,1},{13,5},{2,10},{6,14},... | collective-permute-start | bytes 344072 | tf_op jit(solution)/shard_map/ppermute | solution.py:207

commit v4 on v3

--- a/solution.py
+++ b/solution.py
@@ -160,11 +160,11 @@
     )(rows, pltpu.with_memory_space_constraint(up, pltpu.HBM), ready)
 
 
-def routed_up_kernel(layout, half_ref, other_ref, flat_ref, named_ref, *rest):
-    outs, sums = rest[:-1], rest[-1]
+def routed_kernel(pieces, half_ref, other_ref, flat_ref, down_ref, named_ref, shared_ref, keep_ref, send_ref, sums):
     depth, hidden = flat_ref.shape[0], flat_ref.shape[1] // 2
+    rows, width = keep_ref.shape
     steps = 7
-    block = depth // steps
+    block, piece = depth // steps, width // steps
     for i in range(steps):
         at = slice(i * block, (i + 1) * block)
         left = jnp.concatenate([half_ref[:, at], other_ref[:, at]], axis=0)
@@ -175,27 +175,33 @@
     weight = jnp.sum(named, axis=1, keepdims=True)
     gate, lift = sums[:, :hidden], sums[:, hidden:]
     sums[:, :hidden] = gate / (1.0 + jnp.exp(-gate)) * lift * weight
-    for out, pieces in zip(outs, layout):
-        rows = [sums[first:first + count, :hidden] for first, count in pieces]
-        out[...] = jnp.concatenate(rows, axis=0).astype(jnp.bfloat16)
-
-
-def routed_hidden(half, other, flat, named, layout):
-    count, hidden = 2 * half.shape[0], flat.shape[1] // 2
-    return pl.pallas_call(
-        functools.partial(routed_up_kernel, layout),
-        in_specs=[pl.BlockSpec(memory_space=pltpu.VMEM)] * 4,
-        out_specs=[pl.BlockSpec(memory_space=pltpu.VMEM)] * len(layout),
-        out_shape=[
-            jax.ShapeDtypeStruct((sum(rows for _, rows in pieces), hidden), jnp.bfloat16)
-            for pieces in layout
-        ],
-        scratch_shapes=[pltpu.VMEM((count, 2 * hidden), jnp.float32)],
+    ordered = [sums[first:first + count, :hidden] for first, count in pieces]
+    middle = jnp.concatenate(ordered, axis=0).astype(jnp.bfloat16)
+    own = shared_ref.shape[0] // CORES
+    for i in range(steps):
+        at = slice(i * piece, (i + 1) * piece)
+        term = jnp.dot(middle, down_ref[:, at], preferred_element_type=jnp.float32)
+        for core, out in enumerate((keep_ref, send_ref)):
+            first = core * rows
+            near = term[first:first + own] + shared_ref[core * own:(core + 1) * own, at]
+            out[:, at] = jnp.concatenate([near, term[first + own:first + rows]], axis=0).astype(jnp.bfloat16)
+
+
+def routed_parts(half, other, flat, down, named, shared, pieces):
+    rows, width = half.shape[0], down.shape[1]
+    return pl.pallas_call(
+        functools.partial(routed_kernel, pieces),
+        in_specs=[pl.BlockSpec(memory_space=pltpu.VMEM)] * 6,
+        out_specs=[pl.BlockSpec(memory_space=pltpu.VMEM)] * CORES,
+        out_shape=[jax.ShapeDtypeStruct((rows, width), jnp.bfloat16)] * CORES,
+        scratch_shapes=[pltpu.VMEM((CORES * rows, flat.shape[1]), jnp.float32)],
         compiler_params=pltpu.CompilerParams(vmem_limit_bytes=VMEM_LIMIT),
         cost_estimate=pl.CostEstimate(
-            flops=2 * count * flat.size, bytes_accessed=2 * flat.size, transcendentals=0
-        ),
-    )(half, other, flat, named)
+            flops=2 * CORES * rows * (flat.size + down.size),
+            bytes_accessed=2 * (flat.size + down.size),
+            transcendentals=0,
+        ),
+    )(half, other, flat, down, named, shared)
 
 
 def after(value, ready):
@@ -210,12 +216,6 @@
 def half_ep(rows, experts):
     parts = [exchange(rows, "ep", chip) for chip in range(CORES, experts, CORES)]
     return jnp.concatenate([rows] + parts, axis=0)
-
-
-def pair_sum(partial):
-    half = partial.shape[0] // CORES
-    other = exchange(partial[half:], "ep", 1)
-    return (partial[:half].astype(jnp.float32) + other.astype(jnp.float32)).astype(jnp.bfloat16)
 
 
 def chip_sum(pair, experts):
@@ -239,10 +239,10 @@
     routed_rows = owner_rows(tokens, routes, gates, named, lanes)
     token_half = half_ep(after(tokens, routed_rows), experts)
 
-    groups = [[subs // 2], [k for k in range(subs - 1, 0, -1) if k != subs // 2]]
-    order = [k for group in groups for k in group]
+    order = list(range(2, subs))
     far = jnp.concatenate([exchange(routed_rows, "sub", k) for k in order], axis=0)
     own_half = half_ep(routed_rows, experts)
+    near_half = exchange(own_half, "sub", 1)
     token_all = jnp.concatenate([token_half, exchange(token_half, "ep", 1)], axis=0)
     expert_weights, down_weights, shared_weights = held_weights(
         expert_up[0], expert_down[0], shared_down, routed_rows
@@ -251,32 +251,31 @@
     middle = shared_middle(token_all, shared_up, far)
 
     far_half = half_ep(far, experts)
-    half = after(jnp.concatenate([own_half, far_half], axis=0), middle)
+    half = after(jnp.concatenate([own_half, near_half, far_half], axis=0), middle)
     other = exchange(half, "ep", 1)
 
     chips, split = experts // CORES, own_half.shape[0]
-    layout = [[(core * half.shape[0], split) for core in range(CORES)]]
-    at = 0
-    for group in groups:
-        size = len(group) * count
-        layout.append([
-            (core * half.shape[0] + split + chip * len(order) * count + at, size)
-            for core in range(CORES) for chip in range(chips)
-        ])
-        at += size
-    own_hidden, *far_hidden = routed_hidden(half, other, expert_weights, named, layout)
-
-    def down(hidden, weights):
-        return jnp.dot(hidden, weights, preferred_element_type=jnp.float32)
-
-    pairs = [pair_sum(down(hidden, down_weights).astype(bf)) for hidden in far_hidden]
-    middle, own_hidden = after((middle, own_hidden), pairs[-1])
-    own_part = (down(middle, shared_weights) + down(own_hidden, down_weights)).astype(bf)
-    sums = [chip_sum(pair, experts).astype(bf) for pair in pairs]
-    total = chip_sum(pair_sum(own_part), experts)
-    for rows, group in zip(sums, groups):
-        for at, k in enumerate(group):
-            total = total + exchange(rows[at * count:(at + 1) * count], "sub", k).astype(jnp.float32)
+    pieces = []
+    for core in range(CORES):
+        first = core * half.shape[0]
+        pieces.append((first, 2 * split))
+        pieces += [
+            (first + 2 * split + (chip * len(order) + at) * count, count)
+            for at in range(len(order)) for chip in range(chips)
+        ]
+    shared_part = jnp.dot(middle, shared_weights, preferred_element_type=jnp.float32)
+    keep, send = routed_parts(half, other, expert_weights, down_weights, named, shared_part, pieces)
+    pair = (keep.astype(jnp.float32) + exchange(send, "ep", 1).astype(jnp.float32)).astype(bf)
+
+    sums = [
+        chip_sum(pair[at:at + split], experts).astype(bf)
+        for at in range(2 * split, pair.shape[0], split)
+    ]
+    near = exchange(pair[split:2 * split], "sub", 1)
+    near = (pair[:split].astype(jnp.float32) + near.astype(jnp.float32)).astype(bf)
+    total = chip_sum(near, experts)
+    for rows, k in zip(sums, order):
+        total = total + exchange(rows, "sub", k).astype(jnp.float32)
     return total.astype(bf)
 
 

time: 55.6 us -> 51.2 us (0.921)
  matrix products: 3.62 us -> 1.39 us
  waiting for transfers between devices: 16.8 us -> 15 us
  starting transfers between devices: 18.3 us -> 17.3 us
  Pallas kernels: 15.2 us -> 15.8 us
    dot_general x4 -> x1, matrix products: 3.62 us -> 1.39 us  [per_device(): jnp.dot(middle, shared_weights, preferred_element_type=jnp.float32)]
    ppermute x17 -> x15, waiting for transfers between devices: 16.8 us -> 15 us  [exchange(): return lax.ppermute(rows, axis, [(i, i ^ flip) for i in range(size)])]
    ppermute x17 -> x15, starting transfers between devices: 18.3 us -> 17.3 us  [exchange(): return lax.ppermute(rows, axis, [(i, i ^ flip) for i in range(size)])]
    pallas_call x1, Pallas kernels: 1.14 us -> 1.75 us  [routed_parts(): pl.pallas_call(functools.partial(routed_kernel, pieces), in_specs=[pl.Blo...]
  transfers between devices with their start and end apart: 17 -> 15, of which waited for: 9 -> 6; matrix products, arithmetic and copies ran while one was open for 6% -> 3% of each run, Pallas kernels for 23% -> 25%
where the time goes in v4:
time: 51.2 us; the launch traced here: 51 us
  starting transfers between devices  17.3 us (34%)
  Pallas kernels  15.8 us (31%)
  waiting for transfers between devices  15 us (29%)
  matrix products  1.39 us (3%)
  other arithmetic  1.15 us (2%)
    ppermute x15, starting transfers between devices, exchange(): return lax.ppermute(rows, axis, [(i, i ^ flip) for i in range(size)])  17.3 us
    ppermute x15, waiting for transfers between devices, exchange(): return lax.ppermute(rows, axis, [(i, i ^ flip) for i in range(size)])  15 us
    pallas_call x1, Pallas kernels, shared_middle(): pl.pallas_call(shared_up_kernel, in_specs=[pl.BlockSpec(memory_space=pltp...  6.6 us
    pallas_call x1, Pallas kernels, held_weights(): pl.pallas_call(weights_kernel, in_specs=[pl.BlockSpec(memory_space=pltpu....  6.39 us
    pallas_call x1, Pallas kernels, routed_parts(): pl.pallas_call(functools.partial(routed_kernel, pieces), in_specs=[pl.Blo...  1.75 us
    dot_general x1, matrix products, per_device(): jnp.dot(middle, shared_weights, preferred_element_type=jnp.float32)  1.39 us
    pallas_call x1, Pallas kernels, owner_rows(): pl.pallas_call(owner_kernel, in_specs=[pl.BlockSpec(memory_space=pltpu.HB...  1.09 us
  transfers between devices with their start and end apart: 15, of which 6 were waited for; matrix products, arithmetic and copies ran while one was open for 3% of the time, Pallas kernels for 25%

profile of v4, /device:TPU:0, one launch (start us, length us, event | category | flops | bytes accessed | tf_op | source)
XLA Modules:
  0.0 51.0 jit_solution(12210584352006779245)
XLA Ops:
  0.0 1.1 %shard_map.73.ready_ref = bf16[8,7296]{1,0:T(8,128)(2,1)S(1)} custom-call(bf16[8,7168]{1,0:T(8,128)(2,1)} %tokens_ref.1, s32[2,8]{1,0:T(2,128)} %bitcast.8, bf16[2,8]{1,0:T(2,128)(2,1)} %bitcast.9, f32[1,128]{1,0:T(1,128)S(1)} %compare_convert_fusion.ready_ref.named_ref), custom_call_target="tpu_custom_call" | custom-call | tf_op jit(solution)/shard_map/pallas_call | solution.py:56
  1.1 5.1 %collective-permute-start.3 = (bf16[8,7296]{1,0:T(8,128)(2,1)S(1)}, bf16[8,7296]{1,0:T(8,128)(2,1)S(1)}, u32[]{:S(2)}, u32[]{:S(2)}) collective-permute-start(bf16[8,7296]{1,0:T(8,128)(2,1)S(1)} %shard_map.73.ready_ref), channel_id=1, source_target_pairs={{0,3},{1,2},{2,1},{3,0},{4,7},{5,6},{6,5},{7,4},{8,11},{9,10},{10,... | collective-permute-start | bytes 350216 | tf_op jit(solution)/shard_map/ppermute | solution.py:213
  6.2 1.5 %collective-permute-start = (bf16[8,7296]{1,0:T(8,128)(2,1)S(1)}, bf16[8,7296]{1,0:T(8,128)(2,1)S(1)}, u32[]{:S(2)}, u32[]{:S(2)}) collective-permute-start(bf16[8,7296]{1,0:T(8,128)(2,1)S(1)} %shard_map.73.ready_ref), channel_id=1, source_target_pairs={{0,8},{4,12},{8,0},{12,4},{1,9},{5,13},{9,1},{13,5},{2,10},{6,14},... | collective-permute-start | bytes 350216 | tf_op jit(solution)/shard_map/ppermute | solution.py:213
  7.7 0.5 collective-permute-start.5
  8.3 6.4 %shard_map.74 = (bf16[7168,512]{1,0:T(8,128)(2,1)S(1)}, bf16[256,7168]{1,0:T(8,128)(2,1)S(1)}, bf16[512,7168]{1,0:T(8,128)(2,1)S(1)}) custom-call(bf16[7168,2,256]{2,1,0:T(2,128)(2,1)} %bitcast.6, bf16[256,7168]{1,0:T(8,128)(2,1)} %bitcast.7, bf16[512,7168]{1,0:T(8,128)(2,1)} %shared_ref.1, bf16[8,7296]{1,0:T(8,128)(2,1)S(1)} %shard_map.73.ready_ref), custom_call_target="tpu_custom_call" | custom-call | bytes 14680064 | tf_op jit(solution)/shard_map/pallas_call | solution.py:98
  14.8 0.7 %collective-permute-start.1 = (bf16[16,7296]{1,0:T(8,128)(2,1)S(1)}, bf16[16,7296]{1,0:T(8,128)(2,1)S(1)}, u32[]{:S(2)}, u32[]{:S(2)}) collective-permute-start(bf16[16,7296]{1,0:T(8,128)(2,1)S(1)} %pad_maximum_fusion.1), channel_id=1, source_target_pairs={{0,1},{1,0},{2,3},{3,2},{4,5},{5,4},{6,7},{7,6},{8,9},{9,8},{10,11... | collective-permute-start | bytes 700424 | tf_op jit(solution)/shard_map/ppermute | solution.py:213
  15.5 0.5 %collective-permute-done.2 = bf16[8,7296]{1,0:T(8,128)(2,1)S(1)} collective-permute-done((bf16[8,7296]{1,0:T(8,128)(2,1)S(1)}, bf16[8,7296]{1,0:T(8,128)(2,1)S(1)}, u32[]{:S(2)}, u32[]{:S(2)}) %collective-permute-start.2) | collective-permute-done | bytes 116768 | tf_op jit(solution)/shard_map/ppermute | solution.py:213
  16.1 1.6 %collective-permute-start.4 = (bf16[16,7296]{1,0:T(8,128)(2,1)S(1)}, bf16[16,7296]{1,0:T(8,128)(2,1)S(1)}, u32[]{:S(2)}, u32[]{:S(2)}) collective-permute-start(bf16[16,7296]{1,0:T(8,128)(2,1)S(1)} %pad_maximum_fusion.2.ready_ref), channel_id=1, source_target_pairs={{0,8},{4,12},{8,0},{12,4},{1,9},{5,13},{9,1},{13,5},{2,10},{6,14},... | collective-permute-start | bytes 700424 | tf_op jit(solution)/shard_map/ppermute | solution.py:213
  17.7 6.6 %shard_map.75 = bf16[32,512]{1,0:T(8,128)(2,1)S(1)} custom-call(bf16[32,7168]{1,0:T(8,128)(2,1)S(1)} %pad_maximum_fusion.rows_ref, bf16[7168,2,512]{2,1,0:T(2,128)(2,1)} %up_ref.1, bf16[16,7296]{1,0:T(8,128)(2,1)S(1)} %pad_maximum_fusion.2.ready_ref), custom_call_target="tpu_custom_call" | custom-call | flops 469762048 | bytes 14680064 | tf_op jit(solution)/shard_map/pallas_call | solution.py:140
  24.5 1.4 %fusion.1.shared_ref = f32[32,7168]{1,0:T(8,128)S(1)} fusion(bf16[32,512]{1,0:T(8,128)(2,1)S(1)} %shard_map.75, bf16[512,7168]{1,0:T(8,128)(2,1)S(1)} %get-tuple-element.20), kind=kOutput, calls=%fused_computation.16 | convolution fusion | flops 234881024 | bytes 8290304 | tf_op jit(solution)/shard_map/dot_general | solution.py:266
  25.9 1.1 %collective-permute-done.7.other_ref = bf16[64,7296]{1,0:T(8,128)(2,1)S(1)} collective-permute-done((bf16[64,7296]{1,0:T(8,128)(2,1)S(1)}, bf16[64,7296]{1,0:T(8,128)(2,1)S(1)}, u32[]{:S(2)}, u32[]{:S(2)}) %collective-permute-start.7) | collective-permute-done | bytes 933920 | tf_op jit(solution)/shard_map/ppermute | solution.py:213
  27.0 1.8 %shard_map.76 = (bf16[64,7168]{1,0:T(8,128)(2,1)S(1)}, bf16[64,7168]{1,0:T(8,128)(2,1)S(1)}) custom-call(bf16[64,7296]{1,0:T(8,128)(2,1)S(1)} %constant_dynamic-update-slice_fusion.half_ref, bf16[64,7296]{1,0:T(8,128)(2,1)S(1)} %collective-permute-done.7.other_ref, bf16[7168,512]{1,0:T(8,128)(2,1)S(1)} %get-tuple-element.18.flat_ref, ...), custom_call_target="tpu_custom_call" | custom-call | flops 1409286144 | bytes 11010048 | tf_op jit(solution)/shard_map/pallas_call | solution.py:192
  28.8 0.2 collective-permute-start.8
  29.0 2.3 %collective-permute-done.8 = bf16[64,7168]{1,0:T(8,128)(2,1)S(1)} collective-permute-done((bf16[64,7168]{1,0:T(8,128)(2,1)S(1)}, bf16[64,7168]{1,0:T(8,128)(2,1)S(1)}, u32[]{:S(2)}, u32[]{:S(2)}) %collective-permute-start.8) | collective-permute-done | bytes 917536 | tf_op jit(solution)/shard_map/ppermute | solution.py:213
  31.6 0.7 %collective-permute-start.11 = (bf16[8,7168]{1,0:T(8,128)(2,1)S(1)}, bf16[8,7168]{1,0:T(8,128)(2,1)S(1)}, u32[]{:S(2)}, u32[]{:S(2)}) collective-permute-start(bf16[8,7168]{1,0:T(8,128)(2,1)S(1)} %get-tuple-element.25), channel_id=1, source_target_pairs={{0,8},{4,12},{8,0},{12,4},{1,9},{5,13},{9,1},{13,5},{2,10},{6,14},... | collective-permute-start | bytes 344072 | tf_op jit(solution)/shard_map/ppermute | solution.py:213
  32.3 1.4 %collective-permute-start.13 = (bf16[8,7168]{1,0:T(8,128)(2,1)S(1)}, bf16[8,7168]{1,0:T(8,128)(2,1)S(1)}, u32[]{:S(2)}, u32[]{:S(2)}) collective-permute-start(bf16[8,7168]{1,0:T(8,128)(2,1)S(1)} %get-tuple-element.26), channel_id=1, source_target_pairs={{0,8},{4,12},{8,0},{12,4},{1,9},{5,13},{9,1},{13,5},{2,10},{6,14},... | collective-permute-start | bytes 344072 | tf_op jit(solution)/shard_map/ppermute | solution.py:213
  33.7 0.9 %collective-permute-start.9 = (bf16[16,7168]{1,0:T(8,128)(2,1)S(1)}, bf16[16,7168]{1,0:T(8,128)(2,1)S(1)}, u32[]{:S(2)}, u32[]{:S(2)}) collective-permute-start(bf16[16,7168]{1,0:T(8,128)(2,1)S(1)} %slice.39), channel_id=1, source_target_pairs={{0,1},{1,0},{2,3},{3,2},{4,5},{5,4},{6,7},{7,6},{8,9},{9,8},{10,11... | collective-permute-start | bytes 688136 | tf_op jit(solution)/shard_map/ppermute | solution.py:213
  34.6 3.0 %collective-permute-done.11 = bf16[8,7168]{1,0:T(8,128)(2,1)S(1)} collective-permute-done((bf16[8,7168]{1,0:T(8,128)(2,1)S(1)}, bf16[8,7168]{1,0:T(8,128)(2,1)S(1)}, u32[]{:S(2)}, u32[]{:S(2)}) %collective-permute-start.11) | collective-permute-done | bytes 114720 | tf_op jit(solution)/shard_map/ppermute | solution.py:213
  37.6 1.7 %collective-permute-done.13 = bf16[8,7168]{1,0:T(8,128)(2,1)S(1)} collective-permute-done((bf16[8,7168]{1,0:T(8,128)(2,1)S(1)}, bf16[8,7168]{1,0:T(8,128)(2,1)S(1)}, u32[]{:S(2)}, u32[]{:S(2)}) %collective-permute-start.13) | collective-permute-done | bytes 114720 | tf_op jit(solution)/shard_map/ppermute | solution.py:213
  39.3 1.9 %collective-permute-start.12 = (bf16[8,7168]{1,0:T(8,128)(2,1)S(1)}, bf16[8,7168]{1,0:T(8,128)(2,1)S(1)}, u32[]{:S(2)}, u32[]{:S(2)}) collective-permute-start(bf16[8,7168]{1,0:T(8,128)(2,1)S(1)} %get-tuple-element.23), channel_id=1, source_target_pairs={{0,2},{1,3},{2,0},{3,1},{4,6},{5,7},{6,4},{7,5},{8,10},{9,11},{10,... | collective-permute-start | bytes 344072 | tf_op jit(solution)/shard_map/ppermute | solution.py:213
  41.2 1.4 %collective-permute-start.14 = (bf16[8,7168]{1,0:T(8,128)(2,1)S(1)}, bf16[8,7168]{1,0:T(8,128)(2,1)S(1)}, u32[]{:S(2)}, u32[]{:S(2)}) collective-permute-start(bf16[8,7168]{1,0:T(8,128)(2,1)S(1)} %get-tuple-element.24), channel_id=1, source_target_pairs={{0,3},{1,2},{2,1},{3,0},{4,7},{5,6},{6,5},{7,4},{8,11},{9,10},{10,... | collective-permute-start | bytes 344072 | tf_op jit(solution)/shard_map/ppermute | solution.py:213
  42.8 1.1 %collective-permute-start.10 = (bf16[8,7168]{1,0:T(8,128)(2,1)S(1)}, bf16[8,7168]{1,0:T(8,128)(2,1)S(1)}, u32[]{:S(2)}, u32[]{:S(2)}) collective-permute-start(bf16[8,7168]{1,0:T(8,128)(2,1)S(1)} %slice.41), channel_id=1, source_target_pairs={{0,8},{4,12},{8,0},{12,4},{1,9},{5,13},{9,1},{13,5},{2,10},{6,14},... | collective-permute-start | bytes 344072 | tf_op jit(solution)/shard_map/ppermute | solution.py:213
  43.9 6.4 %collective-permute-done.12 = bf16[8,7168]{1,0:T(8,128)(2,1)S(1)} collective-permute-done((bf16[8,7168]{1,0:T(8,128)(2,1)S(1)}, bf16[8,7168]{1,0:T(8,128)(2,1)S(1)}, u32[]{:S(2)}, u32[]{:S(2)}) %collective-permute-start.12) | collective-permute-done | bytes 114720 | tf_op jit(solution)/shard_map/ppermute | solution.py:213
  50.3 0.7 %add_convert_fusion.2 = bf16[8,7168]{1,0:T(8,128)(2,1)} fusion(bf16[8,7168]{1,0:T(8,128)(2,1)S(1)} %collective-permute-done.14, bf16[8,7168]{1,0:T(8,128)(2,1)S(1)} %collective-permute-done.12, bf16[8,7168]{1,0:T(8,128)(2,1)S(1)} %collective-permute-done.10, bf16[16,7168]{1,0:T(8,128)(2,1)S(1)} %add_convert_fusion.1), kind=kLoop, calls=%fused_computation.6 | loop fusion | flops 458752 | bytes 573440 | tf_op jit(solution)/shard_map/convert_element_type | solution.py:279
  (30 shorter events, 0.8 us)
Async XLA Ops:
  1.1 14.4 %collective-permute-start.3 = (bf16[8,7296]{1,0:T(8,128)(2,1)S(1)}, bf16[8,7296]{1,0:T(8,128)(2,1)S(1)}, u32[]{:S(2)}, u32[]{:S(2)}) collective-permute-start(bf16[8,7296]{1,0:T(8,128)(2,1)S(1)} %shard_map.73.ready_ref), channel_id=1, source_target_pairs={{0,3},{1,2},{2,1},{3,0},{4,7},{5,6},{6,5},{7,4},{8,11},{9,10},{10,... | collective-permute-start | bytes 350216 | tf_op jit(solution)/shard_map/ppermute | solution.py:213
  6.2 9.8 %collective-permute-start.2 = (bf16[8,7296]{1,0:T(8,128)(2,1)S(1)}, bf16[8,7296]{1,0:T(8,128)(2,1)S(1)}, u32[]{:S(2)}, u32[]{:S(2)}) collective-permute-start(bf16[8,7296]{1,0:T(8,128)(2,1)S(1)} %shard_map.73.ready_ref), channel_id=1, source_target_pairs={{0,2},{1,3},{2,0},{3,1},{4,6},{5,7},{6,4},{7,5},{8,10},{9,11},{10,... | collective-permute-start | bytes 350216 | tf_op jit(solution)/shard_map/ppermute | solution.py:213
  6.2 8.6 %collective-permute-start = (bf16[8,7296]{1,0:T(8,128)(2,1)S(1)}, bf16[8,7296]{1,0:T(8,128)(2,1)S(1)}, u32[]{:S(2)}, u32[]{:S(2)}) collective-permute-start(bf16[8,7296]{1,0:T(8,128)(2,1)S(1)} %shard_map.73.ready_ref), channel_id=1, source_target_pairs={{0,8},{4,12},{8,0},{12,4},{1,9},{5,13},{9,1},{13,5},{2,10},{6,14},... | collective-permute-start | bytes 350216 | tf_op jit(solution)/shard_map/ppermute | solution.py:213
  7.7 6.9 %collective-permute-start.5 = (bf16[8,7168]{1,0:T(8,128)(2,1)}, bf16[8,7168]{1,0:T(8,128)(2,1)S(1)}, u32[]{:S(2)}, u32[]{:S(2)}) collective-permute-start(bf16[8,7168]{1,0:T(8,128)(2,1)} %tokens_ref.1), channel_id=1, source_target_pairs={{0,8},{4,12},{8,0},{12,4},{1,9},{5,13},{9,1},{13,5},{2,10},{6,14},... | collective-permute-start | bytes 344072 | tf_op jit(solution)/shard_map/ppermute | solution.py:213
  8.3 6.4 %copy-start = (bf16[8,7168]{1,0:T(8,128)(2,1)S(1)}, bf16[8,7168]{1,0:T(8,128)(2,1)}, u32[]{:S(2)}) copy-start(bf16[8,7168]{1,0:T(8,128)(2,1)} %tokens_ref.1) | copy-start | bytes 344068
  14.7 3.0 %collective-permute-start.6 = (bf16[16,7168]{1,0:T(8,128)(2,1)S(1)}, bf16[16,7168]{1,0:T(8,128)(2,1)S(1)}, u32[]{:S(2)}, u32[]{:S(2)}) collective-permute-start(bf16[16,7168]{1,0:T(8,128)(2,1)S(1)} %pad_maximum_fusion.3), channel_id=1, source_target_pairs={{0,4},{4,0},{8,12},{12,8},{1,5},{5,1},{9,13},{13,9},{2,6},{6,2},{1... | collective-permute-start | bytes 688136 | tf_op jit(solution)/shard_map/ppermute | solution.py:213
  14.8 9.5 %collective-permute-start.1 = (bf16[16,7296]{1,0:T(8,128)(2,1)S(1)}, bf16[16,7296]{1,0:T(8,128)(2,1)S(1)}, u32[]{:S(2)}, u32[]{:S(2)}) collective-permute-start(bf16[16,7296]{1,0:T(8,128)(2,1)S(1)} %pad_maximum_fusion.1), channel_id=1, source_target_pairs={{0,1},{1,0},{2,3},{3,2},{4,5},{5,4},{6,7},{7,6},{8,9},{9,8},{10,11... | collective-permute-start | bytes 700424 | tf_op jit(solution)/shard_map/ppermute | solution.py:213
  16.1 8.3 %collective-permute-start.4 = (bf16[16,7296]{1,0:T(8,128)(2,1)S(1)}, bf16[16,7296]{1,0:T(8,128)(2,1)S(1)}, u32[]{:S(2)}, u32[]{:S(2)}) collective-permute-start(bf16[16,7296]{1,0:T(8,128)(2,1)S(1)} %pad_maximum_fusion.2.ready_ref), channel_id=1, source_target_pairs={{0,8},{4,12},{8,0},{12,4},{1,9},{5,13},{9,1},{13,5},{2,10},{6,14},... | collective-permute-start | bytes 700424 | tf_op jit(solution)/shard_map/ppermute | solution.py:213
  24.5 2.6 %collective-permute-start.7 = (bf16[64,7296]{1,0:T(8,128)(2,1)S(1)}, bf16[64,7296]{1,0:T(8,128)(2,1)S(1)}, u32[]{:S(2)}, u32[]{:S(2)}) collective-permute-start(bf16[64,7296]{1,0:T(8,128)(2,1)S(1)} %constant_dynamic-update-slice_fusion.half_ref), channel_id=1, source_target_pairs={{0,4},{4,0},{8,12},{12,8},{1,5},{5,1},{9,13},{13,9},{2,6},{6,2},{1... | collective-permute-start | bytes 2801672 | tf_op jit(solution)/shard_map/ppermute | solution.py:213
  28.8 2.5 %collective-permute-start.8 = (bf16[64,7168]{1,0:T(8,128)(2,1)S(1)}, bf16[64,7168]{1,0:T(8,128)(2,1)S(1)}, u32[]{:S(2)}, u32[]{:S(2)}) collective-permute-start(bf16[64,7168]{1,0:T(8,128)(2,1)S(1)} %get-tuple-element.22), channel_id=1, source_target_pairs={{0,4},{4,0},{8,12},{12,8},{1,5},{5,1},{9,13},{13,9},{2,6},{6,2},{1... | collective-permute-start | bytes 2752520 | tf_op jit(solution)/shard_map/ppermute | solution.py:213
  31.6 6.1 %collective-permute-start.11 = (bf16[8,7168]{1,0:T(8,128)(2,1)S(1)}, bf16[8,7168]{1,0:T(8,128)(2,1)S(1)}, u32[]{:S(2)}, u32[]{:S(2)}) collective-permute-start(bf16[8,7168]{1,0:T(8,128)(2,1)S(1)} %get-tuple-element.25), channel_id=1, source_target_pairs={{0,8},{4,12},{8,0},{12,4},{1,9},{5,13},{9,1},{13,5},{2,10},{6,14},... | collective-permute-start | bytes 344072 | tf_op jit(solution)/shard_map/ppermute | solution.py:213
  32.3 7.0 %collective-permute-start.13 = (bf16[8,7168]{1,0:T(8,128)(2,1)S(1)}, bf16[8,7168]{1,0:T(8,128)(2,1)S(1)}, u32[]{:S(2)}, u32[]{:S(2)}) collective-permute-start(bf16[8,7168]{1,0:T(8,128)(2,1)S(1)} %get-tuple-element.26), channel_id=1, source_target_pairs={{0,8},{4,12},{8,0},{12,4},{1,9},{5,13},{9,1},{13,5},{2,10},{6,14},... | collective-permute-start | bytes 344072 | tf_op jit(solution)/shard_map/ppermute | solution.py:213
  33.7 9.0 %collective-permute-start.9 = (bf16[16,7168]{1,0:T(8,128)(2,1)S(1)}, bf16[16,7168]{1,0:T(8,128)(2,1)S(1)}, u32[]{:S(2)}, u32[]{:S(2)}) collective-permute-start(bf16[16,7168]{1,0:T(8,128)(2,1)S(1)} %slice.39), channel_id=1, source_target_pairs={{0,1},{1,0},{2,3},{3,2},{4,5},{5,4},{6,7},{7,6},{8,9},{9,8},{10,11... | collective-permute-start | bytes 688136 | tf_op jit(solution)/shard_map/ppermute | solution.py:213
  39.3 11.0 %collective-permute-start.12 = (bf16[8,7168]{1,0:T(8,128)(2,1)S(1)}, bf16[8,7168]{1,0:T(8,128)(2,1)S(1)}, u32[]{:S(2)}, u32[]{:S(2)}) collective-permute-start(bf16[8,7168]{1,0:T(8,128)(2,1)S(1)} %get-tuple-element.23), channel_id=1, source_target_pairs={{0,2},{1,3},{2,0},{3,1},{4,6},{5,7},{6,4},{7,5},{8,10},{9,11},{10,... | collective-permute-start | bytes 344072 | tf_op jit(solution)/shard_map/ppermute | solution.py:213
  41.2 9.1 %collective-permute-start.14 = (bf16[8,7168]{1,0:T(8,128)(2,1)S(1)}, bf16[8,7168]{1,0:T(8,128)(2,1)S(1)}, u32[]{:S(2)}, u32[]{:S(2)}) collective-permute-start(bf16[8,7168]{1,0:T(8,128)(2,1)S(1)} %get-tuple-element.24), channel_id=1, source_target_pairs={{0,3},{1,2},{2,1},{3,0},{4,7},{5,6},{6,5},{7,4},{8,11},{9,10},{10,... | collective-permute-start | bytes 344072 | tf_op jit(solution)/shard_map/ppermute | solution.py:213
  42.8 7.5 %collective-permute-start.10 = (bf16[8,7168]{1,0:T(8,128)(2,1)S(1)}, bf16[8,7168]{1,0:T(8,128)(2,1)S(1)}, u32[]{:S(2)}, u32[]{:S(2)}) collective-permute-start(bf16[8,7168]{1,0:T(8,128)(2,1)S(1)} %slice.41), channel_id=1, source_target_pairs={{0,8},{4,12},{8,0},{12,4},{1,9},{5,13},{9,1},{13,5},{2,10},{6,14},... | collective-permute-start | bytes 344072 | tf_op jit(solution)/shard_map/ppermute | solution.py:213

commit v5 on v4

--- a/solution.py
+++ b/solution.py
@@ -136,7 +136,7 @@
 
 def shared_middle(rows, up, ready):
     count, (width, _, hidden) = rows.shape[0], up.shape
-    steps = 7
+    steps = 14
     return pl.pallas_call(
         shared_up_kernel,
         in_specs=[
@@ -163,7 +163,7 @@
 def routed_kernel(pieces, half_ref, other_ref, flat_ref, down_ref, named_ref, shared_ref, keep_ref, send_ref, sums):
     depth, hidden = flat_ref.shape[0], flat_ref.shape[1] // 2
     rows, width = keep_ref.shape
-    steps = 7
+    steps = 14
     block, piece = depth // steps, width // steps
     for i in range(steps):
         at = slice(i * block, (i + 1) * block)
@@ -218,12 +218,15 @@
     return jnp.concatenate([rows] + parts, axis=0)
 
 
-def chip_sum(pair, experts):
+def chip_sum(pair, experts, earlier=None):
     count = pair.shape[0] * CORES // experts
     total = pair[:count].astype(jnp.float32)
     for chip in range(CORES, experts, CORES):
         at = chip // CORES * count
-        total = total + exchange(pair[at:at + count], "ep", chip).astype(jnp.float32)
+        other = exchange(pair[at:at + count], "ep", chip)
+        if earlier is not None:
+            other = after(other, earlier)
+        total = total + other.astype(jnp.float32)
     return total
 
 
@@ -239,7 +242,7 @@
     routed_rows = owner_rows(tokens, routes, gates, named, lanes)
     token_half = half_ep(after(tokens, routed_rows), experts)
 
-    order = list(range(2, subs))
+    order = list(range(subs - 1, 1, -1))
     far = jnp.concatenate([exchange(routed_rows, "sub", k) for k in order], axis=0)
     own_half = half_ep(routed_rows, experts)
     near_half = exchange(own_half, "sub", 1)
@@ -261,20 +264,20 @@
         pieces.append((first, 2 * split))
         pieces += [
             (first + 2 * split + (chip * len(order) + at) * count, count)
-            for at in range(len(order)) for chip in range(chips)
+            for at in reversed(range(len(order))) for chip in range(chips)
         ]
     shared_part = jnp.dot(middle, shared_weights, preferred_element_type=jnp.float32)
     keep, send = routed_parts(half, other, expert_weights, down_weights, named, shared_part, pieces)
     pair = (keep.astype(jnp.float32) + exchange(send, "ep", 1).astype(jnp.float32)).astype(bf)
 
-    sums = [
-        chip_sum(pair[at:at + split], experts).astype(bf)
-        for at in range(2 * split, pair.shape[0], split)
-    ]
+    sums = []
+    for at in range(2 * split, pair.shape[0], split):
+        earlier = sums[-1] if sums else None
+        sums.append(chip_sum(pair[at:at + split], experts, earlier).astype(bf))
     near = exchange(pair[split:2 * split], "sub", 1)
     near = (pair[:split].astype(jnp.float32) + near.astype(jnp.float32)).astype(bf)
     total = chip_sum(near, experts)
-    for rows, k in zip(sums, order):
+    for rows, k in zip(sums, order[::-1]):
         total = total + exchange(rows, "sub", k).astype(jnp.float32)
     return total.astype(bf)
 

time: 51.2 us -> 49.3 us (0.963)
  waiting for transfers between devices: 15 us -> 11.1 us
  starting transfers between devices: 17.3 us -> 19.7 us
    ppermute x15, waiting for transfers between devices: 15 us -> 11.1 us  [exchange(): return lax.ppermute(rows, axis, [(i, i ^ flip) for i in range(size)])]
    ppermute x15, starting transfers between devices: 17.3 us -> 19.7 us  [exchange(): return lax.ppermute(rows, axis, [(i, i ^ flip) for i in range(size)])]
  transfers between devices with their start and end apart: 15 -> 15, of which waited for: 6 -> 4; matrix products, arithmetic and copies ran while one was open for 3% -> 4% of each run, Pallas kernels for 25% -> 26%
where the time goes in v5:
time: 49.3 us; the launch traced here: 49.1 us
  starting transfers between devices  19.7 us (40%)
  Pallas kernels  15.5 us (31%)
  waiting for transfers between devices  11.1 us (23%)
  matrix products  1.4 us (3%)
  other arithmetic  1.16 us (2%)
    ppermute x15, starting transfers between devices, exchange(): return lax.ppermute(rows, axis, [(i, i ^ flip) for i in range(size)])  19.7 us
    ppermute x15, waiting for transfers between devices, exchange(): return lax.ppermute(rows, axis, [(i, i ^ flip) for i in range(size)])  11.1 us
    pallas_call x1, Pallas kernels, held_weights(): pl.pallas_call(weights_kernel, in_specs=[pl.BlockSpec(memory_space=pltpu....  6.39 us
    pallas_call x1, Pallas kernels, shared_middle(): pl.pallas_call(shared_up_kernel, in_specs=[pl.BlockSpec(memory_space=pltp...  6.27 us
    pallas_call x1, Pallas kernels, routed_parts(): pl.pallas_call(functools.partial(routed_kernel, pieces), in_specs=[pl.Blo...  1.78 us
    dot_general x1, matrix products, per_device(): jnp.dot(middle, shared_weights, preferred_element_type=jnp.float32)  1.4 us
    pallas_call x1, Pallas kernels, owner_rows(): pl.pallas_call(owner_kernel, in_specs=[pl.BlockSpec(memory_space=pltpu.HB...  1.09 us
  transfers between devices with their start and end apart: 15, of which 4 were waited for; matrix products, arithmetic and copies ran while one was open for 4% of the time, Pallas kernels for 26%

profile of v5, /device:TPU:0, one launch (start us, length us, event | category | flops | bytes accessed | tf_op | source)
XLA Modules:
  0.0 49.1 jit_solution(13275421749534203852)
XLA Ops:
  0.0 1.1 %shard_map.73.ready_ref = bf16[8,7296]{1,0:T(8,128)(2,1)S(1)} custom-call(bf16[8,7168]{1,0:T(8,128)(2,1)} %tokens_ref.1, s32[2,8]{1,0:T(2,128)} %bitcast.8, bf16[2,8]{1,0:T(2,128)(2,1)} %bitcast.9, f32[1,128]{1,0:T(1,128)S(1)} %compare_convert_fusion.ready_ref.named_ref), custom_call_target="tpu_custom_call" | custom-call | tf_op jit(solution)/shard_map/pallas_call | solution.py:56
  1.1 4.1 %collective-permute-start.3 = (bf16[8,7296]{1,0:T(8,128)(2,1)S(1)}, bf16[8,7296]{1,0:T(8,128)(2,1)S(1)}, u32[]{:S(2)}, u32[]{:S(2)}) collective-permute-start(bf16[8,7296]{1,0:T(8,128)(2,1)S(1)} %shard_map.73.ready_ref), channel_id=1, source_target_pairs={{0,2},{1,3},{2,0},{3,1},{4,6},{5,7},{6,4},{7,5},{8,10},{9,11},{10,... | collective-permute-start | bytes 350216 | tf_op jit(solution)/shard_map/ppermute | solution.py:213
  5.2 1.3 %collective-permute-start.2 = (bf16[8,7296]{1,0:T(8,128)(2,1)S(1)}, bf16[8,7296]{1,0:T(8,128)(2,1)S(1)}, u32[]{:S(2)}, u32[]{:S(2)}) collective-permute-start(bf16[8,7296]{1,0:T(8,128)(2,1)S(1)} %shard_map.73.ready_ref), channel_id=1, source_target_pairs={{0,3},{1,2},{2,1},{3,0},{4,7},{5,6},{6,5},{7,4},{8,11},{9,10},{10,... | collective-permute-start | bytes 350216 | tf_op jit(solution)/shard_map/ppermute | solution.py:213
  6.6 1.5 %collective-permute-start = (bf16[8,7296]{1,0:T(8,128)(2,1)S(1)}, bf16[8,7296]{1,0:T(8,128)(2,1)S(1)}, u32[]{:S(2)}, u32[]{:S(2)}) collective-permute-start(bf16[8,7296]{1,0:T(8,128)(2,1)S(1)} %shard_map.73.ready_ref), channel_id=1, source_target_pairs={{0,8},{4,12},{8,0},{12,4},{1,9},{5,13},{9,1},{13,5},{2,10},{6,14},... | collective-permute-start | bytes 350216 | tf_op jit(solution)/shard_map/ppermute | solution.py:213
  8.1 0.5 %collective-permute-start.5 = (bf16[8,7168]{1,0:T(8,128)(2,1)}, bf16[8,7168]{1,0:T(8,128)(2,1)S(1)}, u32[]{:S(2)}, u32[]{:S(2)}) collective-permute-start(bf16[8,7168]{1,0:T(8,128)(2,1)} %tokens_ref.1), channel_id=1, source_target_pairs={{0,8},{4,12},{8,0},{12,4},{1,9},{5,13},{9,1},{13,5},{2,10},{6,14},... | collective-permute-start | bytes 344072 | tf_op jit(solution)/shard_map/ppermute | solution.py:213
  8.6 6.4 %shard_map.74 = (bf16[7168,512]{1,0:T(8,128)(2,1)S(1)}, bf16[256,7168]{1,0:T(8,128)(2,1)S(1)}, bf16[512,7168]{1,0:T(8,128)(2,1)S(1)}) custom-call(bf16[7168,2,256]{2,1,0:T(2,128)(2,1)} %bitcast.6, bf16[256,7168]{1,0:T(8,128)(2,1)} %bitcast.7, bf16[512,7168]{1,0:T(8,128)(2,1)} %shared_ref.1, bf16[8,7296]{1,0:T(8,128)(2,1)S(1)} %shard_map.73.ready_ref), custom_call_target="tpu_custom_call" | custom-call | bytes 14680064 | tf_op jit(solution)/shard_map/pallas_call | solution.py:98
  15.2 0.3 collective-permute-start.1
  15.5 1.6 %collective-permute-start.4 = (bf16[16,7296]{1,0:T(8,128)(2,1)S(1)}, bf16[16,7296]{1,0:T(8,128)(2,1)S(1)}, u32[]{:S(2)}, u32[]{:S(2)}) collective-permute-start(bf16[16,7296]{1,0:T(8,128)(2,1)S(1)} %pad_maximum_fusion.2.ready_ref), channel_id=1, source_target_pairs={{0,8},{4,12},{8,0},{12,4},{1,9},{5,13},{9,1},{13,5},{2,10},{6,14},... | collective-permute-start | bytes 700424 | tf_op jit(solution)/shard_map/ppermute | solution.py:213
  17.1 6.3 %shard_map.75 = bf16[32,512]{1,0:T(8,128)(2,1)S(1)} custom-call(bf16[32,7168]{1,0:T(8,128)(2,1)S(1)} %pad_maximum_fusion.rows_ref, bf16[7168,2,512]{2,1,0:T(2,128)(2,1)} %up_ref.1, bf16[16,7296]{1,0:T(8,128)(2,1)S(1)} %pad_maximum_fusion.2.ready_ref), custom_call_target="tpu_custom_call" | custom-call | flops 469762048 | bytes 14680064 | tf_op jit(solution)/shard_map/pallas_call | solution.py:140
  23.6 1.4 %fusion.1.shared_ref = f32[32,7168]{1,0:T(8,128)S(1)} fusion(bf16[32,512]{1,0:T(8,128)(2,1)S(1)} %shard_map.75, bf16[512,7168]{1,0:T(8,128)(2,1)S(1)} %get-tuple-element.21), kind=kOutput, calls=%fused_computation.16 | convolution fusion | flops 234881024 | bytes 8290304 | tf_op jit(solution)/shard_map/dot_general | solution.py:269
  25.0 1.1 %collective-permute-done.7.other_ref = bf16[64,7296]{1,0:T(8,128)(2,1)S(1)} collective-permute-done((bf16[64,7296]{1,0:T(8,128)(2,1)S(1)}, bf16[64,7296]{1,0:T(8,128)(2,1)S(1)}, u32[]{:S(2)}, u32[]{:S(2)}) %collective-permute-start.7) | collective-permute-done | bytes 933920 | tf_op jit(solution)/shard_map/ppermute | solution.py:213
  26.1 1.8 %shard_map.76 = (bf16[64,7168]{1,0:T(8,128)(2,1)S(1)}, bf16[64,7168]{1,0:T(8,128)(2,1)S(1)}) custom-call(bf16[64,7296]{1,0:T(8,128)(2,1)S(1)} %constant_dynamic-update-slice_fusion.half_ref, bf16[64,7296]{1,0:T(8,128)(2,1)S(1)} %collective-permute-done.7.other_ref, bf16[7168,512]{1,0:T(8,128)(2,1)S(1)} %get-tuple-element.19.flat_ref, ...), custom_call_target="tpu_custom_call" | custom-call | flops 1409286144 | bytes 11010048 | tf_op jit(solution)/shard_map/pallas_call | solution.py:192
  27.9 0.2 collective-permute-start.8
  28.1 2.3 %collective-permute-done.8 = bf16[64,7168]{1,0:T(8,128)(2,1)S(1)} collective-permute-done((bf16[64,7168]{1,0:T(8,128)(2,1)S(1)}, bf16[64,7168]{1,0:T(8,128)(2,1)S(1)}, u32[]{:S(2)}, u32[]{:S(2)}) %collective-permute-start.8) | collective-permute-done | bytes 917536 | tf_op jit(solution)/shard_map/ppermute | solution.py:213
  30.4 0.2 add_convert_fusion
  30.6 1.5 %collective-permute-start.11 = (bf16[8,7168]{1,0:T(8,128)(2,1)S(1)}, bf16[8,7168]{1,0:T(8,128)(2,1)S(1)}, u32[]{:S(2)}, u32[]{:S(2)}) collective-permute-start(bf16[8,7168]{1,0:T(8,128)(2,1)S(1)} %get-tuple-element.25), channel_id=1, source_target_pairs={{0,8},{4,12},{8,0},{12,4},{1,9},{5,13},{9,1},{13,5},{2,10},{6,14},... | collective-permute-start | bytes 344072 | tf_op jit(solution)/shard_map/ppermute | solution.py:213
  32.2 0.6 %collective-permute-start.13 = (bf16[8,7168]{1,0:T(8,128)(2,1)S(1)}, bf16[8,7168]{1,0:T(8,128)(2,1)S(1)}, u32[]{:S(2)}, u32[]{:S(2)}) collective-permute-start(bf16[8,7168]{1,0:T(8,128)(2,1)S(1)} %get-tuple-element.26), channel_id=1, source_target_pairs={{0,8},{4,12},{8,0},{12,4},{1,9},{5,13},{9,1},{13,5},{2,10},{6,14},... | collective-permute-start | bytes 344072 | tf_op jit(solution)/shard_map/ppermute | solution.py:213
  32.8 1.8 %collective-permute-start.9 = (bf16[16,7168]{1,0:T(8,128)(2,1)S(1)}, bf16[16,7168]{1,0:T(8,128)(2,1)S(1)}, u32[]{:S(2)}, u32[]{:S(2)}) collective-permute-start(bf16[16,7168]{1,0:T(8,128)(2,1)S(1)} %slice.39), channel_id=1, source_target_pairs={{0,1},{1,0},{2,3},{3,2},{4,5},{5,4},{6,7},{7,6},{8,9},{9,8},{10,11... | collective-permute-start | bytes 688136 | tf_op jit(solution)/shard_map/ppermute | solution.py:213
  34.6 2.1 %collective-permute-done.11 = bf16[8,7168]{1,0:T(8,128)(2,1)S(1)} collective-permute-done((bf16[8,7168]{1,0:T(8,128)(2,1)S(1)}, bf16[8,7168]{1,0:T(8,128)(2,1)S(1)}, u32[]{:S(2)}, u32[]{:S(2)}) %collective-permute-start.11) | collective-permute-done | bytes 114720 | tf_op jit(solution)/shard_map/ppermute | solution.py:213
  36.7 3.1 %collective-permute-start.12 = (bf16[8,7168]{1,0:T(8,128)(2,1)S(1)}, bf16[8,7168]{1,0:T(8,128)(2,1)S(1)}, u32[]{:S(2)}, u32[]{:S(2)}) collective-permute-start(bf16[8,7168]{1,0:T(8,128)(2,1)S(1)} %add_convert_fusion.4), channel_id=1, source_target_pairs={{0,2},{1,3},{2,0},{3,1},{4,6},{5,7},{6,4},{7,5},{8,10},{9,11},{10,... | collective-permute-start | bytes 344072 | tf_op jit(solution)/shard_map/ppermute | solution.py:213
  39.9 1.5 %collective-permute-start.14 = (bf16[8,7168]{1,0:T(8,128)(2,1)S(1)}, bf16[8,7168]{1,0:T(8,128)(2,1)S(1)}, u32[]{:S(2)}, u32[]{:S(2)}) collective-permute-start(bf16[8,7168]{1,0:T(8,128)(2,1)S(1)} %add_convert_fusion.3), channel_id=1, source_target_pairs={{0,3},{1,2},{2,1},{3,0},{4,7},{5,6},{6,5},{7,4},{8,11},{9,10},{10,... | collective-permute-start | bytes 344072 | tf_op jit(solution)/shard_map/ppermute | solution.py:213
  41.5 1.5 %collective-permute-start.10 = (bf16[8,7168]{1,0:T(8,128)(2,1)S(1)}, bf16[8,7168]{1,0:T(8,128)(2,1)S(1)}, u32[]{:S(2)}, u32[]{:S(2)}) collective-permute-start(bf16[8,7168]{1,0:T(8,128)(2,1)S(1)} %slice.41), channel_id=1, source_target_pairs={{0,8},{4,12},{8,0},{12,4},{1,9},{5,13},{9,1},{13,5},{2,10},{6,14},... | collective-permute-start | bytes 344072 | tf_op jit(solution)/shard_map/ppermute | solution.py:213
  42.9 5.5 %collective-permute-done.12 = bf16[8,7168]{1,0:T(8,128)(2,1)S(1)} collective-permute-done((bf16[8,7168]{1,0:T(8,128)(2,1)S(1)}, bf16[8,7168]{1,0:T(8,128)(2,1)S(1)}, u32[]{:S(2)}, u32[]{:S(2)}) %collective-permute-start.12) | collective-permute-done | bytes 114720 | tf_op jit(solution)/shard_map/ppermute | solution.py:213
  48.4 0.7 %add_convert_fusion.2 = bf16[8,7168]{1,0:T(8,128)(2,1)} fusion(bf16[8,7168]{1,0:T(8,128)(2,1)S(1)} %collective-permute-done.14, bf16[8,7168]{1,0:T(8,128)(2,1)S(1)} %collective-permute-done.12, bf16[8,7168]{1,0:T(8,128)(2,1)S(1)} %collective-permute-done.10, bf16[16,7168]{1,0:T(8,128)(2,1)S(1)} %add_convert_fusion.1), kind=kLoop, calls=%fused_computation.6 | loop fusion | flops 458752 | bytes 573440 | tf_op jit(solution)/shard_map/convert_element_type | solution.py:282
  (31 shorter events, 0.6 us)
Async XLA Ops:
  1.1 14.4 %collective-permute-start.3 = (bf16[8,7296]{1,0:T(8,128)(2,1)S(1)}, bf16[8,7296]{1,0:T(8,128)(2,1)S(1)}, u32[]{:S(2)}, u32[]{:S(2)}) collective-permute-start(bf16[8,7296]{1,0:T(8,128)(2,1)S(1)} %shard_map.73.ready_ref), channel_id=1, source_target_pairs={{0,2},{1,3},{2,0},{3,1},{4,6},{5,7},{6,4},{7,5},{8,10},{9,11},{10,... | collective-permute-start | bytes 350216 | tf_op jit(solution)/shard_map/ppermute | solution.py:213
  5.2 10.3 %collective-permute-start.2 = (bf16[8,7296]{1,0:T(8,128)(2,1)S(1)}, bf16[8,7296]{1,0:T(8,128)(2,1)S(1)}, u32[]{:S(2)}, u32[]{:S(2)}) collective-permute-start(bf16[8,7296]{1,0:T(8,128)(2,1)S(1)} %shard_map.73.ready_ref), channel_id=1, source_target_pairs={{0,3},{1,2},{2,1},{3,0},{4,7},{5,6},{6,5},{7,4},{8,11},{9,10},{10,... | collective-permute-start | bytes 350216 | tf_op jit(solution)/shard_map/ppermute | solution.py:213
  6.6 8.6 %collective-permute-start = (bf16[8,7296]{1,0:T(8,128)(2,1)S(1)}, bf16[8,7296]{1,0:T(8,128)(2,1)S(1)}, u32[]{:S(2)}, u32[]{:S(2)}) collective-permute-start(bf16[8,7296]{1,0:T(8,128)(2,1)S(1)} %shard_map.73.ready_ref), channel_id=1, source_target_pairs={{0,8},{4,12},{8,0},{12,4},{1,9},{5,13},{9,1},{13,5},{2,10},{6,14},... | collective-permute-start | bytes 350216 | tf_op jit(solution)/shard_map/ppermute | solution.py:213
  8.1 6.9 %collective-permute-start.5 = (bf16[8,7168]{1,0:T(8,128)(2,1)}, bf16[8,7168]{1,0:T(8,128)(2,1)S(1)}, u32[]{:S(2)}, u32[]{:S(2)}) collective-permute-start(bf16[8,7168]{1,0:T(8,128)(2,1)} %tokens_ref.1), channel_id=1, source_target_pairs={{0,8},{4,12},{8,0},{12,4},{1,9},{5,13},{9,1},{13,5},{2,10},{6,14},... | collective-permute-start | bytes 344072 | tf_op jit(solution)/shard_map/ppermute | solution.py:213
  8.6 6.4 %copy-start = (bf16[8,7168]{1,0:T(8,128)(2,1)S(1)}, bf16[8,7168]{1,0:T(8,128)(2,1)}, u32[]{:S(2)}) copy-start(bf16[8,7168]{1,0:T(8,128)(2,1)} %tokens_ref.1) | copy-start | bytes 344068
  15.0 2.0 %collective-permute-start.6 = (bf16[16,7168]{1,0:T(8,128)(2,1)S(1)}, bf16[16,7168]{1,0:T(8,128)(2,1)S(1)}, u32[]{:S(2)}, u32[]{:S(2)}) collective-permute-start(bf16[16,7168]{1,0:T(8,128)(2,1)S(1)} %pad_maximum_fusion.3), channel_id=1, source_target_pairs={{0,4},{4,0},{8,12},{12,8},{1,5},{5,1},{9,13},{13,9},{2,6},{6,2},{1... | collective-permute-start | bytes 688136 | tf_op jit(solution)/shard_map/ppermute | solution.py:213
  15.2 8.3 %collective-permute-start.1 = (bf16[16,7296]{1,0:T(8,128)(2,1)S(1)}, bf16[16,7296]{1,0:T(8,128)(2,1)S(1)}, u32[]{:S(2)}, u32[]{:S(2)}) collective-permute-start(bf16[16,7296]{1,0:T(8,128)(2,1)S(1)} %pad_maximum_fusion.1), channel_id=1, source_target_pairs={{0,1},{1,0},{2,3},{3,2},{4,5},{5,4},{6,7},{7,6},{8,9},{9,8},{10,11... | collective-permute-start | bytes 700424 | tf_op jit(solution)/shard_map/ppermute | solution.py:213
  15.5 8.0 %collective-permute-start.4 = (bf16[16,7296]{1,0:T(8,128)(2,1)S(1)}, bf16[16,7296]{1,0:T(8,128)(2,1)S(1)}, u32[]{:S(2)}, u32[]{:S(2)}) collective-permute-start(bf16[16,7296]{1,0:T(8,128)(2,1)S(1)} %pad_maximum_fusion.2.ready_ref), channel_id=1, source_target_pairs={{0,8},{4,12},{8,0},{12,4},{1,9},{5,13},{9,1},{13,5},{2,10},{6,14},... | collective-permute-start | bytes 700424 | tf_op jit(solution)/shard_map/ppermute | solution.py:213
  23.5 2.6 %collective-permute-start.7 = (bf16[64,7296]{1,0:T(8,128)(2,1)S(1)}, bf16[64,7296]{1,0:T(8,128)(2,1)S(1)}, u32[]{:S(2)}, u32[]{:S(2)}) collective-permute-start(bf16[64,7296]{1,0:T(8,128)(2,1)S(1)} %constant_dynamic-update-slice_fusion.half_ref), channel_id=1, source_target_pairs={{0,4},{4,0},{8,12},{12,8},{1,5},{5,1},{9,13},{13,9},{2,6},{6,2},{1... | collective-permute-start | bytes 2801672 | tf_op jit(solution)/shard_map/ppermute | solution.py:213
  27.9 2.5 %collective-permute-start.8 = (bf16[64,7168]{1,0:T(8,128)(2,1)S(1)}, bf16[64,7168]{1,0:T(8,128)(2,1)S(1)}, u32[]{:S(2)}, u32[]{:S(2)}) collective-permute-start(bf16[64,7168]{1,0:T(8,128)(2,1)S(1)} %get-tuple-element.23), channel_id=1, source_target_pairs={{0,4},{4,0},{8,12},{12,8},{1,5},{5,1},{9,13},{13,9},{2,6},{6,2},{1... | collective-permute-start | bytes 2752520 | tf_op jit(solution)/shard_map/ppermute | solution.py:213
  30.6 6.1 %collective-permute-start.11 = (bf16[8,7168]{1,0:T(8,128)(2,1)S(1)}, bf16[8,7168]{1,0:T(8,128)(2,1)S(1)}, u32[]{:S(2)}, u32[]{:S(2)}) collective-permute-start(bf16[8,7168]{1,0:T(8,128)(2,1)S(1)} %get-tuple-element.25), channel_id=1, source_target_pairs={{0,8},{4,12},{8,0},{12,4},{1,9},{5,13},{9,1},{13,5},{2,10},{6,14},... | collective-permute-start | bytes 344072 | tf_op jit(solution)/shard_map/ppermute | solution.py:213
  32.2 7.7 %collective-permute-start.13 = (bf16[8,7168]{1,0:T(8,128)(2,1)S(1)}, bf16[8,7168]{1,0:T(8,128)(2,1)S(1)}, u32[]{:S(2)}, u32[]{:S(2)}) collective-permute-start(bf16[8,7168]{1,0:T(8,128)(2,1)S(1)} %get-tuple-element.26), channel_id=1, source_target_pairs={{0,8},{4,12},{8,0},{12,4},{1,9},{5,13},{9,1},{13,5},{2,10},{6,14},... | collective-permute-start | bytes 344072 | tf_op jit(solution)/shard_map/ppermute | solution.py:213
  32.8 8.6 %collective-permute-start.9 = (bf16[16,7168]{1,0:T(8,128)(2,1)S(1)}, bf16[16,7168]{1,0:T(8,128)(2,1)S(1)}, u32[]{:S(2)}, u32[]{:S(2)}) collective-permute-start(bf16[16,7168]{1,0:T(8,128)(2,1)S(1)} %slice.39), channel_id=1, source_target_pairs={{0,1},{1,0},{2,3},{3,2},{4,5},{5,4},{6,7},{7,6},{8,9},{9,8},{10,11... | collective-permute-start | bytes 688136 | tf_op jit(solution)/shard_map/ppermute | solution.py:213
  36.7 11.7 %collective-permute-start.12 = (bf16[8,7168]{1,0:T(8,128)(2,1)S(1)}, bf16[8,7168]{1,0:T(8,128)(2,1)S(1)}, u32[]{:S(2)}, u32[]{:S(2)}) collective-permute-start(bf16[8,7168]{1,0:T(8,128)(2,1)S(1)} %add_convert_fusion.4), channel_id=1, source_target_pairs={{0,2},{1,3},{2,0},{3,1},{4,6},{5,7},{6,4},{7,5},{8,10},{9,11},{10,... | collective-permute-start | bytes 344072 | tf_op jit(solution)/shard_map/ppermute | solution.py:213
  39.9 8.5 %collective-permute-start.14 = (bf16[8,7168]{1,0:T(8,128)(2,1)S(1)}, bf16[8,7168]{1,0:T(8,128)(2,1)S(1)}, u32[]{:S(2)}, u32[]{:S(2)}) collective-permute-start(bf16[8,7168]{1,0:T(8,128)(2,1)S(1)} %add_convert_fusion.3), channel_id=1, source_target_pairs={{0,3},{1,2},{2,1},{3,0},{4,7},{5,6},{6,5},{7,4},{8,11},{9,10},{10,... | collective-permute-start | bytes 344072 | tf_op jit(solution)/shard_map/ppermute | solution.py:213
  41.5 7.0 %collective-permute-start.10 = (bf16[8,7168]{1,0:T(8,128)(2,1)S(1)}, bf16[8,7168]{1,0:T(8,128)(2,1)S(1)}, u32[]{:S(2)}, u32[]{:S(2)}) collective-permute-start(bf16[8,7168]{1,0:T(8,128)(2,1)S(1)} %slice.41), channel_id=1, source_target_pairs={{0,8},{4,12},{8,0},{12,4},{1,9},{5,13},{9,1},{13,5},{2,10},{6,14},... | collective-permute-start | bytes 344072 | tf_op jit(solution)/shard_map/ppermute | solution.py:213

commit v6 on v5

--- a/solution.py
+++ b/solution.py
@@ -11,6 +11,9 @@
 LANES = 128
 CORES = 2
 VMEM_LIMIT = 30 << 20
+UP_BLOCKS = 14
+EARLY_BLOCKS = 5
+SPLIT_ROWS = 64
 
 
 def owner_kernel(tokens_ref, routes_ref, gates_ref, ready_ref, routed_ref, tokens, routes, gates, sems):
@@ -64,68 +67,68 @@
     )(*(pltpu.with_memory_space_constraint(x, pltpu.HBM) for x in operands), ready)
 
 
-def weights_kernel(pair_ref, down_ref, shared_ref, ready_ref, flat_ref, down_out, shared_out, raw, sems):
+def split_kernel(pair_ref, up_ref, ready_ref, flat_ref, early_ref, raw, sems):
     del ready_ref
-    steps = sems.shape[0] - 2
+    steps = sems.shape[0] - 1
     block, hidden = raw.shape[0] // steps, pair_ref.shape[2]
 
     def fetch(i):
         rows = pl.ds(i * block, block)
         return pltpu.make_async_copy(pair_ref.at[rows], raw.at[rows], sems.at[i])
 
-    downs = [
-        pltpu.make_async_copy(down_ref, down_out, sems.at[steps]),
-        pltpu.make_async_copy(shared_ref, shared_out, sems.at[steps + 1]),
-    ]
+    early = pltpu.make_async_copy(up_ref.at[pl.ds(0, early_ref.shape[0])], early_ref, sems.at[steps])
     for i in range(steps):
         fetch(i).start()
-    for copy in downs:
-        copy.start()
+    early.start()
     for i in range(steps):
         fetch(i).wait()
-        at = slice(i * block, (i + 1) * block)
-        both = jnp.swapaxes(raw[at], 0, 1)
-        flat_ref[at, :hidden] = both[0]
-        flat_ref[at, hidden:] = both[1]
-    for copy in downs:
-        copy.wait()
-
-
-def held_weights(pairs, down, shared, ready):
+        for first in range(i * block, (i + 1) * block, SPLIT_ROWS):
+            at = slice(first, first + SPLIT_ROWS)
+            both = jnp.swapaxes(raw[at], 0, 1)
+            flat_ref[at, :hidden] = both[0]
+            flat_ref[at, hidden:] = both[1]
+    early.wait()
+
+
+def flat_pairs(pairs, up, ready):
     depth, _, hidden = pairs.shape
-    steps = 4
-    operands = [pltpu.with_memory_space_constraint(x, pltpu.HBM) for x in (pairs, down, shared)]
+    steps = 7
+    early = depth // UP_BLOCKS * EARLY_BLOCKS
     return pl.pallas_call(
-        weights_kernel,
-        in_specs=[pl.BlockSpec(memory_space=pltpu.HBM)] * 3 + [pl.BlockSpec(memory_space=pl.ANY)],
-        out_specs=[pl.BlockSpec(memory_space=pltpu.VMEM)] * 3,
+        split_kernel,
+        in_specs=[pl.BlockSpec(memory_space=pltpu.HBM)] * 2 + [pl.BlockSpec(memory_space=pl.ANY)],
+        out_specs=[pl.BlockSpec(memory_space=pltpu.VMEM)] * 2,
         out_shape=(
             jax.ShapeDtypeStruct((depth, 2 * hidden), pairs.dtype),
-            jax.ShapeDtypeStruct(down.shape, down.dtype),
-            jax.ShapeDtypeStruct(shared.shape, shared.dtype),
-        ),
-        scratch_shapes=[pltpu.VMEM(pairs.shape, pairs.dtype), pltpu.SemaphoreType.DMA((steps + 2,))],
+            jax.ShapeDtypeStruct((early, *up.shape[1:]), up.dtype),
+        ),
+        scratch_shapes=[pltpu.VMEM(pairs.shape, pairs.dtype), pltpu.SemaphoreType.DMA((steps + 1,))],
         compiler_params=pltpu.CompilerParams(vmem_limit_bytes=VMEM_LIMIT),
         cost_estimate=pl.CostEstimate(
             flops=0, bytes_accessed=8 * depth * hidden, transcendentals=0
         ),
-    )(*operands, ready)
-
-
-def shared_up_kernel(rows_ref, up_ref, ready_ref, middle_ref, up, sums, sems):
+    )(*(pltpu.with_memory_space_constraint(x, pltpu.HBM) for x in (pairs, up)), ready)
+
+
+def shared_up_kernel(rows_ref, early_ref, up_ref, ready_ref, middle_ref, up, sums, sems):
     del ready_ref
-    steps = sems.shape[0]
-    block = up.shape[0] // steps
+    late, early = sems.shape[0], early_ref.shape[0]
+    block = up.shape[0] // late
 
     def fetch(i):
         at = pl.ds(i * block, block)
-        return pltpu.make_async_copy(up_ref.at[at], up.at[at], sems.at[i])
-
-    for i in range(steps):
+        return pltpu.make_async_copy(up_ref.at[pl.ds(early + i * block, block)], up.at[at], sems.at[i])
+
+    for i in range(late):
         fetch(i).start()
-    for i in range(steps):
-        fetch(i).wait()
-        both = jnp.swapaxes(up[i * block:(i + 1) * block], 0, 1)
+    for i in range(early // block + late):
+        at = i * block - early
+        if at >= 0:
+            fetch(at // block).wait()
+            pairs = up[at:at + block]
+        else:
+            pairs = early_ref[i * block:(i + 1) * block]
+        both = jnp.swapaxes(pairs, 0, 1)
         left = rows_ref[:, i * block:(i + 1) * block]
         for half in range(2):
             term = jnp.dot(left, both[half], preferred_element_type=jnp.float32)
@@ -134,12 +137,13 @@
     middle_ref[...] = (gate / (1.0 + jnp.exp(-gate)) * lift).astype(jnp.bfloat16)
 
 
-def shared_middle(rows, up, ready):
+def shared_middle(rows, early, up, ready):
     count, (width, _, hidden) = rows.shape[0], up.shape
-    steps = 14
+    late = width - early.shape[0]
     return pl.pallas_call(
         shared_up_kernel,
         in_specs=[
+            pl.BlockSpec(memory_space=pltpu.VMEM),
             pl.BlockSpec(memory_space=pltpu.VMEM),
             pl.BlockSpec(memory_space=pltpu.HBM),
             pl.BlockSpec(memory_space=pl.ANY),
@@ -147,9 +151,9 @@
         out_specs=pl.BlockSpec(memory_space=pltpu.VMEM),
         out_shape=jax.ShapeDtypeStruct((count, hidden), jnp.bfloat16),
         scratch_shapes=[
-            pltpu.VMEM(up.shape, up.dtype),
+            pltpu.VMEM((late, *up.shape[1:]), up.dtype),
             pltpu.VMEM((2, count, hidden), jnp.float32),
-            pltpu.SemaphoreType.DMA((steps,)),
+            pltpu.SemaphoreType.DMA((UP_BLOCKS - EARLY_BLOCKS,)),
         ],
         compiler_params=pltpu.CompilerParams(vmem_limit_bytes=20 << 20),
         cost_estimate=pl.CostEstimate(
@@ -157,51 +161,56 @@
             bytes_accessed=4 * hidden * width,
             transcendentals=0,
         ),
-    )(rows, pltpu.with_memory_space_constraint(up, pltpu.HBM), ready)
-
-
-def routed_kernel(pieces, half_ref, other_ref, flat_ref, down_ref, named_ref, shared_ref, keep_ref, send_ref, sums):
+    )(rows, early, pltpu.with_memory_space_constraint(up, pltpu.HBM), ready)
+
+
+def routed_kernel(pieces, *refs):
+    rows_refs = refs[:2 * CORES]
+    flat_ref, down_ref, named_ref, shared_ref, keep_ref, near_ref, far_ref, sums = refs[2 * CORES:]
     depth, hidden = flat_ref.shape[0], flat_ref.shape[1] // 2
     rows, width = keep_ref.shape
     steps = 14
     block, piece = depth // steps, width // steps
     for i in range(steps):
         at = slice(i * block, (i + 1) * block)
-        left = jnp.concatenate([half_ref[:, at], other_ref[:, at]], axis=0)
+        left = jnp.concatenate([ref[:, at] for ref in rows_refs], axis=0)
         term = jnp.dot(left, flat_ref[at, :], preferred_element_type=jnp.float32)
         sums[...] = term if i == 0 else sums[...] + term
-    weight = jnp.concatenate([half_ref[:, depth:], other_ref[:, depth:]], axis=0)
+    weight = jnp.concatenate([ref[:, depth:] for ref in rows_refs], axis=0)
     named = weight.astype(jnp.float32) * named_ref[...]
     weight = jnp.sum(named, axis=1, keepdims=True)
     gate, lift = sums[:, :hidden], sums[:, hidden:]
     sums[:, :hidden] = gate / (1.0 + jnp.exp(-gate)) * lift * weight
     ordered = [sums[first:first + count, :hidden] for first, count in pieces]
     middle = jnp.concatenate(ordered, axis=0).astype(jnp.bfloat16)
-    own = shared_ref.shape[0] // CORES
+    own, near = shared_ref.shape[0] // CORES, near_ref.shape[0]
     for i in range(steps):
         at = slice(i * piece, (i + 1) * piece)
         term = jnp.dot(middle, down_ref[:, at], preferred_element_type=jnp.float32)
-        for core, out in enumerate((keep_ref, send_ref)):
-            first = core * rows
-            near = term[first:first + own] + shared_ref[core * own:(core + 1) * own, at]
-            out[:, at] = jnp.concatenate([near, term[first + own:first + rows]], axis=0).astype(jnp.bfloat16)
-
-
-def routed_parts(half, other, flat, down, named, shared, pieces):
-    rows, width = half.shape[0], down.shape[1]
+        shared = shared_ref[:, at]
+        first = jnp.concatenate([term[:own] + shared[:own], term[own:rows]], axis=0)
+        keep_ref[:, at] = first.astype(jnp.bfloat16)
+        second = [term[rows:rows + own] + shared[own:], term[rows + own:rows + near]]
+        near_ref[:, at] = jnp.concatenate(second, axis=0).astype(jnp.bfloat16)
+        far_ref[:, at] = term[rows + near:].astype(jnp.bfloat16)
+
+
+def routed_parts(gathered, flat, down, named, shared, pieces, near):
+    count, width = sum(rows.shape[0] for rows in gathered), down.shape[1]
+    half = count // CORES
     return pl.pallas_call(
         functools.partial(routed_kernel, pieces),
-        in_specs=[pl.BlockSpec(memory_space=pltpu.VMEM)] * 6,
-        out_specs=[pl.BlockSpec(memory_space=pltpu.VMEM)] * CORES,
-        out_shape=[jax.ShapeDtypeStruct((rows, width), jnp.bfloat16)] * CORES,
-        scratch_shapes=[pltpu.VMEM((CORES * rows, flat.shape[1]), jnp.float32)],
+        in_specs=[pl.BlockSpec(memory_space=pltpu.VMEM)] * (len(gathered) + 4),
+        out_specs=[pl.BlockSpec(memory_space=pltpu.VMEM)] * 3,
+        out_shape=[jax.ShapeDtypeStruct((rows, width), jnp.bfloat16) for rows in (half, near, half - near)],
+        scratch_shapes=[pltpu.VMEM((count, flat.shape[1]), jnp.float32)],
         compiler_params=pltpu.CompilerParams(vmem_limit_bytes=VMEM_LIMIT),
         cost_estimate=pl.CostEstimate(
-            flops=2 * CORES * rows * (flat.size + down.size),
+            flops=2 * count * (flat.size + down.size),
             bytes_accessed=2 * (flat.size + down.size),
             transcendentals=0,
         ),
-    )(half, other, flat, down, named, shared)
+    )(*gathered, flat, down, named, shared)
 
 
 def after(value, ready):
@@ -247,34 +256,41 @@
     own_half = half_ep(routed_rows, experts)
     near_half = exchange(own_half, "sub", 1)
     token_all = jnp.concatenate([token_half, exchange(token_half, "ep", 1)], axis=0)
-    expert_weights, down_weights, shared_weights = held_weights(
-        expert_up[0], expert_down[0], shared_down, routed_rows
-    )
+    expert_weights, early = flat_pairs(expert_up[0], shared_up, routed_rows)
     far, expert_weights = lax.optimization_barrier((far, expert_weights))
-    middle = shared_middle(token_all, shared_up, far)
-
-    far_half = half_ep(far, experts)
-    half = after(jnp.concatenate([own_half, near_half, far_half], axis=0), middle)
-    other = exchange(half, "ep", 1)
+    middle = shared_middle(token_all, early, shared_up, far)
+
+    far_chips = [exchange(far, "ep", chip) for chip in range(CORES, experts, CORES)]
+    first = jnp.concatenate([own_half, far], axis=0)
+    late = after(jnp.concatenate([near_half] + far_chips, axis=0), middle)
+    gathered = (first, late, exchange(first, "ep", 1), exchange(late, "ep", 1))
 
     chips, split = experts // CORES, own_half.shape[0]
     pieces = []
     for core in range(CORES):
-        first = core * half.shape[0]
-        pieces.append((first, 2 * split))
-        pieces += [
-            (first + 2 * split + (chip * len(order) + at) * count, count)
-            for at in reversed(range(len(order))) for chip in range(chips)
-        ]
-    shared_part = jnp.dot(middle, shared_weights, preferred_element_type=jnp.float32)
-    keep, send = routed_parts(half, other, expert_weights, down_weights, named, shared_part, pieces)
-    pair = (keep.astype(jnp.float32) + exchange(send, "ep", 1).astype(jnp.float32)).astype(bf)
-
+        at_first = core * (first.shape[0] + late.shape[0])
+        at_late = at_first + first.shape[0]
+        pieces += [(at_first, split), (at_late, split)]
+        for at in reversed(range(len(order))):
+            pieces.append((at_first + split + at * count, count))
+            pieces += [
+                (at_late + split + (chip * len(order) + at) * count, count) for chip in range(chips - 1)
+            ]
+    shared_part = jnp.dot(middle, shared_down, preferred_element_type=jnp.float32)
+    keep, send_near, send_far = routed_parts(
+        gathered, expert_weights, expert_down[0], named, shared_part, pieces, 2 * split
+    )
+
+    def pair_sum(own, send):
+        return (own.astype(jnp.float32) + exchange(send, "ep", 1).astype(jnp.float32)).astype(bf)
+
+    pair = pair_sum(keep[2 * split:], send_far)
     sums = []
-    for at in range(2 * split, pair.shape[0], split):
+    for at in range(0, pair.shape[0], split):
         earlier = sums[-1] if sums else None
         sums.append(chip_sum(pair[at:at + split], experts, earlier).astype(bf))
-    near = exchange(pair[split:2 * split], "sub", 1)
+    pair = pair_sum(keep[:2 * split], send_near)
+    near = exchange(pair[split:], "sub", 1)
     near = (pair[:split].astype(jnp.float32) + near.astype(jnp.float32)).astype(bf)
     total = chip_sum(near, experts)
     for rows, k in zip(sums, order[::-1]):

time: 49.3 us -> 48.5 us (0.984)
  waiting for transfers between devices: 11.1 us -> 15 us
  Pallas kernels: 15.5 us -> 12.6 us
  starting transfers between devices: 19.7 us -> 17.9 us
    ppermute x15 -> x17, waiting for transfers between devices: 11.1 us -> 15 us  [exchange(): return lax.ppermute(rows, axis, [(i, i ^ flip) for i in range(size)])]
    ppermute x15 -> x17, starting transfers between devices: 19.7 us -> 17.9 us  [exchange(): return lax.ppermute(rows, axis, [(i, i ^ flip) for i in range(size)])]
    pallas_call x1, Pallas kernels: 6.39 us -> 4.78 us  [flat_pairs(): pl.pallas_call(split_kernel, in_specs=[pl.BlockSpec(memory_space=pltpu.HB...]
    pallas_call x1, Pallas kernels: 6.27 us -> 4.98 us  [shared_middle(): pl.pallas_call(shared_up_kernel, in_specs=[pl.BlockSpec(memory_space=pltp...]
  transfers between devices with their start and end apart: 15 -> 17, of which waited for: 4 -> 10; matrix products, arithmetic and copies ran while one was open for 4% -> 4% of each run, Pallas kernels for 26% -> 20%
where the time goes in v6:
time: 48.5 us; the launch traced here: 48.4 us
  starting transfers between devices  17.9 us (37%)
  waiting for transfers between devices  15 us (31%)
  Pallas kernels  12.6 us (26%)
  matrix products  1.4 us (3%)
  other arithmetic  1.22 us (3%)
    ppermute x17, starting transfers between devices, exchange(): return lax.ppermute(rows, axis, [(i, i ^ flip) for i in range(size)])  17.9 us
    ppermute x17, waiting for transfers between devices, exchange(): return lax.ppermute(rows, axis, [(i, i ^ flip) for i in range(size)])  15 us
    pallas_call x1, Pallas kernels, shared_middle(): pl.pallas_call(shared_up_kernel, in_specs=[pl.BlockSpec(memory_space=pltp...  4.98 us
    pallas_call x1, Pallas kernels, flat_pairs(): pl.pallas_call(split_kernel, in_specs=[pl.BlockSpec(memory_space=pltpu.HB...  4.78 us
    pallas_call x1, Pallas kernels, routed_parts(): pl.pallas_call(functools.partial(routed_kernel, pieces), in_specs=[pl.Blo...  1.72 us
    dot_general x1, matrix products, per_device(): jnp.dot(middle, shared_down, preferred_element_type=jnp.float32)  1.4 us
    pallas_call x1, Pallas kernels, owner_rows(): pl.pallas_call(owner_kernel, in_specs=[pl.BlockSpec(memory_space=pltpu.HB...  1.09 us
  transfers between devices with their start and end apart: 17, of which 10 were waited for; matrix products, arithmetic and copies ran while one was open for 4% of the time, Pallas kernels for 20%

profile of v6, /device:TPU:0, one launch (start us, length us, event | category | flops | bytes accessed | tf_op | source)
XLA Modules:
  0.0 48.4 jit_solution(8288381294448417668)
XLA Ops:
  0.0 1.1 %shard_map.73.ready_ref = bf16[8,7296]{1,0:T(8,128)(2,1)S(1)} custom-call(bf16[8,7168]{1,0:T(8,128)(2,1)} %tokens_ref.1, s32[2,8]{1,0:T(2,128)} %bitcast.10, bf16[2,8]{1,0:T(2,128)(2,1)} %bitcast.11, f32[1,128]{1,0:T(1,128)S(1)} %compare_convert_fusion.ready_ref.refs_6_), custom_call_target="tpu_custom_call" | custom-call | tf_op jit(solution)/shard_map/pallas_call | solution.py:59
  1.1 3.0 %collective-permute-start.5 = (bf16[8,7168]{1,0:T(8,128)(2,1)}, bf16[8,7168]{1,0:T(8,128)(2,1)S(1)}, u32[]{:S(2)}, u32[]{:S(2)}) collective-permute-start(bf16[8,7168]{1,0:T(8,128)(2,1)} %tokens_ref.1), channel_id=1, source_target_pairs={{0,8},{4,12},{8,0},{12,4},{1,9},{5,13},{9,1},{13,5},{2,10},{6,14},... | collective-permute-start | bytes 344072 | tf_op jit(solution)/shard_map/ppermute | solution.py:222
  4.1 3.6 %collective-permute-start.1 = (bf16[8,7296]{1,0:T(8,128)(2,1)S(1)}, bf16[8,7296]{1,0:T(8,128)(2,1)S(1)}, u32[]{:S(2)}, u32[]{:S(2)}) collective-permute-start(bf16[8,7296]{1,0:T(8,128)(2,1)S(1)} %shard_map.73.ready_ref), channel_id=1, source_target_pairs={{0,3},{1,2},{2,1},{3,0},{4,7},{5,6},{6,5},{7,4},{8,11},{9,10},{10,... | collective-permute-start | bytes 350216 | tf_op jit(solution)/shard_map/ppermute | solution.py:222
  7.7 0.5 %collective-permute-start = (bf16[8,7296]{1,0:T(8,128)(2,1)S(1)}, bf16[8,7296]{1,0:T(8,128)(2,1)S(1)}, u32[]{:S(2)}, u32[]{:S(2)}) collective-permute-start(bf16[8,7296]{1,0:T(8,128)(2,1)S(1)} %shard_map.73.ready_ref), channel_id=1, source_target_pairs={{0,8},{4,12},{8,0},{12,4},{1,9},{5,13},{9,1},{13,5},{2,10},{6,14},... | collective-permute-start | bytes 350216 | tf_op jit(solution)/shard_map/ppermute | solution.py:222
  8.2 4.8 %shard_map.74 = (bf16[7168,512]{1,0:T(8,128)(2,1)S(1)}, bf16[2560,2,512]{2,1,0:T(2,128)(2,1)S(1)}) custom-call(bf16[7168,2,256]{2,1,0:T(2,128)(2,1)} %bitcast.9, bf16[7168,2,512]{2,1,0:T(2,128)(2,1)} %up_ref.3, bf16[8,7296]{1,0:T(8,128)(2,1)S(1)} %shard_map.73.ready_ref), custom_call_target="tpu_custom_call" | custom-call | bytes 14680064 | tf_op jit(solution)/shard_map/pallas_call | solution.py:97
  13.2 4.1 %collective-permute-done.2 = bf16[8,7296]{1,0:T(8,128)(2,1)S(1)} collective-permute-done((bf16[8,7296]{1,0:T(8,128)(2,1)S(1)}, bf16[8,7296]{1,0:T(8,128)(2,1)S(1)}, u32[]{:S(2)}, u32[]{:S(2)}) %collective-permute-start.2) | collective-permute-done | bytes 116768 | tf_op jit(solution)/shard_map/ppermute | solution.py:222
  17.3 0.6 %collective-permute-start.4 = (bf16[16,7296]{1,0:T(8,128)(2,1)S(1)}, bf16[16,7296]{1,0:T(8,128)(2,1)S(1)}, u32[]{:S(2)}, u32[]{:S(2)}) collective-permute-start(bf16[16,7296]{1,0:T(8,128)(2,1)S(1)} %pad_maximum_fusion.3.ready_ref), channel_id=1, source_target_pairs={{0,8},{4,12},{8,0},{12,4},{1,9},{5,13},{9,1},{13,5},{2,10},{6,14},... | collective-permute-start | bytes 700424 | tf_op jit(solution)/shard_map/ppermute | solution.py:222
  18.2 5.0 %shard_map.75 = bf16[32,512]{1,0:T(8,128)(2,1)S(1)} custom-call(bf16[32,7168]{1,0:T(8,128)(2,1)S(1)} %pad_maximum_fusion.2.rows_ref, bf16[2560,2,512]{2,1,0:T(2,128)(2,1)S(1)} %get-tuple-element.18.early_ref, bf16[7168,2,512]{2,1,0:T(2,128)(2,1)} %up_ref.3, bf16[16,7296]{1,0:T(8,128)(2,1)S(1)} %pad_maximum_fusion.3.ready_ref), custom_call_target="tpu_custom_call" | custom-call | flops 469762048 | bytes 14680064 | tf_op jit(solution)/shard_map/pallas_call | solution.py:143
  23.2 0.9 %collective-permute-done.4 = bf16[16,7296]{1,0:T(8,128)(2,1)S(1)} collective-permute-done((bf16[16,7296]{1,0:T(8,128)(2,1)S(1)}, bf16[16,7296]{1,0:T(8,128)(2,1)S(1)}, u32[]{:S(2)}, u32[]{:S(2)}) %collective-permute-start.4) | collective-permute-done | bytes 233504 | tf_op jit(solution)/shard_map/ppermute | solution.py:222
  24.6 1.4 %fusion.1.refs_7_ = f32[32,7168]{1,0:T(8,128)S(1)} fusion(bf16[32,512]{1,0:T(8,128)(2,1)S(1)} %shard_map.75, bf16[512,7168]{1,0:T(8,128)(2,1)S(1)} %bitcast.8), kind=kOutput, calls=%fused_computation.14 | convolution fusion | flops 234881024 | bytes 8290304 | tf_op jit(solution)/shard_map/dot_general | solution.py:279
  26.0 0.4 collective-permute-done.8.refs_3_
  26.4 1.7 %shard_map.76 = (bf16[64,7168]{1,0:T(8,128)(2,1)S(1)}, bf16[32,7168]{1,0:T(8,128)(2,1)S(1)}, bf16[32,7168]{1,0:T(8,128)(2,1)S(1)}) custom-call(bf16[32,7296]{1,0:T(8,128)(2,1)S(1)} %pad_maximum_fusion.refs_0_, bf16[32,7296]{1,0:T(8,128)(2,1)S(1)} %pad_maximum_fusion.1.refs_1_, bf16[32,7296]{1,0:T(8,128)(2,1)S(1)} %collective-permute-done.7.refs_2_, ...), custom_call_target="tpu_custom_call" | custom-call | flops 1409286144 | bytes 11010048 | tf_op jit(solution)/shard_map/pallas_call | solution.py:201
  28.7 1.3 %collective-permute-done.12 = bf16[32,7168]{1,0:T(8,128)(2,1)S(1)} collective-permute-done((bf16[32,7168]{1,0:T(8,128)(2,1)S(1)}, bf16[32,7168]{1,0:T(8,128)(2,1)S(1)}, u32[]{:S(2)}, u32[]{:S(2)}) %collective-permute-start.12) | collective-permute-done | bytes 458784 | tf_op jit(solution)/shard_map/ppermute | solution.py:222
  30.0 0.7 %collective-permute-done.9 = bf16[32,7168]{1,0:T(8,128)(2,1)S(1)} collective-permute-done((bf16[32,7168]{1,0:T(8,128)(2,1)S(1)}, bf16[32,7168]{1,0:T(8,128)(2,1)S(1)}, u32[]{:S(2)}, u32[]{:S(2)}) %collective-permute-start.9) | collective-permute-done | bytes 458784 | tf_op jit(solution)/shard_map/ppermute | solution.py:222
  30.9 1.6 %collective-permute-start.13 = (bf16[8,7168]{1,0:T(8,128)(2,1)S(1)}, bf16[8,7168]{1,0:T(8,128)(2,1)S(1)}, u32[]{:S(2)}, u32[]{:S(2)}) collective-permute-start(bf16[8,7168]{1,0:T(8,128)(2,1)S(1)} %get-tuple-element.27), channel_id=1, source_target_pairs={{0,8},{4,12},{8,0},{12,4},{1,9},{5,13},{9,1},{13,5},{2,10},{6,14},... | collective-permute-start | bytes 344072 | tf_op jit(solution)/shard_map/ppermute | solution.py:222
  32.5 1.4 %collective-permute-start.10 = (bf16[16,7168]{1,0:T(8,128)(2,1)S(1)}, bf16[16,7168]{1,0:T(8,128)(2,1)S(1)}, u32[]{:S(2)}, u32[]{:S(2)}) collective-permute-start(bf16[16,7168]{1,0:T(8,128)(2,1)S(1)} %slice.47), channel_id=1, source_target_pairs={{0,1},{1,0},{2,3},{3,2},{4,5},{5,4},{6,7},{7,6},{8,9},{9,8},{10,11... | collective-permute-start | bytes 688136 | tf_op jit(solution)/shard_map/ppermute | solution.py:222
  33.8 0.5 %collective-permute-start.15 = (bf16[8,7168]{1,0:T(8,128)(2,1)S(1)}, bf16[8,7168]{1,0:T(8,128)(2,1)S(1)}, u32[]{:S(2)}, u32[]{:S(2)}) collective-permute-start(bf16[8,7168]{1,0:T(8,128)(2,1)S(1)} %get-tuple-element.28), channel_id=1, source_target_pairs={{0,8},{4,12},{8,0},{12,4},{1,9},{5,13},{9,1},{13,5},{2,10},{6,14},... | collective-permute-start | bytes 344072 | tf_op jit(solution)/shard_map/ppermute | solution.py:222
  34.3 1.8 %collective-permute-done.13 = bf16[8,7168]{1,0:T(8,128)(2,1)S(1)} collective-permute-done((bf16[8,7168]{1,0:T(8,128)(2,1)S(1)}, bf16[8,7168]{1,0:T(8,128)(2,1)S(1)}, u32[]{:S(2)}, u32[]{:S(2)}) %collective-permute-start.13) | collective-permute-done | bytes 114720 | tf_op jit(solution)/shard_map/ppermute | solution.py:222
  36.1 3.1 %collective-permute-start.14 = (bf16[8,7168]{1,0:T(8,128)(2,1)S(1)}, bf16[8,7168]{1,0:T(8,128)(2,1)S(1)}, u32[]{:S(2)}, u32[]{:S(2)}) collective-permute-start(bf16[8,7168]{1,0:T(8,128)(2,1)S(1)} %add_convert_fusion.5), channel_id=1, source_target_pairs={{0,2},{1,3},{2,0},{3,1},{4,6},{5,7},{6,4},{7,5},{8,10},{9,11},{10,... | collective-permute-start | bytes 344072 | tf_op jit(solution)/shard_map/ppermute | solution.py:222
  39.3 1.9 %collective-permute-start.16 = (bf16[8,7168]{1,0:T(8,128)(2,1)S(1)}, bf16[8,7168]{1,0:T(8,128)(2,1)S(1)}, u32[]{:S(2)}, u32[]{:S(2)}) collective-permute-start(bf16[8,7168]{1,0:T(8,128)(2,1)S(1)} %add_convert_fusion.4), channel_id=1, source_target_pairs={{0,3},{1,2},{2,1},{3,0},{4,7},{5,6},{6,5},{7,4},{8,11},{9,10},{10,... | collective-permute-start | bytes 344072 | tf_op jit(solution)/shard_map/ppermute | solution.py:222
  41.6 0.8 %collective-permute-start.11 = (bf16[8,7168]{1,0:T(8,128)(2,1)S(1)}, bf16[8,7168]{1,0:T(8,128)(2,1)S(1)}, u32[]{:S(2)}, u32[]{:S(2)}) collective-permute-start(bf16[8,7168]{1,0:T(8,128)(2,1)S(1)} %slice.49), channel_id=1, source_target_pairs={{0,8},{4,12},{8,0},{12,4},{1,9},{5,13},{9,1},{13,5},{2,10},{6,14},... | collective-permute-start | bytes 344072 | tf_op jit(solution)/shard_map/ppermute | solution.py:222
  42.5 4.4 %collective-permute-done.16 = bf16[8,7168]{1,0:T(8,128)(2,1)S(1)} collective-permute-done((bf16[8,7168]{1,0:T(8,128)(2,1)S(1)}, bf16[8,7168]{1,0:T(8,128)(2,1)S(1)}, u32[]{:S(2)}, u32[]{:S(2)}) %collective-permute-start.16) | collective-permute-done | bytes 114720 | tf_op jit(solution)/shard_map/ppermute | solution.py:222
  46.9 0.8 %collective-permute-done.14 = bf16[8,7168]{1,0:T(8,128)(2,1)S(1)} collective-permute-done((bf16[8,7168]{1,0:T(8,128)(2,1)S(1)}, bf16[8,7168]{1,0:T(8,128)(2,1)S(1)}, u32[]{:S(2)}, u32[]{:S(2)}) %collective-permute-start.14) | collective-permute-done | bytes 114720 | tf_op jit(solution)/shard_map/ppermute | solution.py:222
  47.7 0.7 %add_convert_fusion.3 = bf16[8,7168]{1,0:T(8,128)(2,1)} fusion(bf16[8,7168]{1,0:T(8,128)(2,1)S(1)} %collective-permute-done.16, bf16[8,7168]{1,0:T(8,128)(2,1)S(1)} %collective-permute-done.14, bf16[8,7168]{1,0:T(8,128)(2,1)S(1)} %collective-permute-done.11, bf16[16,7168]{1,0:T(8,128)(2,1)S(1)} %add_convert_fusion.2), kind=kLoop, calls=%fused_computation.9 | loop fusion | flops 458752 | bytes 573440 | tf_op jit(solution)/shard_map/convert_element_type | solution.py:298
  (39 shorter events, 2.1 us)
Async XLA Ops:
  1.1 11.9 %collective-permute-start.5 = (bf16[8,7168]{1,0:T(8,128)(2,1)}, bf16[8,7168]{1,0:T(8,128)(2,1)S(1)}, u32[]{:S(2)}, u32[]{:S(2)}) collective-permute-start(bf16[8,7168]{1,0:T(8,128)(2,1)} %tokens_ref.1), channel_id=1, source_target_pairs={{0,8},{4,12},{8,0},{12,4},{1,9},{5,13},{9,1},{13,5},{2,10},{6,14},... | collective-permute-start | bytes 344072 | tf_op jit(solution)/shard_map/ppermute | solution.py:222
  4.1 9.0 %collective-permute-start.1 = (bf16[8,7296]{1,0:T(8,128)(2,1)S(1)}, bf16[8,7296]{1,0:T(8,128)(2,1)S(1)}, u32[]{:S(2)}, u32[]{:S(2)}) collective-permute-start(bf16[8,7296]{1,0:T(8,128)(2,1)S(1)} %shard_map.73.ready_ref), channel_id=1, source_target_pairs={{0,3},{1,2},{2,1},{3,0},{4,7},{5,6},{6,5},{7,4},{8,11},{9,10},{10,... | collective-permute-start | bytes 350216 | tf_op jit(solution)/shard_map/ppermute | solution.py:222
  7.7 9.6 %collective-permute-start.2 = (bf16[8,7296]{1,0:T(8,128)(2,1)S(1)}, bf16[8,7296]{1,0:T(8,128)(2,1)S(1)}, u32[]{:S(2)}, u32[]{:S(2)}) collective-permute-start(bf16[8,7296]{1,0:T(8,128)(2,1)S(1)} %shard_map.73.ready_ref), channel_id=1, source_target_pairs={{0,2},{1,3},{2,0},{3,1},{4,6},{5,7},{6,4},{7,5},{8,10},{9,11},{10,... | collective-permute-start | bytes 350216 | tf_op jit(solution)/shard_map/ppermute | solution.py:222
  7.7 10.2 %collective-permute-start = (bf16[8,7296]{1,0:T(8,128)(2,1)S(1)}, bf16[8,7296]{1,0:T(8,128)(2,1)S(1)}, u32[]{:S(2)}, u32[]{:S(2)}) collective-permute-start(bf16[8,7296]{1,0:T(8,128)(2,1)S(1)} %shard_map.73.ready_ref), channel_id=1, source_target_pairs={{0,8},{4,12},{8,0},{12,4},{1,9},{5,13},{9,1},{13,5},{2,10},{6,14},... | collective-permute-start | bytes 350216 | tf_op jit(solution)/shard_map/ppermute | solution.py:222
  8.2 4.8 %copy-start.1 = (bf16[8,7168]{1,0:T(8,128)(2,1)S(1)}, bf16[8,7168]{1,0:T(8,128)(2,1)}, u32[]{:S(2)}) copy-start(bf16[8,7168]{1,0:T(8,128)(2,1)} %tokens_ref.1) | copy-start | bytes 344068
  13.1 5.1 %collective-permute-start.6 = (bf16[16,7168]{1,0:T(8,128)(2,1)S(1)}, bf16[16,7168]{1,0:T(8,128)(2,1)S(1)}, u32[]{:S(2)}, u32[]{:S(2)}) collective-permute-start(bf16[16,7168]{1,0:T(8,128)(2,1)S(1)} %pad_maximum_fusion.5), channel_id=1, source_target_pairs={{0,4},{4,0},{8,12},{12,8},{1,5},{5,1},{9,13},{13,9},{2,6},{6,2},{1... | collective-permute-start | bytes 688136 | tf_op jit(solution)/shard_map/ppermute | solution.py:222
  17.3 6.8 %collective-permute-start.4 = (bf16[16,7296]{1,0:T(8,128)(2,1)S(1)}, bf16[16,7296]{1,0:T(8,128)(2,1)S(1)}, u32[]{:S(2)}, u32[]{:S(2)}) collective-permute-start(bf16[16,7296]{1,0:T(8,128)(2,1)S(1)} %pad_maximum_fusion.3.ready_ref), channel_id=1, source_target_pairs={{0,8},{4,12},{8,0},{12,4},{1,9},{5,13},{9,1},{13,5},{2,10},{6,14},... | collective-permute-start | bytes 700424 | tf_op jit(solution)/shard_map/ppermute | solution.py:222
  17.9 6.5 %collective-permute-start.3 = (bf16[16,7296]{1,0:T(8,128)(2,1)S(1)}, bf16[16,7296]{1,0:T(8,128)(2,1)S(1)}, u32[]{:S(2)}, u32[]{:S(2)}) collective-permute-start(bf16[16,7296]{1,0:T(8,128)(2,1)S(1)} %pad_maximum_fusion.4), channel_id=1, source_target_pairs={{0,1},{1,0},{2,3},{3,2},{4,5},{5,4},{6,7},{7,6},{8,9},{9,8},{10,11... | collective-permute-start | bytes 700424 | tf_op jit(solution)/shard_map/ppermute | solution.py:222
  18.1 7.9 %collective-permute-start.7 = (bf16[32,7296]{1,0:T(8,128)(2,1)S(1)}, bf16[32,7296]{1,0:T(8,128)(2,1)S(1)}, u32[]{:S(2)}, u32[]{:S(2)}) collective-permute-start(bf16[32,7296]{1,0:T(8,128)(2,1)S(1)} %pad_maximum_fusion.refs_0_), channel_id=1, source_target_pairs={{0,4},{4,0},{8,12},{12,8},{1,5},{5,1},{9,13},{13,9},{2,6},{6,2},{1... | collective-permute-start | bytes 1400840 | tf_op jit(solution)/shard_map/ppermute | solution.py:222
  18.1 6.4 %slice-start = ((s8[7340032]{0:T(1024)(128)(4,1)}), s8[4194304]{0:T(1024)(128)(4,1)S(1)}, s32[]{:S(2)}) async-start(s8[7340032]{0:T(1024)(128)(4,1)} %bitcast.7), calls=%async_computation | async-start | bytes 8388608
  18.2 6.4 %slice-start.1 = ((s8[7340032]{0:T(1024)(128)(4,1)}), s8[3145728]{0:T(1024)(128)(4,1)S(1)}, s32[]{:S(2)}) async-start(s8[7340032]{0:T(1024)(128)(4,1)} %bitcast.7), calls=%async_computation.1 | async-start | bytes 6291456
  23.2 3.2 %copy-start = (bf16[1,256,7168]{2,1,0:T(8,128)(2,1)S(1)}, bf16[1,256,7168]{2,1,0:T(8,128)(2,1)}, u32[]{:S(2)}) copy-start(bf16[1,256,7168]{2,1,0:T(8,128)(2,1)} %param.11) | copy-start | bytes 11010052
  24.5 1.9 %collective-permute-start.8 = (bf16[32,7296]{1,0:T(8,128)(2,1)S(1)}, bf16[32,7296]{1,0:T(8,128)(2,1)S(1)}, u32[]{:S(2)}, u32[]{:S(2)}) collective-permute-start(bf16[32,7296]{1,0:T(8,128)(2,1)S(1)} %pad_maximum_fusion.1.refs_1_), channel_id=1, source_target_pairs={{0,4},{4,0},{8,12},{12,8},{1,5},{5,1},{9,13},{13,9},{2,6},{6,2},{1... | collective-permute-start | bytes 1400840 | tf_op jit(solution)/shard_map/ppermute | solution.py:222
  28.1 1.9 %collective-permute-start.12 = (bf16[32,7168]{1,0:T(8,128)(2,1)S(1)}, bf16[32,7168]{1,0:T(8,128)(2,1)S(1)}, u32[]{:S(2)}, u32[]{:S(2)}) collective-permute-start(bf16[32,7168]{1,0:T(8,128)(2,1)S(1)} %get-tuple-element.23), channel_id=1, source_target_pairs={{0,4},{4,0},{8,12},{12,8},{1,5},{5,1},{9,13},{13,9},{2,6},{6,2},{1... | collective-permute-start | bytes 1376264 | tf_op jit(solution)/shard_map/ppermute | solution.py:222
  28.3 2.3 %collective-permute-start.9 = (bf16[32,7168]{1,0:T(8,128)(2,1)S(1)}, bf16[32,7168]{1,0:T(8,128)(2,1)S(1)}, u32[]{:S(2)}, u32[]{:S(2)}) collective-permute-start(bf16[32,7168]{1,0:T(8,128)(2,1)S(1)} %get-tuple-element.22), channel_id=1, source_target_pairs={{0,4},{4,0},{8,12},{12,8},{1,5},{5,1},{9,13},{13,9},{2,6},{6,2},{1... | collective-permute-start | bytes 1376264 | tf_op jit(solution)/shard_map/ppermute | solution.py:222
  30.9 5.3 %collective-permute-start.13 = (bf16[8,7168]{1,0:T(8,128)(2,1)S(1)}, bf16[8,7168]{1,0:T(8,128)(2,1)S(1)}, u32[]{:S(2)}, u32[]{:S(2)}) collective-permute-start(bf16[8,7168]{1,0:T(8,128)(2,1)S(1)} %get-tuple-element.27), channel_id=1, source_target_pairs={{0,8},{4,12},{8,0},{12,4},{1,9},{5,13},{9,1},{13,5},{2,10},{6,14},... | collective-permute-start | bytes 344072 | tf_op jit(solution)/shard_map/ppermute | solution.py:222
  32.5 9.1 %collective-permute-start.10 = (bf16[16,7168]{1,0:T(8,128)(2,1)S(1)}, bf16[16,7168]{1,0:T(8,128)(2,1)S(1)}, u32[]{:S(2)}, u32[]{:S(2)}) collective-permute-start(bf16[16,7168]{1,0:T(8,128)(2,1)S(1)} %slice.47), channel_id=1, source_target_pairs={{0,1},{1,0},{2,3},{3,2},{4,5},{5,4},{6,7},{7,6},{8,9},{9,8},{10,11... | collective-permute-start | bytes 688136 | tf_op jit(solution)/shard_map/ppermute | solution.py:222
  33.8 5.5 %collective-permute-start.15 = (bf16[8,7168]{1,0:T(8,128)(2,1)S(1)}, bf16[8,7168]{1,0:T(8,128)(2,1)S(1)}, u32[]{:S(2)}, u32[]{:S(2)}) collective-permute-start(bf16[8,7168]{1,0:T(8,128)(2,1)S(1)} %get-tuple-element.28), channel_id=1, source_target_pairs={{0,8},{4,12},{8,0},{12,4},{1,9},{5,13},{9,1},{13,5},{2,10},{6,14},... | collective-permute-start | bytes 344072 | tf_op jit(solution)/shard_map/ppermute | solution.py:222
  36.1 11.5 %collective-permute-start.14 = (bf16[8,7168]{1,0:T(8,128)(2,1)S(1)}, bf16[8,7168]{1,0:T(8,128)(2,1)S(1)}, u32[]{:S(2)}, u32[]{:S(2)}) collective-permute-start(bf16[8,7168]{1,0:T(8,128)(2,1)S(1)} %add_convert_fusion.5), channel_id=1, source_target_pairs={{0,2},{1,3},{2,0},{3,1},{4,6},{5,7},{6,4},{7,5},{8,10},{9,11},{10,... | collective-permute-start | bytes 344072 | tf_op jit(solution)/shard_map/ppermute | solution.py:222
  39.3 7.5 %collective-permute-start.16 = (bf16[8,7168]{1,0:T(8,128)(2,1)S(1)}, bf16[8,7168]{1,0:T(8,128)(2,1)S(1)}, u32[]{:S(2)}, u32[]{:S(2)}) collective-permute-start(bf16[8,7168]{1,0:T(8,128)(2,1)S(1)} %add_convert_fusion.4), channel_id=1, source_target_pairs={{0,3},{1,2},{2,1},{3,0},{4,7},{5,6},{6,5},{7,4},{8,11},{9,10},{10,... | collective-permute-start | bytes 344072 | tf_op jit(solution)/shard_map/ppermute | solution.py:222
  41.6 6.1 %collective-permute-start.11 = (bf16[8,7168]{1,0:T(8,128)(2,1)S(1)}, bf16[8,7168]{1,0:T(8,128)(2,1)S(1)}, u32[]{:S(2)}, u32[]{:S(2)}) collective-permute-start(bf16[8,7168]{1,0:T(8,128)(2,1)S(1)} %slice.49), channel_id=1, source_target_pairs={{0,8},{4,12},{8,0},{12,4},{1,9},{5,13},{9,1},{13,5},{2,10},{6,14},... | collective-permute-start | bytes 344072 | tf_op jit(solution)/shard_map/ppermute | solution.py:222

commit v7 on v6

--- a/solution.py
+++ b/solution.py
@@ -257,7 +257,7 @@
     near_half = exchange(own_half, "sub", 1)
     token_all = jnp.concatenate([token_half, exchange(token_half, "ep", 1)], axis=0)
     expert_weights, early = flat_pairs(expert_up[0], shared_up, routed_rows)
-    far, expert_weights = lax.optimization_barrier((far, expert_weights))
+    far, expert_weights, _ = lax.optimization_barrier((far, expert_weights, (own_half, token_half)))
     middle = shared_middle(token_all, early, shared_up, far)
 
     far_chips = [exchange(far, "ep", chip) for chip in range(CORES, experts, CORES)]

time: 48.5 us -> 48.2 us (level)
  starting transfers between devices: 17.9 us -> 15.9 us
  local copies, waits for them, and re-layouts: 0.07 us -> 1.02 us
  waiting for transfers between devices: 15 us -> 15.7 us
    ppermute x17, starting transfers between devices: 17.9 us -> 15.9 us  [exchange(): return lax.ppermute(rows, axis, [(i, i ^ flip) for i in range(size)])]
    unnamed x8 -> x9, local copies, waits for them, and re-layouts: 0.03 us -> 0.96 us
    ppermute x17, waiting for transfers between devices: 15 us -> 15.7 us  [exchange(): return lax.ppermute(rows, axis, [(i, i ^ flip) for i in range(size)])]
  transfers between devices with their start and end apart: 17 -> 17, of which waited for: 10 -> 9; matrix products, arithmetic and copies ran while one was open for 4% -> 6% of each run, Pallas kernels for 20% -> 20%
where the time goes in v7:
time: 48.2 us; the launch traced here: 48 us
  starting transfers between devices  15.9 us (33%)
  waiting for transfers between devices  15.7 us (33%)
  Pallas kernels  12.6 us (26%)
  matrix products  1.4 us (3%)
  other arithmetic  1.21 us (3%)
  local copies, waits for them, and re-layouts  1.02 us (2%)
    ppermute x17, starting transfers between devices, exchange(): return lax.ppermute(rows, axis, [(i, i ^ flip) for i in range(size)])  15.9 us
    ppermute x17, waiting for transfers between devices, exchange(): return lax.ppermute(rows, axis, [(i, i ^ flip) for i in range(size)])  15.7 us
    pallas_call x1, Pallas kernels, shared_middle(): pl.pallas_call(shared_up_kernel, in_specs=[pl.BlockSpec(memory_space=pltp...  4.97 us
    pallas_call x1, Pallas kernels, flat_pairs(): pl.pallas_call(split_kernel, in_specs=[pl.BlockSpec(memory_space=pltpu.HB...  4.78 us
    pallas_call x1, Pallas kernels, routed_parts(): pl.pallas_call(functools.partial(routed_kernel, pieces), in_specs=[pl.Blo...  1.72 us
    dot_general x1, matrix products, per_device(): jnp.dot(middle, shared_down, preferred_element_type=jnp.float32)  1.4 us
    pallas_call x1, Pallas kernels, owner_rows(): pl.pallas_call(owner_kernel, in_specs=[pl.BlockSpec(memory_space=pltpu.HB...  1.09 us
    unnamed x9, local copies, waits for them, and re-layouts  0.96 us
  transfers between devices with their start and end apart: 17, of which 9 were waited for; matrix products, arithmetic and copies ran while one was open for 6% of the time, Pallas kernels for 20%

profile of v7, /device:TPU:0, one launch (start us, length us, event | category | flops | bytes accessed | tf_op | source)
XLA Modules:
  0.0 48.0 jit_solution(16648620355542247118)
XLA Ops:
  0.0 1.1 %shard_map.73.ready_ref = bf16[8,7296]{1,0:T(8,128)(2,1)S(1)} custom-call(bf16[8,7168]{1,0:T(8,128)(2,1)} %tokens_ref.1, s32[2,8]{1,0:T(2,128)} %bitcast.10, bf16[2,8]{1,0:T(2,128)(2,1)} %bitcast.11, f32[1,128]{1,0:T(1,128)S(1)} %compare_convert_fusion.ready_ref.refs_6_), custom_call_target="tpu_custom_call" | custom-call | tf_op jit(solution)/shard_map/pallas_call | solution.py:59
  1.1 3.0 %collective-permute-start = (bf16[8,7296]{1,0:T(8,128)(2,1)S(1)}, bf16[8,7296]{1,0:T(8,128)(2,1)S(1)}, u32[]{:S(2)}, u32[]{:S(2)}) collective-permute-start(bf16[8,7296]{1,0:T(8,128)(2,1)S(1)} %shard_map.73.ready_ref), channel_id=1, source_target_pairs={{0,8},{4,12},{8,0},{12,4},{1,9},{5,13},{9,1},{13,5},{2,10},{6,14},... | collective-permute-start | bytes 350216 | tf_op jit(solution)/shard_map/ppermute | solution.py:222
  4.1 3.6 %collective-permute-start.1 = (bf16[8,7296]{1,0:T(8,128)(2,1)S(1)}, bf16[8,7296]{1,0:T(8,128)(2,1)S(1)}, u32[]{:S(2)}, u32[]{:S(2)}) collective-permute-start(bf16[8,7296]{1,0:T(8,128)(2,1)S(1)} %shard_map.73.ready_ref), channel_id=1, source_target_pairs={{0,3},{1,2},{2,1},{3,0},{4,7},{5,6},{6,5},{7,4},{8,11},{9,10},{10,... | collective-permute-start | bytes 350216 | tf_op jit(solution)/shard_map/ppermute | solution.py:222
  8.2 0.9 %constant_dynamic-update-slice_fusion.1 = bf16[16,7168]{1,0:T(8,128)(2,1)S(1)} fusion(bf16[8,7168]{1,0:T(8,128)(2,1)} %tokens_ref.1), kind=kLoop, calls=%fused_computation.12 | loop fusion | bytes 229376
  9.2 4.8 %shard_map.74 = (bf16[7168,512]{1,0:T(8,128)(2,1)S(1)}, bf16[2560,2,512]{2,1,0:T(2,128)(2,1)S(1)}) custom-call(bf16[7168,2,256]{2,1,0:T(2,128)(2,1)} %bitcast.9, bf16[7168,2,512]{2,1,0:T(2,128)(2,1)} %up_ref.3, bf16[8,7296]{1,0:T(8,128)(2,1)S(1)} %shard_map.73.ready_ref), custom_call_target="tpu_custom_call" | custom-call | bytes 14680064 | tf_op jit(solution)/shard_map/pallas_call | solution.py:97
  14.1 0.6 %collective-permute-start.4 = (bf16[16,7296]{1,0:T(8,128)(2,1)S(1)}, bf16[16,7296]{1,0:T(8,128)(2,1)S(1)}, u32[]{:S(2)}, u32[]{:S(2)}) collective-permute-start(bf16[16,7296]{1,0:T(8,128)(2,1)S(1)} %pad_maximum_fusion.4), channel_id=1, source_target_pairs={{0,1},{1,0},{2,3},{3,2},{4,5},{5,4},{6,7},{7,6},{8,9},{9,8},{10,11... | collective-permute-start | bytes 700424 | tf_op jit(solution)/shard_map/ppermute | solution.py:222
  14.8 2.5 %collective-permute-done.2 = bf16[8,7296]{1,0:T(8,128)(2,1)S(1)} collective-permute-done((bf16[8,7296]{1,0:T(8,128)(2,1)S(1)}, bf16[8,7296]{1,0:T(8,128)(2,1)S(1)}, u32[]{:S(2)}, u32[]{:S(2)}) %collective-permute-start.2) | collective-permute-done | bytes 116768 | tf_op jit(solution)/shard_map/ppermute | solution.py:222
  17.3 0.6 %collective-permute-start.5 = (bf16[16,7296]{1,0:T(8,128)(2,1)S(1)}, bf16[16,7296]{1,0:T(8,128)(2,1)S(1)}, u32[]{:S(2)}, u32[]{:S(2)}) collective-permute-start(bf16[16,7296]{1,0:T(8,128)(2,1)S(1)} %pad_maximum_fusion.3.ready_ref), channel_id=1, source_target_pairs={{0,8},{4,12},{8,0},{12,4},{1,9},{5,13},{9,1},{13,5},{2,10},{6,14},... | collective-permute-start | bytes 700424 | tf_op jit(solution)/shard_map/ppermute | solution.py:222
  18.1 5.0 %shard_map.75 = bf16[32,512]{1,0:T(8,128)(2,1)S(1)} custom-call(bf16[32,7168]{1,0:T(8,128)(2,1)S(1)} %pad_maximum_fusion.2.rows_ref, bf16[2560,2,512]{2,1,0:T(2,128)(2,1)S(1)} %get-tuple-element.18.early_ref, bf16[7168,2,512]{2,1,0:T(2,128)(2,1)} %up_ref.3, bf16[16,7296]{1,0:T(8,128)(2,1)S(1)} %pad_maximum_fusion.3.ready_ref), custom_call_target="tpu_custom_call" | custom-call | flops 469762048 | bytes 14680064 | tf_op jit(solution)/shard_map/pallas_call | solution.py:143
  23.1 1.0 %collective-permute-done.5 = bf16[16,7296]{1,0:T(8,128)(2,1)S(1)} collective-permute-done((bf16[16,7296]{1,0:T(8,128)(2,1)S(1)}, bf16[16,7296]{1,0:T(8,128)(2,1)S(1)}, u32[]{:S(2)}, u32[]{:S(2)}) %collective-permute-start.5) | collective-permute-done | bytes 233504 | tf_op jit(solution)/shard_map/ppermute | solution.py:222
  24.3 1.4 %fusion.1.refs_7_ = f32[32,7168]{1,0:T(8,128)S(1)} fusion(bf16[32,512]{1,0:T(8,128)(2,1)S(1)} %shard_map.75, bf16[512,7168]{1,0:T(8,128)(2,1)S(1)} %bitcast.8), kind=kOutput, calls=%fused_computation.15 | convolution fusion | flops 234881024 | bytes 8290304 | tf_op jit(solution)/shard_map/dot_general | solution.py:279
  26.0 1.7 %shard_map.76 = (bf16[64,7168]{1,0:T(8,128)(2,1)S(1)}, bf16[32,7168]{1,0:T(8,128)(2,1)S(1)}, bf16[32,7168]{1,0:T(8,128)(2,1)S(1)}) custom-call(bf16[32,7296]{1,0:T(8,128)(2,1)S(1)} %pad_maximum_fusion.refs_0_, bf16[32,7296]{1,0:T(8,128)(2,1)S(1)} %pad_maximum_fusion.1.refs_1_, bf16[32,7296]{1,0:T(8,128)(2,1)S(1)} %collective-permute-done.7.refs_2_, ...), custom_call_target="tpu_custom_call" | custom-call | flops 1409286144 | bytes 11010048 | tf_op jit(solution)/shard_map/pallas_call | solution.py:201
  28.4 1.3 %collective-permute-done.12 = bf16[32,7168]{1,0:T(8,128)(2,1)S(1)} collective-permute-done((bf16[32,7168]{1,0:T(8,128)(2,1)S(1)}, bf16[32,7168]{1,0:T(8,128)(2,1)S(1)}, u32[]{:S(2)}, u32[]{:S(2)}) %collective-permute-start.12) | collective-permute-done | bytes 458784 | tf_op jit(solution)/shard_map/ppermute | solution.py:222
  29.7 0.7 %collective-permute-done.9 = bf16[32,7168]{1,0:T(8,128)(2,1)S(1)} collective-permute-done((bf16[32,7168]{1,0:T(8,128)(2,1)S(1)}, bf16[32,7168]{1,0:T(8,128)(2,1)S(1)}, u32[]{:S(2)}, u32[]{:S(2)}) %collective-permute-start.9) | collective-permute-done | bytes 458784 | tf_op jit(solution)/shard_map/ppermute | solution.py:222
  30.6 1.1 %collective-permute-start.13 = (bf16[8,7168]{1,0:T(8,128)(2,1)S(1)}, bf16[8,7168]{1,0:T(8,128)(2,1)S(1)}, u32[]{:S(2)}, u32[]{:S(2)}) collective-permute-start(bf16[8,7168]{1,0:T(8,128)(2,1)S(1)} %get-tuple-element.27), channel_id=1, source_target_pairs={{0,8},{4,12},{8,0},{12,4},{1,9},{5,13},{9,1},{13,5},{2,10},{6,14},... | collective-permute-start | bytes 344072 | tf_op jit(solution)/shard_map/ppermute | solution.py:222
  31.6 0.6 %collective-permute-start.10 = (bf16[16,7168]{1,0:T(8,128)(2,1)S(1)}, bf16[16,7168]{1,0:T(8,128)(2,1)S(1)}, u32[]{:S(2)}, u32[]{:S(2)}) collective-permute-start(bf16[16,7168]{1,0:T(8,128)(2,1)S(1)} %slice.47), channel_id=1, source_target_pairs={{0,1},{1,0},{2,3},{3,2},{4,5},{5,4},{6,7},{7,6},{8,9},{9,8},{10,11... | collective-permute-start | bytes 688136 | tf_op jit(solution)/shard_map/ppermute | solution.py:222
  32.2 0.6 %collective-permute-start.15 = (bf16[8,7168]{1,0:T(8,128)(2,1)S(1)}, bf16[8,7168]{1,0:T(8,128)(2,1)S(1)}, u32[]{:S(2)}, u32[]{:S(2)}) collective-permute-start(bf16[8,7168]{1,0:T(8,128)(2,1)S(1)} %get-tuple-element.28), channel_id=1, source_target_pairs={{0,8},{4,12},{8,0},{12,4},{1,9},{5,13},{9,1},{13,5},{2,10},{6,14},... | collective-permute-start | bytes 344072 | tf_op jit(solution)/shard_map/ppermute | solution.py:222
  32.8 3.8 %collective-permute-done.13 = bf16[8,7168]{1,0:T(8,128)(2,1)S(1)} collective-permute-done((bf16[8,7168]{1,0:T(8,128)(2,1)S(1)}, bf16[8,7168]{1,0:T(8,128)(2,1)S(1)}, u32[]{:S(2)}, u32[]{:S(2)}) %collective-permute-start.13) | collective-permute-done | bytes 114720 | tf_op jit(solution)/shard_map/ppermute | solution.py:222
  37.1 1.1 %collective-permute-done.15 = bf16[8,7168]{1,0:T(8,128)(2,1)S(1)} collective-permute-done((bf16[8,7168]{1,0:T(8,128)(2,1)S(1)}, bf16[8,7168]{1,0:T(8,128)(2,1)S(1)}, u32[]{:S(2)}, u32[]{:S(2)}) %collective-permute-start.15) | collective-permute-done | bytes 114720 | tf_op jit(solution)/shard_map/ppermute | solution.py:222
  38.3 2.4 %collective-permute-start.16 = (bf16[8,7168]{1,0:T(8,128)(2,1)S(1)}, bf16[8,7168]{1,0:T(8,128)(2,1)S(1)}, u32[]{:S(2)}, u32[]{:S(2)}) collective-permute-start(bf16[8,7168]{1,0:T(8,128)(2,1)S(1)} %add_convert_fusion.4), channel_id=1, source_target_pairs={{0,3},{1,2},{2,1},{3,0},{4,7},{5,6},{6,5},{7,4},{8,11},{9,10},{10,... | collective-permute-start | bytes 344072 | tf_op jit(solution)/shard_map/ppermute | solution.py:222
  40.8 1.6 %collective-permute-start.11 = (bf16[8,7168]{1,0:T(8,128)(2,1)S(1)}, bf16[8,7168]{1,0:T(8,128)(2,1)S(1)}, u32[]{:S(2)}, u32[]{:S(2)}) collective-permute-start(bf16[8,7168]{1,0:T(8,128)(2,1)S(1)} %slice.49), channel_id=1, source_target_pairs={{0,8},{4,12},{8,0},{12,4},{1,9},{5,13},{9,1},{13,5},{2,10},{6,14},... | collective-permute-start | bytes 344072 | tf_op jit(solution)/shard_map/ppermute | solution.py:222
  42.4 2.9 %collective-permute-done.16 = bf16[8,7168]{1,0:T(8,128)(2,1)S(1)} collective-permute-done((bf16[8,7168]{1,0:T(8,128)(2,1)S(1)}, bf16[8,7168]{1,0:T(8,128)(2,1)S(1)}, u32[]{:S(2)}, u32[]{:S(2)}) %collective-permute-start.16) | collective-permute-done | bytes 114720 | tf_op jit(solution)/shard_map/ppermute | solution.py:222
  45.3 2.0 %collective-permute-done.14 = bf16[8,7168]{1,0:T(8,128)(2,1)S(1)} collective-permute-done((bf16[8,7168]{1,0:T(8,128)(2,1)S(1)}, bf16[8,7168]{1,0:T(8,128)(2,1)S(1)}, u32[]{:S(2)}, u32[]{:S(2)}) %collective-permute-start.14) | collective-permute-done | bytes 114720 | tf_op jit(solution)/shard_map/ppermute | solution.py:222
  47.3 0.7 %add_convert_fusion.3 = bf16[8,7168]{1,0:T(8,128)(2,1)} fusion(bf16[8,7168]{1,0:T(8,128)(2,1)S(1)} %collective-permute-done.16, bf16[8,7168]{1,0:T(8,128)(2,1)S(1)} %collective-permute-done.14, bf16[8,7168]{1,0:T(8,128)(2,1)S(1)} %collective-permute-done.11, bf16[16,7168]{1,0:T(8,128)(2,1)S(1)} %add_convert_fusion.2), kind=kLoop, calls=%fused_computation.8 | loop fusion | flops 458752 | bytes 573440 | tf_op jit(solution)/shard_map/convert_element_type | solution.py:298
  (40 shorter events, 2.8 us)
Async XLA Ops:
  1.1 13.0 %collective-permute-start = (bf16[8,7296]{1,0:T(8,128)(2,1)S(1)}, bf16[8,7296]{1,0:T(8,128)(2,1)S(1)}, u32[]{:S(2)}, u32[]{:S(2)}) collective-permute-start(bf16[8,7296]{1,0:T(8,128)(2,1)S(1)} %shard_map.73.ready_ref), channel_id=1, source_target_pairs={{0,8},{4,12},{8,0},{12,4},{1,9},{5,13},{9,1},{13,5},{2,10},{6,14},... | collective-permute-start | bytes 350216 | tf_op jit(solution)/shard_map/ppermute | solution.py:222
  4.1 10.6 %collective-permute-start.1 = (bf16[8,7296]{1,0:T(8,128)(2,1)S(1)}, bf16[8,7296]{1,0:T(8,128)(2,1)S(1)}, u32[]{:S(2)}, u32[]{:S(2)}) collective-permute-start(bf16[8,7296]{1,0:T(8,128)(2,1)S(1)} %shard_map.73.ready_ref), channel_id=1, source_target_pairs={{0,3},{1,2},{2,1},{3,0},{4,7},{5,6},{6,5},{7,4},{8,11},{9,10},{10,... | collective-permute-start | bytes 350216 | tf_op jit(solution)/shard_map/ppermute | solution.py:222
  7.7 9.6 %collective-permute-start.2 = (bf16[8,7296]{1,0:T(8,128)(2,1)S(1)}, bf16[8,7296]{1,0:T(8,128)(2,1)S(1)}, u32[]{:S(2)}, u32[]{:S(2)}) collective-permute-start(bf16[8,7296]{1,0:T(8,128)(2,1)S(1)} %shard_map.73.ready_ref), channel_id=1, source_target_pairs={{0,2},{1,3},{2,0},{3,1},{4,6},{5,7},{6,4},{7,5},{8,10},{9,11},{10,... | collective-permute-start | bytes 350216 | tf_op jit(solution)/shard_map/ppermute | solution.py:222
  7.7 6.2 %collective-permute-start.3 = (bf16[8,7168]{1,0:T(8,128)(2,1)}, bf16[8,7168]{1,0:T(8,128)(2,1)S(1)}, u32[]{:S(2)}, u32[]{:S(2)}) collective-permute-start(bf16[8,7168]{1,0:T(8,128)(2,1)} %tokens_ref.1), channel_id=1, source_target_pairs={{0,8},{4,12},{8,0},{12,4},{1,9},{5,13},{9,1},{13,5},{2,10},{6,14},... | collective-permute-start | bytes 344072 | tf_op jit(solution)/shard_map/ppermute | solution.py:222
  9.2 8.8 %copy-start.1 = (bf16[8,7168]{1,0:T(8,128)(2,1)S(1)}, bf16[8,7168]{1,0:T(8,128)(2,1)}, u32[]{:S(2)}) copy-start(bf16[8,7168]{1,0:T(8,128)(2,1)} %tokens_ref.1) | copy-start | bytes 344068
  14.0 4.0 %collective-permute-start.6 = (bf16[16,7168]{1,0:T(8,128)(2,1)S(1)}, bf16[16,7168]{1,0:T(8,128)(2,1)S(1)}, u32[]{:S(2)}, u32[]{:S(2)}) collective-permute-start(bf16[16,7168]{1,0:T(8,128)(2,1)S(1)} %constant_dynamic-update-slice_fusion), channel_id=1, source_target_pairs={{0,4},{4,0},{8,12},{12,8},{1,5},{5,1},{9,13},{13,9},{2,6},{6,2},{1... | collective-permute-start | bytes 688136 | tf_op jit(solution)/shard_map/ppermute | solution.py:222
  14.1 10.0 %collective-permute-start.4 = (bf16[16,7296]{1,0:T(8,128)(2,1)S(1)}, bf16[16,7296]{1,0:T(8,128)(2,1)S(1)}, u32[]{:S(2)}, u32[]{:S(2)}) collective-permute-start(bf16[16,7296]{1,0:T(8,128)(2,1)S(1)} %pad_maximum_fusion.4), channel_id=1, source_target_pairs={{0,1},{1,0},{2,3},{3,2},{4,5},{5,4},{6,7},{7,6},{8,9},{9,8},{10,11... | collective-permute-start | bytes 700424 | tf_op jit(solution)/shard_map/ppermute | solution.py:222
  17.3 6.8 %collective-permute-start.5 = (bf16[16,7296]{1,0:T(8,128)(2,1)S(1)}, bf16[16,7296]{1,0:T(8,128)(2,1)S(1)}, u32[]{:S(2)}, u32[]{:S(2)}) collective-permute-start(bf16[16,7296]{1,0:T(8,128)(2,1)S(1)} %pad_maximum_fusion.3.ready_ref), channel_id=1, source_target_pairs={{0,8},{4,12},{8,0},{12,4},{1,9},{5,13},{9,1},{13,5},{2,10},{6,14},... | collective-permute-start | bytes 700424 | tf_op jit(solution)/shard_map/ppermute | solution.py:222
  17.9 7.7 %collective-permute-start.7 = (bf16[32,7296]{1,0:T(8,128)(2,1)S(1)}, bf16[32,7296]{1,0:T(8,128)(2,1)S(1)}, u32[]{:S(2)}, u32[]{:S(2)}) collective-permute-start(bf16[32,7296]{1,0:T(8,128)(2,1)S(1)} %pad_maximum_fusion.refs_0_), channel_id=1, source_target_pairs={{0,4},{4,0},{8,12},{12,8},{1,5},{5,1},{9,13},{13,9},{2,6},{6,2},{1... | collective-permute-start | bytes 1400840 | tf_op jit(solution)/shard_map/ppermute | solution.py:222
  18.0 6.2 %slice-start = ((s8[7340032]{0:T(1024)(128)(4,1)}), s8[4194304]{0:T(1024)(128)(4,1)S(1)}, s32[]{:S(2)}) async-start(s8[7340032]{0:T(1024)(128)(4,1)} %bitcast.7), calls=%async_computation | async-start | bytes 8388608
  18.1 6.1 %slice-start.1 = ((s8[7340032]{0:T(1024)(128)(4,1)}), s8[3145728]{0:T(1024)(128)(4,1)S(1)}, s32[]{:S(2)}) async-start(s8[7340032]{0:T(1024)(128)(4,1)} %bitcast.7), calls=%async_computation.1 | async-start | bytes 6291456
  23.1 3.0 %copy-start = (bf16[1,256,7168]{2,1,0:T(8,128)(2,1)S(1)}, bf16[1,256,7168]{2,1,0:T(8,128)(2,1)}, u32[]{:S(2)}) copy-start(bf16[1,256,7168]{2,1,0:T(8,128)(2,1)} %param.11) | copy-start | bytes 11010052
  24.2 1.9 %collective-permute-start.8 = (bf16[32,7296]{1,0:T(8,128)(2,1)S(1)}, bf16[32,7296]{1,0:T(8,128)(2,1)S(1)}, u32[]{:S(2)}, u32[]{:S(2)}) collective-permute-start(bf16[32,7296]{1,0:T(8,128)(2,1)S(1)} %pad_maximum_fusion.1.refs_1_), channel_id=1, source_target_pairs={{0,4},{4,0},{8,12},{12,8},{1,5},{5,1},{9,13},{13,9},{2,6},{6,2},{1... | collective-permute-start | bytes 1400840 | tf_op jit(solution)/shard_map/ppermute | solution.py:222
  27.8 1.9 %collective-permute-start.12 = (bf16[32,7168]{1,0:T(8,128)(2,1)S(1)}, bf16[32,7168]{1,0:T(8,128)(2,1)S(1)}, u32[]{:S(2)}, u32[]{:S(2)}) collective-permute-start(bf16[32,7168]{1,0:T(8,128)(2,1)S(1)} %get-tuple-element.23), channel_id=1, source_target_pairs={{0,4},{4,0},{8,12},{12,8},{1,5},{5,1},{9,13},{13,9},{2,6},{6,2},{1... | collective-permute-start | bytes 1376264 | tf_op jit(solution)/shard_map/ppermute | solution.py:222
  28.0 2.3 %collective-permute-start.9 = (bf16[32,7168]{1,0:T(8,128)(2,1)S(1)}, bf16[32,7168]{1,0:T(8,128)(2,1)S(1)}, u32[]{:S(2)}, u32[]{:S(2)}) collective-permute-start(bf16[32,7168]{1,0:T(8,128)(2,1)S(1)} %get-tuple-element.22), channel_id=1, source_target_pairs={{0,4},{4,0},{8,12},{12,8},{1,5},{5,1},{9,13},{13,9},{2,6},{6,2},{1... | collective-permute-start | bytes 1376264 | tf_op jit(solution)/shard_map/ppermute | solution.py:222
  30.6 6.1 %collective-permute-start.13 = (bf16[8,7168]{1,0:T(8,128)(2,1)S(1)}, bf16[8,7168]{1,0:T(8,128)(2,1)S(1)}, u32[]{:S(2)}, u32[]{:S(2)}) collective-permute-start(bf16[8,7168]{1,0:T(8,128)(2,1)S(1)} %get-tuple-element.27), channel_id=1, source_target_pairs={{0,8},{4,12},{8,0},{12,4},{1,9},{5,13},{9,1},{13,5},{2,10},{6,14},... | collective-permute-start | bytes 344072 | tf_op jit(solution)/shard_map/ppermute | solution.py:222
  31.6 9.1 %collective-permute-start.10 = (bf16[16,7168]{1,0:T(8,128)(2,1)S(1)}, bf16[16,7168]{1,0:T(8,128)(2,1)S(1)}, u32[]{:S(2)}, u32[]{:S(2)}) collective-permute-start(bf16[16,7168]{1,0:T(8,128)(2,1)S(1)} %slice.47), channel_id=1, source_target_pairs={{0,1},{1,0},{2,3},{3,2},{4,5},{5,4},{6,7},{7,6},{8,9},{9,8},{10,11... | collective-permute-start | bytes 688136 | tf_op jit(solution)/shard_map/ppermute | solution.py:222
  32.2 6.0 %collective-permute-start.15 = (bf16[8,7168]{1,0:T(8,128)(2,1)S(1)}, bf16[8,7168]{1,0:T(8,128)(2,1)S(1)}, u32[]{:S(2)}, u32[]{:S(2)}) collective-permute-start(bf16[8,7168]{1,0:T(8,128)(2,1)S(1)} %get-tuple-element.28), channel_id=1, source_target_pairs={{0,8},{4,12},{8,0},{12,4},{1,9},{5,13},{9,1},{13,5},{2,10},{6,14},... | collective-permute-start | bytes 344072 | tf_op jit(solution)/shard_map/ppermute | solution.py:222
  36.6 10.7 %collective-permute-start.14 = (bf16[8,7168]{1,0:T(8,128)(2,1)S(1)}, bf16[8,7168]{1,0:T(8,128)(2,1)S(1)}, u32[]{:S(2)}, u32[]{:S(2)}) collective-permute-start(bf16[8,7168]{1,0:T(8,128)(2,1)S(1)} %add_convert_fusion.5), channel_id=1, source_target_pairs={{0,2},{1,3},{2,0},{3,1},{4,6},{5,7},{6,4},{7,5},{8,10},{9,11},{10,... | collective-permute-start | bytes 344072 | tf_op jit(solution)/shard_map/ppermute | solution.py:222
  38.3 7.0 %collective-permute-start.16 = (bf16[8,7168]{1,0:T(8,128)(2,1)S(1)}, bf16[8,7168]{1,0:T(8,128)(2,1)S(1)}, u32[]{:S(2)}, u32[]{:S(2)}) collective-permute-start(bf16[8,7168]{1,0:T(8,128)(2,1)S(1)} %add_convert_fusion.4), channel_id=1, source_target_pairs={{0,3},{1,2},{2,1},{3,0},{4,7},{5,6},{6,5},{7,4},{8,11},{9,10},{10,... | collective-permute-start | bytes 344072 | tf_op jit(solution)/shard_map/ppermute | solution.py:222
  40.8 6.5 %collective-permute-start.11 = (bf16[8,7168]{1,0:T(8,128)(2,1)S(1)}, bf16[8,7168]{1,0:T(8,128)(2,1)S(1)}, u32[]{:S(2)}, u32[]{:S(2)}) collective-permute-start(bf16[8,7168]{1,0:T(8,128)(2,1)S(1)} %slice.49), channel_id=1, source_target_pairs={{0,8},{4,12},{8,0},{12,4},{1,9},{5,13},{9,1},{13,5},{2,10},{6,14},... | collective-permute-start | bytes 344072 | tf_op jit(solution)/shard_map/ppermute | solution.py:222

commit v8 on v7

--- a/solution.py
+++ b/solution.py
@@ -257,10 +257,10 @@
     near_half = exchange(own_half, "sub", 1)
     token_all = jnp.concatenate([token_half, exchange(token_half, "ep", 1)], axis=0)
     expert_weights, early = flat_pairs(expert_up[0], shared_up, routed_rows)
-    far, expert_weights, _ = lax.optimization_barrier((far, expert_weights, (own_half, token_half)))
+    far, expert_weights, _ = lax.optimization_barrier((far, expert_weights, token_half))
     middle = shared_middle(token_all, early, shared_up, far)
 
-    far_chips = [exchange(far, "ep", chip) for chip in range(CORES, experts, CORES)]
+    far_chips = [exchange(after(far, own_half), "ep", chip) for chip in range(CORES, experts, CORES)]
     first = jnp.concatenate([own_half, far], axis=0)
     late = after(jnp.concatenate([near_half] + far_chips, axis=0), middle)
     gathered = (first, late, exchange(first, "ep", 1), exchange(late, "ep", 1))

time: 48.2 us -> 48.1 us (level)
  waiting for transfers between devices: 15.7 us -> 10.7 us
  starting transfers between devices: 15.9 us -> 20.6 us
    ppermute x17, waiting for transfers between devices: 15.7 us -> 10.7 us  [exchange(): return lax.ppermute(rows, axis, [(i, i ^ flip) for i in range(size)])]
    ppermute x17, starting transfers between devices: 15.9 us -> 20.6 us  [exchange(): return lax.ppermute(rows, axis, [(i, i ^ flip) for i in range(size)])]
  transfers between devices with their start and end apart: 17 -> 17, of which waited for: 9 -> 6; matrix products, arithmetic and copies ran while one was open for 6% -> 6% of each run, Pallas kernels for 20% -> 20%
where the time goes in v8:
time: 48.1 us; the launch traced here: 48 us
  starting transfers between devices  20.6 us (43%)
  Pallas kernels  12.6 us (26%)
  waiting for transfers between devices  10.7 us (22%)
  matrix products  1.39 us (3%)
  local copies, waits for them, and re-layouts  1.3 us (3%)
  other arithmetic  1.21 us (3%)
    ppermute x17, starting transfers between devices, exchange(): return lax.ppermute(rows, axis, [(i, i ^ flip) for i in range(size)])  20.6 us
    ppermute x17, waiting for transfers between devices, exchange(): return lax.ppermute(rows, axis, [(i, i ^ flip) for i in range(size)])  10.7 us
    pallas_call x1, Pallas kernels, shared_middle(): pl.pallas_call(shared_up_kernel, in_specs=[pl.BlockSpec(memory_space=pltp...  4.98 us
    pallas_call x1, Pallas kernels, flat_pairs(): pl.pallas_call(split_kernel, in_specs=[pl.BlockSpec(memory_space=pltpu.HB...  4.78 us
    pallas_call x1, Pallas kernels, routed_parts(): pl.pallas_call(functools.partial(routed_kernel, pieces), in_specs=[pl.Blo...  1.72 us
    dot_general x1, matrix products, per_device(): jnp.dot(middle, shared_down, preferred_element_type=jnp.float32)  1.39 us
    unnamed x9, local copies, waits for them, and re-layouts  1.25 us
    pallas_call x1, Pallas kernels, owner_rows(): pl.pallas_call(owner_kernel, in_specs=[pl.BlockSpec(memory_space=pltpu.HB...  1.09 us
  transfers between devices with their start and end apart: 17, of which 6 were waited for; matrix products, arithmetic and copies ran while one was open for 6% of the time, Pallas kernels for 20%

profile of v8, /device:TPU:0, one launch (start us, length us, event | category | flops | bytes accessed | tf_op | source)
XLA Modules:
  0.0 48.0 jit_solution(3568148357260964159)
XLA Ops:
  0.0 1.1 %shard_map.73.ready_ref = bf16[8,7296]{1,0:T(8,128)(2,1)S(1)} custom-call(bf16[8,7168]{1,0:T(8,128)(2,1)} %tokens_ref.1, s32[2,8]{1,0:T(2,128)} %bitcast.10, bf16[2,8]{1,0:T(2,128)(2,1)} %bitcast.11, f32[1,128]{1,0:T(1,128)S(1)} %compare_convert_fusion.ready_ref.refs_6_), custom_call_target="tpu_custom_call" | custom-call | tf_op jit(solution)/shard_map/pallas_call | solution.py:59
  1.1 5.1 %collective-permute-start.1 = (bf16[8,7296]{1,0:T(8,128)(2,1)S(1)}, bf16[8,7296]{1,0:T(8,128)(2,1)S(1)}, u32[]{:S(2)}, u32[]{:S(2)}) collective-permute-start(bf16[8,7296]{1,0:T(8,128)(2,1)S(1)} %shard_map.73.ready_ref), channel_id=1, source_target_pairs={{0,3},{1,2},{2,1},{3,0},{4,7},{5,6},{6,5},{7,4},{8,11},{9,10},{10,... | collective-permute-start | bytes 350216 | tf_op jit(solution)/shard_map/ppermute | solution.py:222
  6.2 1.5 %collective-permute-start = (bf16[8,7296]{1,0:T(8,128)(2,1)S(1)}, bf16[8,7296]{1,0:T(8,128)(2,1)S(1)}, u32[]{:S(2)}, u32[]{:S(2)}) collective-permute-start(bf16[8,7296]{1,0:T(8,128)(2,1)S(1)} %shard_map.73.ready_ref), channel_id=1, source_target_pairs={{0,8},{4,12},{8,0},{12,4},{1,9},{5,13},{9,1},{13,5},{2,10},{6,14},... | collective-permute-start | bytes 350216 | tf_op jit(solution)/shard_map/ppermute | solution.py:222
  8.2 0.9 %constant_dynamic-update-slice_fusion.1 = bf16[16,7168]{1,0:T(8,128)(2,1)S(1)} fusion(bf16[8,7168]{1,0:T(8,128)(2,1)} %tokens_ref.1), kind=kLoop, calls=%fused_computation.12 | loop fusion | bytes 229376
  9.2 4.8 %shard_map.74 = (bf16[7168,512]{1,0:T(8,128)(2,1)S(1)}, bf16[2560,2,512]{2,1,0:T(2,128)(2,1)S(1)}) custom-call(bf16[7168,2,256]{2,1,0:T(2,128)(2,1)} %bitcast.9, bf16[7168,2,512]{2,1,0:T(2,128)(2,1)} %up_ref.3, bf16[8,7296]{1,0:T(8,128)(2,1)S(1)} %shard_map.73.ready_ref), custom_call_target="tpu_custom_call" | custom-call | bytes 14680064 | tf_op jit(solution)/shard_map/pallas_call | solution.py:97
  14.1 2.0 %collective-permute-done.2 = bf16[8,7296]{1,0:T(8,128)(2,1)S(1)} collective-permute-done((bf16[8,7296]{1,0:T(8,128)(2,1)S(1)}, bf16[8,7296]{1,0:T(8,128)(2,1)S(1)}, u32[]{:S(2)}, u32[]{:S(2)}) %collective-permute-start.2) | collective-permute-done | bytes 116768 | tf_op jit(solution)/shard_map/ppermute | solution.py:222
  16.2 1.6 %collective-permute-start.5 = (bf16[16,7296]{1,0:T(8,128)(2,1)S(1)}, bf16[16,7296]{1,0:T(8,128)(2,1)S(1)}, u32[]{:S(2)}, u32[]{:S(2)}) collective-permute-start(bf16[16,7296]{1,0:T(8,128)(2,1)S(1)} %pad_maximum_fusion.3.ready_ref), channel_id=1, source_target_pairs={{0,8},{4,12},{8,0},{12,4},{1,9},{5,13},{9,1},{13,5},{2,10},{6,14},... | collective-permute-start | bytes 700424 | tf_op jit(solution)/shard_map/ppermute | solution.py:222
  18.0 5.0 %shard_map.75 = bf16[32,512]{1,0:T(8,128)(2,1)S(1)} custom-call(bf16[32,7168]{1,0:T(8,128)(2,1)S(1)} %pad_maximum_fusion.2.rows_ref, bf16[2560,2,512]{2,1,0:T(2,128)(2,1)S(1)} %get-tuple-element.20.early_ref, bf16[7168,2,512]{2,1,0:T(2,128)(2,1)} %up_ref.3, bf16[16,7296]{1,0:T(8,128)(2,1)S(1)} %pad_maximum_fusion.3.ready_ref), custom_call_target="tpu_custom_call" | custom-call | flops 469762048 | bytes 14680064 | tf_op jit(solution)/shard_map/pallas_call | solution.py:143
  23.1 0.5 %collective-permute-start.8 = (bf16[32,7296]{1,0:T(8,128)(2,1)S(1)}, bf16[32,7296]{1,0:T(8,128)(2,1)S(1)}, u32[]{:S(2)}, u32[]{:S(2)}) collective-permute-start(bf16[32,7296]{1,0:T(8,128)(2,1)S(1)} %pad_maximum_fusion.1.refs_1_), channel_id=1, source_target_pairs={{0,4},{4,0},{8,12},{12,8},{1,5},{5,1},{9,13},{13,9},{2,6},{6,2},{1... | collective-permute-start | bytes 1400840 | tf_op jit(solution)/shard_map/ppermute | solution.py:222
  23.9 1.4 %fusion.1.refs_7_ = f32[32,7168]{1,0:T(8,128)S(1)} fusion(bf16[32,512]{1,0:T(8,128)(2,1)S(1)} %shard_map.75, bf16[512,7168]{1,0:T(8,128)(2,1)S(1)} %bitcast.8), kind=kOutput, calls=%fused_computation.15 | convolution fusion | flops 234881024 | bytes 8290304 | tf_op jit(solution)/shard_map/dot_general | solution.py:279
  25.3 1.7 %shard_map.76 = (bf16[64,7168]{1,0:T(8,128)(2,1)S(1)}, bf16[32,7168]{1,0:T(8,128)(2,1)S(1)}, bf16[32,7168]{1,0:T(8,128)(2,1)S(1)}) custom-call(bf16[32,7296]{1,0:T(8,128)(2,1)S(1)} %pad_maximum_fusion.refs_0_, bf16[32,7296]{1,0:T(8,128)(2,1)S(1)} %pad_maximum_fusion.1.refs_1_, bf16[32,7296]{1,0:T(8,128)(2,1)S(1)} %collective-permute-done.7.refs_2_, ...), custom_call_target="tpu_custom_call" | custom-call | flops 1409286144 | bytes 11010048 | tf_op jit(solution)/shard_map/pallas_call | solution.py:201
  27.0 0.5 %collective-permute-start.12 = (bf16[32,7168]{1,0:T(8,128)(2,1)S(1)}, bf16[32,7168]{1,0:T(8,128)(2,1)S(1)}, u32[]{:S(2)}, u32[]{:S(2)}) collective-permute-start(bf16[32,7168]{1,0:T(8,128)(2,1)S(1)} %get-tuple-element.25), channel_id=1, source_target_pairs={{0,4},{4,0},{8,12},{12,8},{1,5},{5,1},{9,13},{13,9},{2,6},{6,2},{1... | collective-permute-start | bytes 1376264 | tf_op jit(solution)/shard_map/ppermute | solution.py:222
  27.7 1.4 %collective-permute-done.12 = bf16[32,7168]{1,0:T(8,128)(2,1)S(1)} collective-permute-done((bf16[32,7168]{1,0:T(8,128)(2,1)S(1)}, bf16[32,7168]{1,0:T(8,128)(2,1)S(1)}, u32[]{:S(2)}, u32[]{:S(2)}) %collective-permute-start.12) | collective-permute-done | bytes 458784 | tf_op jit(solution)/shard_map/ppermute | solution.py:222
  29.0 0.7 %collective-permute-done.9 = bf16[32,7168]{1,0:T(8,128)(2,1)S(1)} collective-permute-done((bf16[32,7168]{1,0:T(8,128)(2,1)S(1)}, bf16[32,7168]{1,0:T(8,128)(2,1)S(1)}, u32[]{:S(2)}, u32[]{:S(2)}) %collective-permute-start.9) | collective-permute-done | bytes 458784 | tf_op jit(solution)/shard_map/ppermute | solution.py:222
  29.9 1.1 %collective-permute-start.13 = (bf16[8,7168]{1,0:T(8,128)(2,1)S(1)}, bf16[8,7168]{1,0:T(8,128)(2,1)S(1)}, u32[]{:S(2)}, u32[]{:S(2)}) collective-permute-start(bf16[8,7168]{1,0:T(8,128)(2,1)S(1)} %get-tuple-element.29), channel_id=1, source_target_pairs={{0,8},{4,12},{8,0},{12,4},{1,9},{5,13},{9,1},{13,5},{2,10},{6,14},... | collective-permute-start | bytes 344072 | tf_op jit(solution)/shard_map/ppermute | solution.py:222
  31.1 1.7 %collective-permute-start.10 = (bf16[16,7168]{1,0:T(8,128)(2,1)S(1)}, bf16[16,7168]{1,0:T(8,128)(2,1)S(1)}, u32[]{:S(2)}, u32[]{:S(2)}) collective-permute-start(bf16[16,7168]{1,0:T(8,128)(2,1)S(1)} %slice.47), channel_id=1, source_target_pairs={{0,1},{1,0},{2,3},{3,2},{4,5},{5,4},{6,7},{7,6},{8,9},{9,8},{10,11... | collective-permute-start | bytes 688136 | tf_op jit(solution)/shard_map/ppermute | solution.py:222
  32.8 1.2 %collective-permute-start.15 = (bf16[8,7168]{1,0:T(8,128)(2,1)S(1)}, bf16[8,7168]{1,0:T(8,128)(2,1)S(1)}, u32[]{:S(2)}, u32[]{:S(2)}) collective-permute-start(bf16[8,7168]{1,0:T(8,128)(2,1)S(1)} %get-tuple-element.30), channel_id=1, source_target_pairs={{0,8},{4,12},{8,0},{12,4},{1,9},{5,13},{9,1},{13,5},{2,10},{6,14},... | collective-permute-start | bytes 344072 | tf_op jit(solution)/shard_map/ppermute | solution.py:222
  34.1 1.7 %collective-permute-done.13 = bf16[8,7168]{1,0:T(8,128)(2,1)S(1)} collective-permute-done((bf16[8,7168]{1,0:T(8,128)(2,1)S(1)}, bf16[8,7168]{1,0:T(8,128)(2,1)S(1)}, u32[]{:S(2)}, u32[]{:S(2)}) %collective-permute-start.13) | collective-permute-done | bytes 114720 | tf_op jit(solution)/shard_map/ppermute | solution.py:222
  35.8 3.2 %collective-permute-start.14 = (bf16[8,7168]{1,0:T(8,128)(2,1)S(1)}, bf16[8,7168]{1,0:T(8,128)(2,1)S(1)}, u32[]{:S(2)}, u32[]{:S(2)}) collective-permute-start(bf16[8,7168]{1,0:T(8,128)(2,1)S(1)} %add_convert_fusion.5), channel_id=1, source_target_pairs={{0,2},{1,3},{2,0},{3,1},{4,6},{5,7},{6,4},{7,5},{8,10},{9,11},{10,... | collective-permute-start | bytes 344072 | tf_op jit(solution)/shard_map/ppermute | solution.py:222
  39.1 1.6 %collective-permute-start.16 = (bf16[8,7168]{1,0:T(8,128)(2,1)S(1)}, bf16[8,7168]{1,0:T(8,128)(2,1)S(1)}, u32[]{:S(2)}, u32[]{:S(2)}) collective-permute-start(bf16[8,7168]{1,0:T(8,128)(2,1)S(1)} %add_convert_fusion.4), channel_id=1, source_target_pairs={{0,3},{1,2},{2,1},{3,0},{4,7},{5,6},{6,5},{7,4},{8,11},{9,10},{10,... | collective-permute-start | bytes 344072 | tf_op jit(solution)/shard_map/ppermute | solution.py:222
  40.8 1.6 %collective-permute-start.11 = (bf16[8,7168]{1,0:T(8,128)(2,1)S(1)}, bf16[8,7168]{1,0:T(8,128)(2,1)S(1)}, u32[]{:S(2)}, u32[]{:S(2)}) collective-permute-start(bf16[8,7168]{1,0:T(8,128)(2,1)S(1)} %slice.49), channel_id=1, source_target_pairs={{0,8},{4,12},{8,0},{12,4},{1,9},{5,13},{9,1},{13,5},{2,10},{6,14},... | collective-permute-start | bytes 344072 | tf_op jit(solution)/shard_map/ppermute | solution.py:222
  42.4 3.4 %collective-permute-done.16 = bf16[8,7168]{1,0:T(8,128)(2,1)S(1)} collective-permute-done((bf16[8,7168]{1,0:T(8,128)(2,1)S(1)}, bf16[8,7168]{1,0:T(8,128)(2,1)S(1)}, u32[]{:S(2)}, u32[]{:S(2)}) %collective-permute-start.16) | collective-permute-done | bytes 114720 | tf_op jit(solution)/shard_map/ppermute | solution.py:222
  45.7 1.6 %collective-permute-done.14 = bf16[8,7168]{1,0:T(8,128)(2,1)S(1)} collective-permute-done((bf16[8,7168]{1,0:T(8,128)(2,1)S(1)}, bf16[8,7168]{1,0:T(8,128)(2,1)S(1)}, u32[]{:S(2)}, u32[]{:S(2)}) %collective-permute-start.14) | collective-permute-done | bytes 114720 | tf_op jit(solution)/shard_map/ppermute | solution.py:222
  47.3 0.7 %add_convert_fusion.3 = bf16[8,7168]{1,0:T(8,128)(2,1)} fusion(bf16[8,7168]{1,0:T(8,128)(2,1)S(1)} %collective-permute-done.16, bf16[8,7168]{1,0:T(8,128)(2,1)S(1)} %collective-permute-done.14, bf16[8,7168]{1,0:T(8,128)(2,1)S(1)} %collective-permute-done.11, bf16[16,7168]{1,0:T(8,128)(2,1)S(1)} %add_convert_fusion.2), kind=kLoop, calls=%fused_computation.8 | loop fusion | flops 458752 | bytes 573440 | tf_op jit(solution)/shard_map/convert_element_type | solution.py:298
  (40 shorter events, 1.7 us)
Async XLA Ops:
  1.1 13.0 %collective-permute-start.1 = (bf16[8,7296]{1,0:T(8,128)(2,1)S(1)}, bf16[8,7296]{1,0:T(8,128)(2,1)S(1)}, u32[]{:S(2)}, u32[]{:S(2)}) collective-permute-start(bf16[8,7296]{1,0:T(8,128)(2,1)S(1)} %shard_map.73.ready_ref), channel_id=1, source_target_pairs={{0,3},{1,2},{2,1},{3,0},{4,7},{5,6},{6,5},{7,4},{8,11},{9,10},{10,... | collective-permute-start | bytes 350216 | tf_op jit(solution)/shard_map/ppermute | solution.py:222
  6.2 9.8 %collective-permute-start.2 = (bf16[8,7296]{1,0:T(8,128)(2,1)S(1)}, bf16[8,7296]{1,0:T(8,128)(2,1)S(1)}, u32[]{:S(2)}, u32[]{:S(2)}) collective-permute-start(bf16[8,7296]{1,0:T(8,128)(2,1)S(1)} %shard_map.73.ready_ref), channel_id=1, source_target_pairs={{0,2},{1,3},{2,0},{3,1},{4,6},{5,7},{6,4},{7,5},{8,10},{9,11},{10,... | collective-permute-start | bytes 350216 | tf_op jit(solution)/shard_map/ppermute | solution.py:222
  6.2 9.9 %collective-permute-start = (bf16[8,7296]{1,0:T(8,128)(2,1)S(1)}, bf16[8,7296]{1,0:T(8,128)(2,1)S(1)}, u32[]{:S(2)}, u32[]{:S(2)}) collective-permute-start(bf16[8,7296]{1,0:T(8,128)(2,1)S(1)} %shard_map.73.ready_ref), channel_id=1, source_target_pairs={{0,8},{4,12},{8,0},{12,4},{1,9},{5,13},{9,1},{13,5},{2,10},{6,14},... | collective-permute-start | bytes 350216 | tf_op jit(solution)/shard_map/ppermute | solution.py:222
  7.7 6.2 %collective-permute-start.3 = (bf16[8,7168]{1,0:T(8,128)(2,1)}, bf16[8,7168]{1,0:T(8,128)(2,1)S(1)}, u32[]{:S(2)}, u32[]{:S(2)}) collective-permute-start(bf16[8,7168]{1,0:T(8,128)(2,1)} %tokens_ref.1), channel_id=1, source_target_pairs={{0,8},{4,12},{8,0},{12,4},{1,9},{5,13},{9,1},{13,5},{2,10},{6,14},... | collective-permute-start | bytes 344072 | tf_op jit(solution)/shard_map/ppermute | solution.py:222
  9.2 8.7 %copy-start.1 = (bf16[8,7168]{1,0:T(8,128)(2,1)S(1)}, bf16[8,7168]{1,0:T(8,128)(2,1)}, u32[]{:S(2)}) copy-start(bf16[8,7168]{1,0:T(8,128)(2,1)} %tokens_ref.1) | copy-start | bytes 344068
  14.0 3.9 %collective-permute-start.6 = (bf16[16,7168]{1,0:T(8,128)(2,1)S(1)}, bf16[16,7168]{1,0:T(8,128)(2,1)S(1)}, u32[]{:S(2)}, u32[]{:S(2)}) collective-permute-start(bf16[16,7168]{1,0:T(8,128)(2,1)S(1)} %constant_dynamic-update-slice_fusion), channel_id=1, source_target_pairs={{0,4},{4,0},{8,12},{12,8},{1,5},{5,1},{9,13},{13,9},{2,6},{6,2},{1... | collective-permute-start | bytes 688136 | tf_op jit(solution)/shard_map/ppermute | solution.py:222
  16.1 6.9 %collective-permute-start.4 = (bf16[16,7296]{1,0:T(8,128)(2,1)S(1)}, bf16[16,7296]{1,0:T(8,128)(2,1)S(1)}, u32[]{:S(2)}, u32[]{:S(2)}) collective-permute-start(bf16[16,7296]{1,0:T(8,128)(2,1)S(1)} %pad_maximum_fusion.4), channel_id=1, source_target_pairs={{0,1},{1,0},{2,3},{3,2},{4,5},{5,4},{6,7},{7,6},{8,9},{9,8},{10,11... | collective-permute-start | bytes 700424 | tf_op jit(solution)/shard_map/ppermute | solution.py:222
  16.2 6.8 %collective-permute-start.5 = (bf16[16,7296]{1,0:T(8,128)(2,1)S(1)}, bf16[16,7296]{1,0:T(8,128)(2,1)S(1)}, u32[]{:S(2)}, u32[]{:S(2)}) collective-permute-start(bf16[16,7296]{1,0:T(8,128)(2,1)S(1)} %pad_maximum_fusion.3.ready_ref), channel_id=1, source_target_pairs={{0,8},{4,12},{8,0},{12,4},{1,9},{5,13},{9,1},{13,5},{2,10},{6,14},... | collective-permute-start | bytes 700424 | tf_op jit(solution)/shard_map/ppermute | solution.py:222
  17.8 7.5 %collective-permute-start.7 = (bf16[32,7296]{1,0:T(8,128)(2,1)S(1)}, bf16[32,7296]{1,0:T(8,128)(2,1)S(1)}, u32[]{:S(2)}, u32[]{:S(2)}) collective-permute-start(bf16[32,7296]{1,0:T(8,128)(2,1)S(1)} %pad_maximum_fusion.refs_0_), channel_id=1, source_target_pairs={{0,4},{4,0},{8,12},{12,8},{1,5},{5,1},{9,13},{13,9},{2,6},{6,2},{1... | collective-permute-start | bytes 1400840 | tf_op jit(solution)/shard_map/ppermute | solution.py:222
  17.9 5.7 %slice-start = ((s8[7340032]{0:T(1024)(128)(4,1)}), s8[4194304]{0:T(1024)(128)(4,1)S(1)}, s32[]{:S(2)}) async-start(s8[7340032]{0:T(1024)(128)(4,1)} %bitcast.7), calls=%async_computation | async-start | bytes 8388608
  18.0 5.9 %slice-start.1 = ((s8[7340032]{0:T(1024)(128)(4,1)}), s8[3145728]{0:T(1024)(128)(4,1)S(1)}, s32[]{:S(2)}) async-start(s8[7340032]{0:T(1024)(128)(4,1)} %bitcast.7), calls=%async_computation.1 | async-start | bytes 6291456
  23.0 2.3 %copy-start = (bf16[1,256,7168]{2,1,0:T(8,128)(2,1)S(1)}, bf16[1,256,7168]{2,1,0:T(8,128)(2,1)}, u32[]{:S(2)}) copy-start(bf16[1,256,7168]{2,1,0:T(8,128)(2,1)} %param.11) | copy-start | bytes 11010052
  23.1 2.2 %collective-permute-start.8 = (bf16[32,7296]{1,0:T(8,128)(2,1)S(1)}, bf16[32,7296]{1,0:T(8,128)(2,1)S(1)}, u32[]{:S(2)}, u32[]{:S(2)}) collective-permute-start(bf16[32,7296]{1,0:T(8,128)(2,1)S(1)} %pad_maximum_fusion.1.refs_1_), channel_id=1, source_target_pairs={{0,4},{4,0},{8,12},{12,8},{1,5},{5,1},{9,13},{13,9},{2,6},{6,2},{1... | collective-permute-start | bytes 1400840 | tf_op jit(solution)/shard_map/ppermute | solution.py:222
  27.0 2.0 %collective-permute-start.12 = (bf16[32,7168]{1,0:T(8,128)(2,1)S(1)}, bf16[32,7168]{1,0:T(8,128)(2,1)S(1)}, u32[]{:S(2)}, u32[]{:S(2)}) collective-permute-start(bf16[32,7168]{1,0:T(8,128)(2,1)S(1)} %get-tuple-element.25), channel_id=1, source_target_pairs={{0,4},{4,0},{8,12},{12,8},{1,5},{5,1},{9,13},{13,9},{2,6},{6,2},{1... | collective-permute-start | bytes 1376264 | tf_op jit(solution)/shard_map/ppermute | solution.py:222
  27.6 2.1 %collective-permute-start.9 = (bf16[32,7168]{1,0:T(8,128)(2,1)S(1)}, bf16[32,7168]{1,0:T(8,128)(2,1)S(1)}, u32[]{:S(2)}, u32[]{:S(2)}) collective-permute-start(bf16[32,7168]{1,0:T(8,128)(2,1)S(1)} %get-tuple-element.24), channel_id=1, source_target_pairs={{0,4},{4,0},{8,12},{12,8},{1,5},{5,1},{9,13},{13,9},{2,6},{6,2},{1... | collective-permute-start | bytes 1376264 | tf_op jit(solution)/shard_map/ppermute | solution.py:222
  29.9 5.9 %collective-permute-start.13 = (bf16[8,7168]{1,0:T(8,128)(2,1)S(1)}, bf16[8,7168]{1,0:T(8,128)(2,1)S(1)}, u32[]{:S(2)}, u32[]{:S(2)}) collective-permute-start(bf16[8,7168]{1,0:T(8,128)(2,1)S(1)} %get-tuple-element.29), channel_id=1, source_target_pairs={{0,8},{4,12},{8,0},{12,4},{1,9},{5,13},{9,1},{13,5},{2,10},{6,14},... | collective-permute-start | bytes 344072 | tf_op jit(solution)/shard_map/ppermute | solution.py:222
  31.1 9.6 %collective-permute-start.10 = (bf16[16,7168]{1,0:T(8,128)(2,1)S(1)}, bf16[16,7168]{1,0:T(8,128)(2,1)S(1)}, u32[]{:S(2)}, u32[]{:S(2)}) collective-permute-start(bf16[16,7168]{1,0:T(8,128)(2,1)S(1)} %slice.47), channel_id=1, source_target_pairs={{0,1},{1,0},{2,3},{3,2},{4,5},{5,4},{6,7},{7,6},{8,9},{9,8},{10,11... | collective-permute-start | bytes 688136 | tf_op jit(solution)/shard_map/ppermute | solution.py:222
  32.8 6.2 %collective-permute-start.15 = (bf16[8,7168]{1,0:T(8,128)(2,1)S(1)}, bf16[8,7168]{1,0:T(8,128)(2,1)S(1)}, u32[]{:S(2)}, u32[]{:S(2)}) collective-permute-start(bf16[8,7168]{1,0:T(8,128)(2,1)S(1)} %get-tuple-element.30), channel_id=1, source_target_pairs={{0,8},{4,12},{8,0},{12,4},{1,9},{5,13},{9,1},{13,5},{2,10},{6,14},... | collective-permute-start | bytes 344072 | tf_op jit(solution)/shard_map/ppermute | solution.py:222
  35.8 11.5 %collective-permute-start.14 = (bf16[8,7168]{1,0:T(8,128)(2,1)S(1)}, bf16[8,7168]{1,0:T(8,128)(2,1)S(1)}, u32[]{:S(2)}, u32[]{:S(2)}) collective-permute-start(bf16[8,7168]{1,0:T(8,128)(2,1)S(1)} %add_convert_fusion.5), channel_id=1, source_target_pairs={{0,2},{1,3},{2,0},{3,1},{4,6},{5,7},{6,4},{7,5},{8,10},{9,11},{10,... | collective-permute-start | bytes 344072 | tf_op jit(solution)/shard_map/ppermute | solution.py:222
  39.1 6.7 %collective-permute-start.16 = (bf16[8,7168]{1,0:T(8,128)(2,1)S(1)}, bf16[8,7168]{1,0:T(8,128)(2,1)S(1)}, u32[]{:S(2)}, u32[]{:S(2)}) collective-permute-start(bf16[8,7168]{1,0:T(8,128)(2,1)S(1)} %add_convert_fusion.4), channel_id=1, source_target_pairs={{0,3},{1,2},{2,1},{3,0},{4,7},{5,6},{6,5},{7,4},{8,11},{9,10},{10,... | collective-permute-start | bytes 344072 | tf_op jit(solution)/shard_map/ppermute | solution.py:222
  40.8 6.5 %collective-permute-start.11 = (bf16[8,7168]{1,0:T(8,128)(2,1)S(1)}, bf16[8,7168]{1,0:T(8,128)(2,1)S(1)}, u32[]{:S(2)}, u32[]{:S(2)}) collective-permute-start(bf16[8,7168]{1,0:T(8,128)(2,1)S(1)} %slice.49), channel_id=1, source_target_pairs={{0,8},{4,12},{8,0},{12,4},{1,9},{5,13},{9,1},{13,5},{2,10},{6,14},... | collective-permute-start | bytes 344072 | tf_op jit(solution)/shard_map/ppermute | solution.py:222
